TPU v7x, 32 devices: a whole 2x2x4 slice. The times are simulated.
32 devices in a mesh: groups: 2 (over y), ctx: 8 (over z, x), batch: 2 (over core).
Axes of the slice: x: 2, y: 2, z: 4, core: 2. Of those that a mesh axis runs over, the one named last changes fastest.
Arguments:
- q_latent: bfloat16 [4, 64, 128, 576], P(('groups', 'batch'), 'ctx'), parts along dimension 0
- kv_new: bfloat16 [4, 64, 576], P(('groups', 'batch'), 'ctx'), parts along dimension 0
- kv_cache: bfloat16 [4, 1024, 576], P(('groups', 'batch'), 'ctx'), parts along dimension 0, may hold values from -6 to 6
- index_q: bfloat16 [4, 64, 64, 128], P(('groups', 'batch'), 'ctx'), parts along dimension 0, may hold values from -0.59765625 to 0.59765625
- index_weight: bfloat16 [4, 64, 64], P(('groups', 'batch'), 'ctx'), parts along dimension 0, may hold values from -3 to 3
- index_keys: bfloat16 [4, 1024, 128], P(('groups', 'batch'), 'ctx'), parts along dimension 0, may hold values from -6 to 6
- block_list: int32 [4, 8, 4], P(('groups', 'batch'), 'ctx'), parts along dimension 0, may hold values from 0 to 15, as said below
- context_len: int32 [4], P(('groups', 'batch')), parts along dimension 0, may hold values from 512 to 1024, as said below
Outputs:
- attended: bfloat16 [4, 64, 128, 512], P(('groups', 'batch'), 'ctx'), parts along dimension 0
- block_score: float32 [4, 64, 16], P(('groups', 'batch'), 'ctx'), parts along dimension 0
There are 2 independent parts, one for each index of `groups`. A program takes and returns all parts, laid end to end along the dimension named above; each array names one. Nothing has to cross between parts.
Inputs may be any that keep to these rules, and one draw needn't show every extreme that they name: `block_list`: each entry is a page of the session's cache that starts below context_len; the 4 pages of one query tile are held by 4 different indices of ctx (page b by index b // 2). `context_len`: session 0 of every part has all 1024 cached tokens valid.
All inputs are finite; a program needn't handle non-finite values.
Results may differ from a plain program's by a relative error of at most 0.0035.
Values may be sent and summed in bfloat16 or wider, within the bound.
No kernel may reach another device: no remote copies, remote signals or barrier semaphores. Data moves between devices by JAX's collectives and lax.ppermute only.
A program may use at most 128 MiB of HBM per device.

v0:
```python
import jax
import jax.numpy as jnp
from jax import lax
from jax.sharding import PartitionSpec as P

DR = 64
BLK = 64


softmax_scale = 0.07216878364870322
neg_fill = -1e30


def on_device(
    q_latent, kv_new, kv_cache, index_q, index_weight, index_keys, block_list, context_len
):
    ctx_count = lax.axis_size("ctx")
    my_index = lax.axis_index("ctx")
    tile_len = q_latent.shape[1]
    head_count = q_latent.shape[2]
    row_width = q_latent.shape[3]
    latent_width = row_width - DR
    ctx_rows = kv_cache.shape[1]
    blocks_dev = ctx_rows // BLK
    block_total = blocks_dev * ctx_count
    index_heads = index_q.shape[2]
    index_width = index_q.shape[3]
    length = context_len[0]
    head_weight = index_weight[0]
    index_rows = index_q[0].reshape(tile_len * index_heads, index_width)
    weight_f32 = head_weight.astype(jnp.float32)
    piece = lax.all_gather(index_keys[0], "ctx", axis=0, tiled=True)
    count = piece.shape[0]
    products = jnp.dot(index_rows, piece.T, preferred_element_type=jnp.float32)
    activ = jnp.maximum(products, 0.0).reshape(tile_len, index_heads, count)
    weighted = jnp.einsum("tjr,tj->tr", activ, weight_f32, precision=lax.Precision.HIGHEST)
    positions = jnp.arange(count)
    weighted = jnp.where(positions[None, :] < length, weighted, 0.0)
    summed = jax.ops.segment_sum(weighted.T, positions // BLK, num_segments=block_total)
    block_sums = summed.T
    block_score = (block_sums / BLK).reshape(1, tile_len, block_total)
    all_lists = lax.all_gather(block_list[0], "ctx", axis=0, tiled=True)
    is_mine = all_lists // blocks_dev == my_index
    slot_index = jnp.sum(jnp.where(is_mine, all_lists % blocks_dev, 0), axis=1)
    wanted = jnp.any(is_mine, axis=1)
    own_blocks = kv_cache[0].reshape(blocks_dev, BLK, row_width)
    outgoing = jnp.where(wanted[:, None, None], own_blocks[slot_index], jnp.zeros((), jnp.bfloat16))
    incoming = lax.all_to_all(outgoing, "ctx", split_axis=0, concat_axis=0, tiled=True)
    chosen = block_list[0, 0]
    cached_rows = incoming[chosen // blocks_dev].reshape(-1, row_width)
    positions = (chosen[:, None] * BLK + jnp.arange(BLK)[None, :]).reshape(-1)
    key_rows = jnp.concatenate([cached_rows, kv_new[0]], axis=0)
    query_rows = q_latent[0].reshape(tile_len * head_count, row_width)
    scores = jnp.dot(query_rows, key_rows.T, preferred_element_type=jnp.float32) * softmax_scale
    cache_ok = positions < length
    token_of = jnp.arange(tile_len * head_count) // head_count
    new_ok = jnp.arange(tile_len)[None, :] <= token_of[:, None]
    allowed = jnp.concatenate(
        [
            jnp.broadcast_to(cache_ok[None, :], (tile_len * head_count, cached_rows.shape[0])),
            new_ok,
        ],
        axis=1,
    )
    scores = jnp.where(allowed, scores, neg_fill)
    highest = jnp.max(scores, axis=1, keepdims=True)
    expo = jnp.exp(scores - highest)
    total = jnp.sum(expo, axis=1, keepdims=True)
    probs = expo.astype(jnp.bfloat16)
    mixed = jnp.dot(probs, key_rows[:, :latent_width], preferred_element_type=jnp.float32) / total
    attended = mixed.astype(jnp.bfloat16).reshape(1, tile_len, head_count, latent_width)
    return (attended, block_score)


def solution(mesh):
    placed = (
        P(("groups", "batch"), "ctx", None, None),
        P(("groups", "batch"), "ctx", None),
        P(("groups", "batch"), "ctx", None),
        P(("groups", "batch"), "ctx", None, None),
        P(("groups", "batch"), "ctx", None),
        P(("groups", "batch"), "ctx", None),
        P(("groups", "batch"), "ctx", None),
        P(("groups", "batch")),
    )
    return jax.shard_map(
        on_device,
        mesh=mesh,
        in_specs=placed,
        out_specs=(P(("groups", "batch"), "ctx", None, None), P(("groups", "batch"), "ctx", None)),
        check_vma=False,
    )
```

profile of v0, /device:TPU:0, one launch (start us, length us, event | category | flops | bytes accessed | tf_op | source)
XLA Modules:
  0.0 81.9 jit_solution(13980660554015847011)
XLA Ops:
  0.6 0.0 copy-start
  0.6 22.4 %all-gather = s32[8,1,4]{2,1,0:T(1,128)S(1)} all-gather(s32[1,1,4]{2,1,0:T(1,128)} %param.14), channel_id=2, replica_groups=mesh['groups'=2,'ctx'=8,'batch'=2] {'ctx'}, dimensions={0}, use_global_device_ids=true | all-gather | bytes 144 | tf_op jit(solution)/shard_map/all_gather | solution.py:42
  23.1 0.1 copy.17
  23.2 1.1 %copy.18 = bf16[1,128,576]{2,1,0:T(8,128)(2,1)S(1)} copy(bf16[1,128,576]{1,2,0:T(8,128)(2,1)} %param.10) | data formatting | bytes 294912 | tf_op args[2]
  24.3 0.7 gather_fusion
  25.0 0.0 copy-start.5
  25.0 0.0 copy-start.3
  25.0 1.0 %broadcast_select_fusion = bf16[8,64,576]{2,1,0:T(8,128)(2,1)} fusion(bf16[8,64,576]{2,1,0:T(8,128)(2,1)S(1)} %gather_fusion, pred[8]{0:T(512)(128)(4,1)S(1)} %get-tuple-element.2), kind=kLoop, calls=%fused_computation.13 | loop fusion | flops 294912 | bytes 1179656 | tf_op jit(solution)/shard_map/jit(_where)/select_n | solution.py:47
  26.0 3.5 %all-to-all-start = ((bf16[8,64,576]{2,1,0:T(8,128)(2,1)}), bf16[8,64,576]{2,1,0:T(8,128)(2,1)S(1)}, u32[]{:S(2)}, u32[]{:S(2)}) async-start(bf16[8,64,576]{2,1,0:T(8,128)(2,1)} %broadcast_select_fusion), calls=%async_computation | async-start | bytes 1310720 | tf_op jit(solution)/shard_map/all_to_all | solution.py:48
  29.5 0.0 copy-done.5
  30.2 0.0 copy-done.3
  30.2 35.8 %all-gather.1 = bf16[1,1024,128]{2,1,0:T(8,128)(2,1)S(1)} all-gather(bf16[1,128,128]{2,1,0:T(8,128)(2,1)S(1)} %copy-done.3), channel_id=3, replica_groups=mesh['groups'=2,'ctx'=8,'batch'=2] {'ctx'}, dimensions={1}, use_global_device_ids=true | all-gather | bytes 294912 | tf_op jit(solution)/shard_map/all_gather | solution.py:32
  66.0 0.1 add_compare_fusion
  66.1 0.0 copy-done
  66.1 0.0 copy-start.4
  66.1 0.4 convolution_maximum_fusion
  66.5 0.0 copy-start.1
  66.6 0.2 copy-done.4
  66.8 0.8 fusion.21
  67.6 0.1 reshape.218
  67.7 0.1 copy-done.1
  67.8 1.8 %copy.19 = bf16[1,8,128,576]{2,1,3,0:T(8,128)(2,1)} copy(bf16[1,8,128,576]{2,3,1,0:T(8,128)(2,1)S(1)} %copy-done.1) | data formatting | bytes 2359296 | tf_op args[0]
  69.6 0.2 copy.22
  69.8 8.1 %scatter_custom_fusion = f32[16,8]{1,0:T(8,128)S(1)} fusion(s32[1024]{0:T(1024)S(1)} %bitcast.90, f32[8,1,1024]{0,2,1:T(8,128)S(1)} %copy.22, f32[]{:T(128)} %constant.90.clone.1, pred[1024]{0:T(1024)(128)(4,1)S(1)} %iota_compare_fusion.1), kind=kCustom, calls=%fused_computation.15 | custom fusion | flops 16384 | bytes 526848 | tf_op jit(solution)/shard_map/scatter-add | solution.py:39
  78.0 0.7 copy.20
  78.7 0.0 all-to-all-done
  78.7 0.6 gather_fusion.1
  79.3 0.0 copy-done.2
  79.3 0.0 copy-done.6
  79.3 0.6 fusion.36
  80.0 0.2 fusion.4
  80.1 1.7 %divide_convert_fusion = bf16[1024,512]{1,0:T(8,128)(2,1)} fusion(f32[1024]{0:T(1024)S(1)} %fusion.4, f32[1024,264]{0,1:T(8,128)S(1)} %get-tuple-element.5, f32[1024]{0:T(1024)S(1)} %get-tuple-element.4, bf16[8,576]{1,0:T(8,128)(2,1)S(1)} %bitcast.92, bf16[256,576]{1,0:T(8,128)(2,1)S(1)} %bitcast.87), kind=kOutput, calls=%fused_computation.3 | convolution fusion | flops 278953984 | bytes 2442240 | tf_op jit(solution)/shard_map/dot_general | solution.py:70
  (15 shorter events, 0.1 us)
Async XLA Ops:
  0.6 65.5 %copy-start = (bf16[1,8,64,128]{3,2,1,0:T(8,128)(2,1)S(1)}, bf16[1,8,64,128]{3,2,1,0:T(8,128)(2,1)}, u32[]{:S(2)}) copy-start(bf16[1,8,64,128]{3,2,1,0:T(8,128)(2,1)} %param.11) | copy-start | bytes 393220
  25.0 4.5 %copy-start.5 = (s32[1,1,4]{2,1,0:T(1,128)S(1)}, s32[1,1,4]{2,1,0:T(1,128)}, u32[]{:S(2)}) copy-start(s32[1,1,4]{2,1,0:T(1,128)} %param.14) | copy-start | bytes 52
  25.0 5.2 %copy-start.3 = (bf16[1,128,128]{2,1,0:T(8,128)(2,1)S(1)}, bf16[1,128,128]{2,1,0:T(8,128)(2,1)}, u32[]{:S(2)}) copy-start(bf16[1,128,128]{2,1,0:T(8,128)(2,1)} %param.13) | copy-start | bytes 98308
  26.0 52.7 %all-to-all-start = ((bf16[8,64,576]{2,1,0:T(8,128)(2,1)}), bf16[8,64,576]{2,1,0:T(8,128)(2,1)S(1)}, u32[]{:S(2)}, u32[]{:S(2)}) async-start(bf16[8,64,576]{2,1,0:T(8,128)(2,1)} %broadcast_select_fusion), calls=%async_computation | async-start | bytes 1310720 | tf_op jit(solution)/shard_map/all_to_all | solution.py:48
  66.1 0.7 copy-start.4
  66.5 1.3 %copy-start.1 = (bf16[1,8,128,576]{2,3,1,0:T(8,128)(2,1)S(1)}, bf16[1,8,128,576]{2,3,1,0:T(8,128)(2,1)}, u32[]{:S(2)}) copy-start(bf16[1,8,128,576]{2,3,1,0:T(8,128)(2,1)} %param.8) | copy-start | bytes 3538948
  69.6 9.7 %copy-start.2 = (bf16[1,8,128,576]{2,1,3,0:T(8,128)(2,1)S(1)}, bf16[1,8,128,576]{2,1,3,0:T(8,128)(2,1)}, u32[]{:S(2)}) copy-start(bf16[1,8,128,576]{2,1,3,0:T(8,128)(2,1)} %copy.19) | copy-start | bytes 3538948
  69.6 9.7 %copy-start.6 = (bf16[1,8,576]{2,1,0:T(8,128)(2,1)S(1)}, bf16[1,8,576]{2,1,0:T(8,128)(2,1)}, u32[]{:S(2)}) copy-start(bf16[1,8,576]{2,1,0:T(8,128)(2,1)} %param.9) | copy-start | bytes 27652
where the time goes:
time: 82.2 us; the launch traced here: 81.9 us
  blocking collectives  58.3 us (71%)
  other arithmetic  9.49 us (12%)
  local copies, waits for them, and re-layouts  5.54 us (7%)
  matrix products  3.57 us (4%)
  starting transfers between devices  3.54 us (4%)
  between operations  1.46 us (2%)
    all_gather x1, blocking collectives, on_device(): piece = lax.all_gather(index_keys[0], 'ctx', axis=0, tiled=True)  35.8 us
    all_gather x1, blocking collectives, on_device(): all_lists = lax.all_gather(block_list[0], 'ctx', axis=0, tiled=True)  22.4 us
    scatter-add x1, other arithmetic, on_device(): jax.ops.segment_sum(weighted.T, positions // BLK, num_segments=block_total)  8.14 us
    all_to_all x1, starting transfers between devices, on_device(): lax.all_to_all(outgoing, 'ctx', split_axis=0, concat_axis=0, tiled=True)  3.54 us
    unnamed x16, local copies, waits for them, and re-layouts  3.23 us
    dot_general x1, matrix products, on_device(): jnp.dot(probs, key_rows[:, :latent_width], preferred_element_type=jnp.flo...  1.74 us
  transfers between devices with their start and end apart: 1, of which 0 were waited for; matrix products, arithmetic and copies ran while one was open for 15% of the time, Pallas kernels for 0%

commit v1 on v0

--- a/solution.py
+++ b/solution.py
@@ -1,6 +1,11 @@
+import functools
+import math
+
 import jax
 import jax.numpy as jnp
 from jax import lax
+from jax.experimental import pallas as pl
+from jax.experimental.pallas import tpu as pltpu
 from jax.sharding import PartitionSpec as P
 
 DR = 64
@@ -9,6 +14,226 @@
 
 softmax_scale = 0.07216878364870322
 neg_fill = -1e30
+F32 = jnp.float32
+BF16 = jnp.bfloat16
+
+
+def nt_dot(a, b):
+    return lax.dot_general(a, b, (((1,), (1,)), ((), ())), preferred_element_type=F32)
+
+
+def lanes_from(source_of_lane, on):
+    row = lax.broadcasted_iota(jnp.int32, (2 * BLK, 2 * BLK), 0)
+    return jnp.where((row == source_of_lane) & on, 1.0, 0.0).astype(BF16)
+
+
+def prep_kernel(width, count, list_ref, pages_ref, keys_ref, out_ref):
+    me = lax.axis_index("ctx")
+    out_ref[0:width, :] = pages_ref[...]
+    rows = keys_ref.shape[0]
+    out_ref[width : width + rows, :] = keys_ref[...]
+    row = lax.broadcasted_iota(jnp.int32, (16, 2 * BLK), 0)
+    flags = jnp.zeros((16, 2 * BLK), F32)
+    other = jnp.bitwise_xor(me, 1)
+    for place, step in enumerate((count - 2, 2, 4)):
+        holder = lax.rem(other + step, count)
+        upper = jnp.int32(0)
+        for j in range(list_ref.shape[0]):
+            upper = jnp.where(list_ref[j] == 2 * holder + 1, 1, upper)
+        flags = jnp.where(row == place, upper.astype(F32), flags)
+    out_ref[width + rows :, :] = flags.astype(BF16)
+
+
+def wanted_half(flag, lower_lanes):
+    lane = lax.broadcasted_iota(jnp.int32, (2 * BLK, 2 * BLK), 1)
+    upper = flag.astype(F32).astype(jnp.int32) * BLK
+    if lower_lanes:
+        return lanes_from(lane + upper, lane < BLK)
+    return lanes_from(lane - BLK + upper, lane >= BLK)
+
+
+def pick_two_kernel(width, flags_ref, before_ref, after_ref, out_ref):
+    flags = flags_ref[...]
+    both = jnp.dot(before_ref[0:width, :], wanted_half(flags[0:1, :], True), preferred_element_type=F32)
+    both += jnp.dot(after_ref[0:width, :], wanted_half(flags[1:2, :], False), preferred_element_type=F32)
+    out_ref[0:width, :] = both.astype(BF16)
+    rows = 2 * BLK
+    out_ref[width : width + rows, :] = before_ref[width : width + rows, :]
+    out_ref[width + rows : width + 2 * rows, :] = after_ref[width : width + rows, :]
+
+
+def pick_one_kernel(width, top, flags_ref, far_ref, out_ref):
+    flag = flags_ref[2:3, :]
+    low = width - top
+    upper = jnp.dot(far_ref[top:width, :], wanted_half(flag, False), preferred_element_type=F32)
+    lower = jnp.dot(far_ref[0:top, :], wanted_half(flag, True), preferred_element_type=F32)
+    out_ref[0:top, :] = (upper[0:top, :] + lower).astype(BF16)
+    out_ref[top:low, :] = upper[top:low, :].astype(BF16)
+    rows = 2 * BLK
+    out_ref[low : low + rows, :] = far_ref[width : width + rows, :]
+
+
+def q_rows_kernel(q_ref, out_ref):
+    tokens, _, heads = q_ref.shape
+    for t in range(tokens):
+        out_ref[t * heads : (t + 1) * heads, :] = q_ref[t].T
+
+
+def index_kernel(
+    count, width, low, length_ref, weight_ref, query_ref, own, near, below, above, far, two, one, out_ref, sums
+):
+    me = lax.axis_index("ctx")
+    length = length_ref[0]
+    rows = 2 * BLK
+    query = query_ref[...]
+    total = query.shape[0]
+    row = lax.broadcasted_iota(jnp.int32, (rows, 1), 0)
+    mate = jnp.bitwise_xor(me, 1)
+    parts = (
+        (own, width, me),
+        (near, width, mate),
+        (below, width, me + count - 2),
+        (above, width, me + 2),
+        (far, width, me + 4),
+        (two, width, mate + count - 2),
+        (two, width + rows, mate + 2),
+        (one, low, mate + 4),
+    )
+    for ref, start, holder in parts:
+        holder = lax.rem(holder, count)
+        keys = ref[start : start + rows, :]
+        keys = jnp.where(row < length - holder * rows, keys, jnp.zeros((), BF16))
+        activ = jnp.maximum(nt_dot(keys, query), 0.0)
+        sums[pl.ds(2 * holder, 1), :] = jnp.sum(activ[0:BLK, :], axis=0, keepdims=True)
+        sums[pl.ds(2 * holder + 1, 1), :] = jnp.sum(activ[BLK:rows, :], axis=0, keepdims=True)
+    weight = weight_ref[...].astype(F32)
+    tokens, heads = weight.shape
+    wide = jnp.concatenate([weight] * tokens, axis=1)
+    lane = lax.broadcasted_iota(jnp.int32, (tokens, total), 1)
+    token = lax.broadcasted_iota(jnp.int32, (tokens, total), 0)
+    wide = jnp.where(lane // heads == token, wide, 0.0)
+    score = lax.dot_general(
+        wide, sums[...], (((1,), (1,)), ((), ())), precision=lax.Precision.HIGHEST, preferred_element_type=F32
+    )
+    out_ref[...] = score * (1.0 / BLK)
+
+
+def attend_kernel(
+    count, width, latent, top, list_ref, length_ref, q_ref, new_ref, own, near, below, above, far, two, one,
+    out_ref, upper_rows, lower_rows, key_rows,
+):
+    me = lax.axis_index("ctx")
+    length = length_ref[0]
+    low = width - top
+    for slot, ref in enumerate((own, above, far, below, near, two)):
+        upper_rows[slot] = ref[0:top, :]
+        lower_rows[slot] = ref[top:width, :]
+    upper_rows[6] = one[0:top, :]
+    lower_rows[6] = one[0:low, :]
+    pages = list_ref.shape[0]
+    tokens = new_ref.shape[0]
+    key_rows[pages * BLK :, :] = jnp.zeros((key_rows.shape[0] - pages * BLK, width), BF16)
+    key_rows[pages * BLK : pages * BLK + tokens, :] = new_ref[...]
+    row = lax.broadcasted_iota(jnp.int32, (BLK, 2 * BLK), 0)
+    lane = lax.broadcasted_iota(jnp.int32, (BLK, 2 * BLK), 1)
+    wide = key_rows.shape[0]
+    column = lax.broadcasted_iota(jnp.int32, (1, wide), 1)
+    limit = jnp.zeros((1, wide), jnp.int32)
+    for j in range(pages):
+        page = list_ref[j]
+        holder, half = page // 2, lax.rem(page, 2)
+        step = lax.rem((holder // 2) - (me // 2) + count // 2, count // 2)
+        same = lax.rem(holder + me, 2) == 0
+        slot = jnp.where(same, step, jnp.where(step == 0, 4, jnp.where(step == 2, 6, 5)))
+        high = jnp.where(same | (step == 0), half, jnp.where(step == 1, 1, 0))
+        high_low = jnp.where(slot == 6, 1, high)
+        pick_upper = jnp.where(lane == row + high * BLK, 1.0, 0.0).astype(BF16)
+        pick_lower = jnp.where(lane == row + high_low * BLK, 1.0, 0.0).astype(BF16)
+        place = slice(j * BLK, (j + 1) * BLK)
+        key_rows[place, 0:top] = nt_dot(pick_upper, upper_rows[slot]).astype(BF16)
+        key_rows[place, top:width] = nt_dot(pick_lower, lower_rows[slot]).astype(BF16)
+        limit = jnp.where(column // BLK == j, length - page * BLK + j * BLK, limit)
+    heads = q_ref.shape[0] // tokens
+    keys = key_rows[...]
+    values = key_rows[:, 0:latent]
+    for t in range(tokens):
+        bound = jnp.where(column >= pages * BLK, pages * BLK + t + 1, limit)
+        place = slice(t * heads, (t + 1) * heads)
+        scores = nt_dot(q_ref[place, :], keys) * softmax_scale
+        scores = jnp.where(column < bound, scores, neg_fill)
+        highest = jnp.max(scores, axis=1, keepdims=True)
+        expo = jnp.exp(scores - highest)
+        total = jnp.sum(expo, axis=1, keepdims=True)
+        mixed = jnp.dot(expo.astype(BF16), values, preferred_element_type=F32) / total
+        out_ref[place, :] = mixed.astype(BF16)
+
+
+VMEM = pl.BlockSpec(memory_space=pltpu.VMEM)
+SMEM = pl.BlockSpec(memory_space=pltpu.SMEM)
+
+
+def call(body, shape, in_specs, scratch=(), flops=0, moved=0):
+    return pl.pallas_call(
+        body,
+        out_shape=jax.ShapeDtypeStruct(*shape),
+        in_specs=in_specs,
+        out_specs=VMEM,
+        scratch_shapes=scratch,
+        cost_estimate=pl.CostEstimate(flops=flops, bytes_accessed=moved, transcendentals=0),
+        compiler_params=pltpu.CompilerParams(vmem_limit_bytes=32 * 1024 * 1024),
+    )
+
+
+def on_ring(
+    q_latent, kv_new, kv_cache, index_q, index_weight, index_keys, block_list, context_len
+):
+    count = lax.axis_size("ctx")
+    tile_len, head_count, width = q_latent.shape[1:]
+    latent = width - DR
+    rows = kv_cache.shape[1]
+    chosen = block_list[0, 0]
+    top = 256
+    low = width - top
+    pages = kv_cache[0].T
+    query = jnp.transpose(q_latent[0], (0, 2, 1))
+
+    def shift(x, by):
+        return lax.ppermute(x, "ctx", [(i, (i + by) % count) for i in range(count)])
+
+    def swap(x):
+        return lax.ppermute(x, "ctx", [(i, i ^ 1) for i in range(count)])
+
+    whole = width + rows + 16
+    own = call(
+        functools.partial(prep_kernel, width, count), ((whole, rows), BF16), [SMEM, VMEM, VMEM], moved=2 * whole * rows * 2
+    )(chosen, pages, index_keys[0])
+    near = swap(own)
+    below = shift(own, 2)
+    above = shift(own, -2)
+    far = shift(own, 4)
+    flags = near[width + rows :, :]
+    two = swap(
+        call(functools.partial(pick_two_kernel, width), ((width + 2 * rows, rows), BF16), [VMEM] * 3)(flags, below, above)
+    )
+    one = swap(
+        call(functools.partial(pick_one_kernel, width, top), ((low + rows, rows), BF16), [VMEM] * 2)(flags, far)
+    )
+    q_rows = call(q_rows_kernel, ((tile_len * head_count, width), BF16), [VMEM], moved=4 * tile_len * head_count * width)(query)
+    index_rows = index_q[0].reshape(-1, index_q.shape[3])
+    block_score = call(
+        functools.partial(index_kernel, count, width, low),
+        ((tile_len, 2 * count), F32),
+        [SMEM] + [VMEM] * 9,
+        [pltpu.VMEM((2 * count, index_rows.shape[0]), F32)],
+    )(context_len, index_weight[0], index_rows, own, near, below, above, far, two, one)
+    wide = -(-(chosen.shape[0] * BLK + tile_len) // 128) * 128
+    attended = call(
+        functools.partial(attend_kernel, count, width, latent, top),
+        ((tile_len * head_count, latent), BF16),
+        [SMEM] * 2 + [VMEM] * 9,
+        [pltpu.VMEM((7, top, rows), BF16), pltpu.VMEM((7, low, rows), BF16), pltpu.VMEM((wide, width), BF16)],
+    )(chosen, context_len, q_rows, kv_new[0], own, near, below, above, far, two, one)
+    return attended.reshape(1, tile_len, head_count, latent), block_score[None]
 
 
 def on_device(
@@ -84,7 +309,7 @@
         P(("groups", "batch")),
     )
     return jax.shard_map(
-        on_device,
+        on_ring if mesh.shape["ctx"] == 8 else on_device,
         mesh=mesh,
         in_specs=placed,
         out_specs=(P(("groups", "batch"), "ctx", None, None), P(("groups", "batch"), "ctx", None)),

time: 82.2 us -> 38.7 us (0.47)
  blocking collectives: 58.3 us -> 0 us
  waiting for transfers between devices: 0.01 us -> 17.8 us
  other arithmetic: 9.49 us -> 0 us
  Pallas kernels: 0 us -> 8.07 us
  starting transfers between devices: 3.54 us -> 8.82 us
  matrix products: 3.57 us -> 0 us
  local copies, waits for them, and re-layouts: 5.54 us -> 2.44 us
    all_gather x2 -> x0, blocking collectives: 58.3 us -> none  [the longest x1 35.8 us: on_device(): piece = lax.all_gather(index_keys[0], 'ctx', axis=0, tiled=True)]
    ppermute x0 -> x6, waiting for transfers between devices: none -> 17.8 us  [the longest x3 14.3 us: shift(): return lax.ppermute(x, 'ctx', [(i, (i + by) % count) for i in range(count)])]
    ppermute x0 -> x6, starting transfers between devices: none -> 8.82 us  [the longest x3 4.61 us: shift(): return lax.ppermute(x, 'ctx', [(i, (i + by) % count) for i in range(count)])]
    scatter-add x1 -> x0, other arithmetic: 8.14 us -> none  [on_device(): jax.ops.segment_sum(weighted.T, positions // BLK, num_segments=block_total)]
    pallas_call x0 -> x6, Pallas kernels: none -> 8.07 us  [the longest x1 5.43 us: on_ring(): call(functools.partial(attend_kernel, count, width, latent, top), ((tile_...]
    dot_general x4 -> x0, matrix products: 3.57 us -> none  [the longest x1 1.74 us: on_device(): jnp.dot(probs, key_rows[:, :latent_width], preferred_element_type=jnp.flo...]
    all_to_all x1 -> x0, starting transfers between devices: 3.54 us -> none  [on_device(): lax.all_to_all(outgoing, 'ctx', split_axis=0, concat_axis=0, tiled=True)]
    gather x2 -> x0, local copies, waits for them, and re-layouts: 1.27 us -> none  [the longest x1 0.67 us: on_device(): own_blocks[slot_index]]
  transfers between devices with their start and end apart: 1 -> 6, of which waited for: 0 -> 4; matrix products, arithmetic and copies ran while one was open for 15% -> 0% of each run, Pallas kernels for 0% -> 2%
where the time goes in v1:
time: 38.7 us; the launch traced here: 38.5 us
  waiting for transfers between devices  17.8 us (46%)
  starting transfers between devices  8.82 us (23%)
  Pallas kernels  8.07 us (21%)
  local copies, waits for them, and re-layouts  2.44 us (6%)
  between operations  1.38 us (4%)
    ppermute x3, waiting for transfers between devices, shift(): return lax.ppermute(x, 'ctx', [(i, (i + by) % count) for i in range(count)])  14.3 us
    pallas_call x1, Pallas kernels, on_ring(): call(functools.partial(attend_kernel, count, width, latent, top), ((tile_...  5.43 us
    ppermute x3, starting transfers between devices, shift(): return lax.ppermute(x, 'ctx', [(i, (i + by) % count) for i in range(count)])  4.61 us
    ppermute x3, starting transfers between devices, swap(): return lax.ppermute(x, 'ctx', [(i, i ^ 1) for i in range(count)])  4.2 us
    ppermute x3, waiting for transfers between devices, swap(): return lax.ppermute(x, 'ctx', [(i, i ^ 1) for i in range(count)])  3.49 us
    unnamed x16, local copies, waits for them, and re-layouts  2.44 us
    pallas_call x1, Pallas kernels, on_ring(): call(functools.partial(index_kernel, count, width, low), ((tile_len, 2 *...  1.25 us
  transfers between devices with their start and end apart: 6, of which 4 were waited for; matrix products, arithmetic and copies ran while one was open for 0% of the time, Pallas kernels for 2%

profile of v1, /device:TPU:0, one launch (start us, length us, event | category | flops | bytes accessed | tf_op | source)
XLA Modules:
  0.0 38.5 jit_solution(267975394762500318)
XLA Ops:
  0.6 0.0 copy-start
  0.6 0.0 copy-start.1
  0.6 1.0 %copy-done.1 = bf16[1,128,576]{1,2,0:T(8,128)(2,1)S(1)} copy-done((bf16[1,128,576]{1,2,0:T(8,128)(2,1)S(1)}, bf16[1,128,576]{1,2,0:T(8,128)(2,1)}, u32[]{:S(2)}) %copy-start.1) | copy-done | bytes 147480
  1.6 0.8 %copy-done.3 = bf16[1,128,128]{2,1,0:T(8,128)(2,1)S(1)} copy-done((bf16[1,128,128]{2,1,0:T(8,128)(2,1)S(1)}, bf16[1,128,128]{2,1,0:T(8,128)(2,1)}, u32[]{:S(2)}) %copy-start.3) | copy-done | bytes 32792
  2.4 0.7 %copy-done.6 = s32[1,1,4]{2,1,0:T(1,128)S(1)} copy-done((s32[1,1,4]{2,1,0:T(1,128)S(1)}, s32[1,1,4]{2,1,0:T(1,128)}, u32[]{:S(2)}) %copy-start.6) | copy-done | bytes 40
  3.1 0.6 %shard_map.96.own = bf16[720,128]{1,0:T(8,128)(2,1)S(1)} custom-call(s32[4]{0:T(128)S(1)} %bitcast.19, bf16[576,128]{1,0:T(8,128)(2,1)S(1)} %bitcast.14, bf16[128,128]{1,0:T(8,128)(2,1)S(1)} %bitcast.16), custom_call_target="tpu_custom_call" | custom-call | bytes 368640 | tf_op jit(solution)/shard_map/pallas_call | solution.py:207
  3.6 3.0 %collective-permute-start = (bf16[720,128]{1,0:T(8,128)(2,1)S(1)}, bf16[720,128]{1,0:T(8,128)(2,1)S(1)}, u32[]{:S(2)}, u32[]{:S(2)}) collective-permute-start(bf16[720,128]{1,0:T(8,128)(2,1)S(1)} %shard_map.96.own), channel_id=1, source_target_pairs={{0,2},{2,0},{4,6},{6,4},{8,10},{10,8},{12,14},{14,12},{1,3},{3,1},... | collective-permute-start | bytes 552968 | tf_op jit(solution)/shard_map/ppermute | solution.py:204
  6.6 1.6 %collective-permute-start.1 = (bf16[720,128]{1,0:T(8,128)(2,1)S(1)}, bf16[720,128]{1,0:T(8,128)(2,1)S(1)}, u32[]{:S(2)}, u32[]{:S(2)}) collective-permute-start(bf16[720,128]{1,0:T(8,128)(2,1)S(1)} %shard_map.96.own), channel_id=1, source_target_pairs={{0,4},{2,6},{4,8},{6,10},{8,12},{10,14},{12,0},{14,2},{1,5},{3,7},... | collective-permute-start | bytes 552968 | tf_op jit(solution)/shard_map/ppermute | solution.py:201
  8.2 2.2 %collective-permute-start.2 = (bf16[720,128]{1,0:T(8,128)(2,1)S(1)}, bf16[720,128]{1,0:T(8,128)(2,1)S(1)}, u32[]{:S(2)}, u32[]{:S(2)}) collective-permute-start(bf16[720,128]{1,0:T(8,128)(2,1)S(1)} %shard_map.96.own), channel_id=1, source_target_pairs={{0,12},{2,14},{4,0},{6,2},{8,4},{10,6},{12,8},{14,10},{1,13},{3,15... | collective-permute-start | bytes 552968 | tf_op jit(solution)/shard_map/ppermute | solution.py:201
  10.5 0.8 %collective-permute-start.3 = (bf16[720,128]{1,0:T(8,128)(2,1)S(1)}, bf16[720,128]{1,0:T(8,128)(2,1)S(1)}, u32[]{:S(2)}, u32[]{:S(2)}) collective-permute-start(bf16[720,128]{1,0:T(8,128)(2,1)S(1)} %shard_map.96.own), channel_id=1, source_target_pairs={{0,8},{2,10},{4,12},{6,14},{8,0},{10,2},{12,4},{14,6},{1,9},{3,11}... | collective-permute-start | bytes 552968 | tf_op jit(solution)/shard_map/ppermute | solution.py:201
  11.3 0.0 collective-permute-done.near
  11.3 4.8 %collective-permute-done.1.before_ref.below = bf16[720,128]{1,0:T(8,128)(2,1)S(1)} collective-permute-done((bf16[720,128]{1,0:T(8,128)(2,1)S(1)}, bf16[720,128]{1,0:T(8,128)(2,1)S(1)}, u32[]{:S(2)}, u32[]{:S(2)}) %collective-permute-start.1) | collective-permute-done | bytes 184352 | tf_op jit(solution)/shard_map/ppermute | solution.py:201
  16.0 1.9 %collective-permute-done.2.after_ref.above = bf16[720,128]{1,0:T(8,128)(2,1)S(1)} collective-permute-done((bf16[720,128]{1,0:T(8,128)(2,1)S(1)}, bf16[720,128]{1,0:T(8,128)(2,1)S(1)}, u32[]{:S(2)}, u32[]{:S(2)}) %collective-permute-start.2) | collective-permute-done | bytes 184352 | tf_op jit(solution)/shard_map/ppermute | solution.py:201
  18.0 0.2 shard_map.97
  18.2 0.6 %collective-permute-start.4 = (bf16[832,128]{1,0:T(8,128)(2,1)S(1)}, bf16[832,128]{1,0:T(8,128)(2,1)S(1)}, u32[]{:S(2)}, u32[]{:S(2)}) collective-permute-start(bf16[832,128]{1,0:T(8,128)(2,1)S(1)} %shard_map.97), channel_id=1, source_target_pairs={{0,2},{2,0},{4,6},{6,4},{8,10},{10,8},{12,14},{14,12},{1,3},{3,1},... | collective-permute-start | bytes 638984 | tf_op jit(solution)/shard_map/ppermute | solution.py:204
  18.8 7.6 %collective-permute-done.3.far_ref.far = bf16[720,128]{1,0:T(8,128)(2,1)S(1)} collective-permute-done((bf16[720,128]{1,0:T(8,128)(2,1)S(1)}, bf16[720,128]{1,0:T(8,128)(2,1)S(1)}, u32[]{:S(2)}, u32[]{:S(2)}) %collective-permute-start.3) | collective-permute-done | bytes 184352 | tf_op jit(solution)/shard_map/ppermute | solution.py:201
  26.4 0.2 shard_map.98
  26.6 0.0 copy-start.4
  26.7 0.0 copy-start.7
  26.7 0.6 %collective-permute-start.5 = (bf16[448,128]{1,0:T(8,128)(2,1)S(1)}, bf16[448,128]{1,0:T(8,128)(2,1)S(1)}, u32[]{:S(2)}, u32[]{:S(2)}) collective-permute-start(bf16[448,128]{1,0:T(8,128)(2,1)S(1)} %shard_map.98), channel_id=1, source_target_pairs={{0,2},{2,0},{4,6},{6,4},{8,10},{10,8},{12,14},{14,12},{1,3},{3,1},... | collective-permute-start | bytes 344072 | tf_op jit(solution)/shard_map/ppermute | solution.py:204
  27.9 0.0 copy-done
  27.9 0.4 %shard_map.95.q_ref = bf16[1024,576]{1,0:T(8,128)(2,1)S(1)} custom-call(bf16[8,576,128]{2,1,0:T(8,128)(2,1)S(1)} %bitcast.13), custom_call_target="tpu_custom_call" | custom-call | bytes 2359296 | tf_op jit(solution)/shard_map/pallas_call | solution.py:221
  28.3 3.5 %collective-permute-done.5.one = bf16[448,128]{1,0:T(8,128)(2,1)S(1)} collective-permute-done((bf16[448,128]{1,0:T(8,128)(2,1)S(1)}, bf16[448,128]{1,0:T(8,128)(2,1)S(1)}, u32[]{:S(2)}, u32[]{:S(2)}) %collective-permute-start.5) | collective-permute-done | bytes 114720 | tf_op jit(solution)/shard_map/ppermute | solution.py:204
  31.8 0.0 collective-permute-done.4.two
  31.8 0.0 copy-done.4
  31.8 0.0 copy-done.7
  31.8 0.0 copy-start.2
  31.8 0.0 copy-start.5
  31.8 5.4 %shard_map.99 = bf16[1024,512]{1,0:T(8,128)(2,1)} custom-call(s32[4]{0:T(128)S(1)} %bitcast.20, s32[1]{0:T(128)S(6)} %copy.10.length_ref, bf16[1024,576]{1,0:T(8,128)(2,1)S(1)} %shard_map.95.q_ref, bf16[8,576]{1,0:T(8,128)(2,1)S(1)} %bitcast.17, bf16[720,128]{1,0:T(8,128)(2,1)S(1)} %shard_map.96.own, bf16[720,128]{1,0:T(8,128)(2,1)S(1)} %collective-permute-done.near, ...), custom_call_target="tpu_custom_call" | custom-call | tf_op jit(solution)/shard_map/pallas_call | solution.py:230
  37.3 0.0 copy-done.2
  37.3 0.0 copy-done.5
  37.3 1.2 %shard_map.100 = f32[8,16]{1,0:T(8,128)} custom-call(s32[1]{0:T(128)S(6)} %copy.10.length_ref, bf16[8,64]{1,0:T(8,128)(2,1)S(1)} %bitcast.18, bf16[512,128]{1,0:T(8,128)(2,1)S(1)} %bitcast.15, bf16[720,128]{1,0:T(8,128)(2,1)S(1)} %shard_map.96.own, bf16[720,128]{1,0:T(8,128)(2,1)S(1)} %collective-permute-done.near, ...), custom_call_target="tpu_custom_call" | custom-call | tf_op jit(solution)/shard_map/pallas_call | solution.py:223
  (3 shorter events, 0.0 us)
Async XLA Ops:
  0.6 27.3 %copy-start = (bf16[1,8,128,576]{2,3,1,0:T(8,128)(2,1)S(1)}, bf16[1,8,128,576]{2,3,1,0:T(8,128)(2,1)}, u32[]{:S(2)}) copy-start(bf16[1,8,128,576]{2,3,1,0:T(8,128)(2,1)} %param.8) | copy-start | bytes 3538948
  0.6 1.0 %copy-start.1 = (bf16[1,128,576]{1,2,0:T(8,128)(2,1)S(1)}, bf16[1,128,576]{1,2,0:T(8,128)(2,1)}, u32[]{:S(2)}) copy-start(bf16[1,128,576]{1,2,0:T(8,128)(2,1)} %param.10) | copy-start | bytes 442372
  1.6 0.8 %copy-start.3 = (bf16[1,128,128]{2,1,0:T(8,128)(2,1)S(1)}, bf16[1,128,128]{2,1,0:T(8,128)(2,1)}, u32[]{:S(2)}) copy-start(bf16[1,128,128]{2,1,0:T(8,128)(2,1)} %param.13) | copy-start | bytes 98308
  2.4 0.7 %copy-start.6 = (s32[1,1,4]{2,1,0:T(1,128)S(1)}, s32[1,1,4]{2,1,0:T(1,128)}, u32[]{:S(2)}) copy-start(s32[1,1,4]{2,1,0:T(1,128)} %param.14) | copy-start | bytes 52
  3.6 7.6 %collective-permute-start = (bf16[720,128]{1,0:T(8,128)(2,1)S(1)}, bf16[720,128]{1,0:T(8,128)(2,1)S(1)}, u32[]{:S(2)}, u32[]{:S(2)}) collective-permute-start(bf16[720,128]{1,0:T(8,128)(2,1)S(1)} %shard_map.96.own), channel_id=1, source_target_pairs={{0,2},{2,0},{4,6},{6,4},{8,10},{10,8},{12,14},{14,12},{1,3},{3,1},... | collective-permute-start | bytes 552968 | tf_op jit(solution)/shard_map/ppermute | solution.py:204
  6.6 9.4 %collective-permute-start.1 = (bf16[720,128]{1,0:T(8,128)(2,1)S(1)}, bf16[720,128]{1,0:T(8,128)(2,1)S(1)}, u32[]{:S(2)}, u32[]{:S(2)}) collective-permute-start(bf16[720,128]{1,0:T(8,128)(2,1)S(1)} %shard_map.96.own), channel_id=1, source_target_pairs={{0,4},{2,6},{4,8},{6,10},{8,12},{10,14},{12,0},{14,2},{1,5},{3,7},... | collective-permute-start | bytes 552968 | tf_op jit(solution)/shard_map/ppermute | solution.py:201
  8.2 9.8 %collective-permute-start.2 = (bf16[720,128]{1,0:T(8,128)(2,1)S(1)}, bf16[720,128]{1,0:T(8,128)(2,1)S(1)}, u32[]{:S(2)}, u32[]{:S(2)}) collective-permute-start(bf16[720,128]{1,0:T(8,128)(2,1)S(1)} %shard_map.96.own), channel_id=1, source_target_pairs={{0,12},{2,14},{4,0},{6,2},{8,4},{10,6},{12,8},{14,10},{1,13},{3,15... | collective-permute-start | bytes 552968 | tf_op jit(solution)/shard_map/ppermute | solution.py:201
  10.5 16.0 %collective-permute-start.3 = (bf16[720,128]{1,0:T(8,128)(2,1)S(1)}, bf16[720,128]{1,0:T(8,128)(2,1)S(1)}, u32[]{:S(2)}, u32[]{:S(2)}) collective-permute-start(bf16[720,128]{1,0:T(8,128)(2,1)S(1)} %shard_map.96.own), channel_id=1, source_target_pairs={{0,8},{2,10},{4,12},{6,14},{8,0},{10,2},{12,4},{14,6},{1,9},{3,11}... | collective-permute-start | bytes 552968 | tf_op jit(solution)/shard_map/ppermute | solution.py:201
  18.2 13.6 %collective-permute-start.4 = (bf16[832,128]{1,0:T(8,128)(2,1)S(1)}, bf16[832,128]{1,0:T(8,128)(2,1)S(1)}, u32[]{:S(2)}, u32[]{:S(2)}) collective-permute-start(bf16[832,128]{1,0:T(8,128)(2,1)S(1)} %shard_map.97), channel_id=1, source_target_pairs={{0,2},{2,0},{4,6},{6,4},{8,10},{10,8},{12,14},{14,12},{1,3},{3,1},... | collective-permute-start | bytes 638984 | tf_op jit(solution)/shard_map/ppermute | solution.py:204
  26.6 5.2 %copy-start.4 = (bf16[1,8,576]{2,1,0:T(8,128)(2,1)S(1)}, bf16[1,8,576]{2,1,0:T(8,128)(2,1)}, u32[]{:S(2)}) copy-start(bf16[1,8,576]{2,1,0:T(8,128)(2,1)} %param.9) | copy-start | bytes 27652
  26.7 5.2 %copy-start.7 = (s32[1,1,4]{2,1,0:T(1,128)S(1)}, s32[1,1,4]{2,1,0:T(1,128)}, u32[]{:S(2)}) copy-start(s32[1,1,4]{2,1,0:T(1,128)} %param.14) | copy-start | bytes 52
  26.7 5.1 %collective-permute-start.5 = (bf16[448,128]{1,0:T(8,128)(2,1)S(1)}, bf16[448,128]{1,0:T(8,128)(2,1)S(1)}, u32[]{:S(2)}, u32[]{:S(2)}) collective-permute-start(bf16[448,128]{1,0:T(8,128)(2,1)S(1)} %shard_map.98), channel_id=1, source_target_pairs={{0,2},{2,0},{4,6},{6,4},{8,10},{10,8},{12,14},{14,12},{1,3},{3,1},... | collective-permute-start | bytes 344072 | tf_op jit(solution)/shard_map/ppermute | solution.py:204
  31.8 5.5 %copy-start.2 = (bf16[1,8,64,128]{3,2,1,0:T(8,128)(2,1)S(1)}, bf16[1,8,64,128]{3,2,1,0:T(8,128)(2,1)}, u32[]{:S(2)}) copy-start(bf16[1,8,64,128]{3,2,1,0:T(8,128)(2,1)} %param.11) | copy-start | bytes 393220
  31.8 5.5 %copy-start.5 = (bf16[1,8,64]{2,1,0:T(8,128)(2,1)S(1)}, bf16[1,8,64]{2,1,0:T(8,128)(2,1)}, u32[]{:S(2)}) copy-start(bf16[1,8,64]{2,1,0:T(8,128)(2,1)} %param.12) | copy-start | bytes 3076

commit v2 on v0

--- a/solution.py
+++ b/solution.py
@@ -1,6 +1,11 @@
+import functools
+import math
+
 import jax
 import jax.numpy as jnp
 from jax import lax
+from jax.experimental import pallas as pl
+from jax.experimental.pallas import tpu as pltpu
 from jax.sharding import PartitionSpec as P
 
 DR = 64
@@ -9,6 +14,279 @@
 
 softmax_scale = 0.07216878364870322
 neg_fill = -1e30
+F32 = jnp.float32
+BF16 = jnp.bfloat16
+
+
+def nt_dot(a, b):
+    return lax.dot_general(a, b, (((1,), (1,)), ((), ())), preferred_element_type=F32)
+
+
+def turn(x):
+    return jnp.concatenate([x[:, BLK:], x[:, :BLK]], axis=1)
+
+
+def pick_kernel(step, count, width, top, list_ref, line_ref, out_ref):
+    holder = lax.rem(lax.axis_index("ctx") + step, count)
+    asked = jnp.where(list_ref[...] == 2 * holder + 1, 1.0, 0.0)
+    upper = jnp.max(asked, axis=1, keepdims=True) > 0.5
+    low = width - top
+    rows = 2 * BLK
+    lane = lax.broadcasted_iota(jnp.int32, (1, rows), 1)
+    keep = jnp.logical_xor(lane < BLK, upper)
+    first = line_ref[0:low, :].astype(F32)
+    second = line_ref[top:width, :].astype(F32)
+    first = jnp.where(upper, turn(first), first)
+    second = jnp.where(upper, second, turn(second))
+    out_ref[0:low, :] = jnp.where(lane < BLK, first, second).astype(BF16)
+    out_ref[low : low + rows, :] = line_ref[width : width + rows, :]
+
+
+def prepare_kernel(q_hbm, new_hbm, rows_ref, scores_ref, new_rows_ref, q_ref, new_ref, sems):
+    tokens, _, heads = q_ref.shape
+    first = pltpu.make_async_copy(new_hbm, new_ref.at[0:tokens], sems.at[tokens])
+    first.start()
+    copies = [pltpu.make_async_copy(q_hbm.at[t], q_ref.at[t], sems.at[t]) for t in range(tokens)]
+    for copy in copies:
+        copy.start()
+    new_ref[tokens:, :] = jnp.zeros_like(new_ref[tokens:, :])
+    first.wait()
+    new_rows_ref[...] = new_ref[:, 0 : new_rows_ref.shape[1]]
+    column = lax.broadcasted_iota(jnp.int32, (1, new_ref.shape[0]), 1)
+    for t in range(tokens):
+        copies[t].wait()
+        rows_ref[t * heads : (t + 1) * heads, :] = q_ref[t].T
+    scores = nt_dot(rows_ref[...], new_ref[...])
+    for t in range(tokens):
+        place = slice(t * heads, (t + 1) * heads)
+        scores_ref[place, :] = jnp.where(column <= t, scores[place, :], neg_fill)
+
+
+def page_sums(keys, query, room, holder, sums):
+    rows = 2 * BLK
+    row = lax.broadcasted_iota(jnp.int32, (rows, rows), 0)
+    keys = jnp.where(row < room, keys, jnp.zeros((), BF16))
+    activ = jnp.maximum(nt_dot(keys, query), 0.0)
+    sums[pl.ds(2 * holder, 1), :] = jnp.sum(activ[0:BLK, :], axis=0, keepdims=True)
+    sums[pl.ds(2 * holder + 1, 1), :] = jnp.sum(activ[BLK:rows, :], axis=0, keepdims=True)
+
+
+def weigh(weight_ref, sums):
+    weight = weight_ref[...].astype(F32)
+    tokens, heads = weight.shape
+    total = sums.shape[1]
+    lane = lax.broadcasted_iota(jnp.int32, (tokens, total), 1)
+    token = lax.broadcasted_iota(jnp.int32, (tokens, total), 0)
+    wide = jnp.where(lane // heads == token, jnp.concatenate([weight] * tokens, axis=1), 0.0)
+    score = lax.dot_general(
+        wide, sums[...], (((1,), (1,)), ((), ())), precision=lax.Precision.HIGHEST, preferred_element_type=F32
+    )
+    return score * (1.0 / BLK)
+
+
+def early_kernel(
+    count, width, latent, top, list_ref, length_ref, weight_ref, query_ref,
+    own, near, below, above, far, side_below, side_above,
+    score_ref, turned_ref, rows_ref, marks_ref, slots, sums,
+):
+    me = lax.axis_index("ctx")
+    mate = jnp.bitwise_xor(me, 1)
+    last = lax.rem(mate + 4, count)
+    low = width - top
+    rows = 2 * BLK
+    for slot, ref in enumerate((own, above, far, below, near)):
+        slots[slot] = ref[0:width, :]
+    for slot, ref in ((5, side_above), (7, side_below)):
+        slots[slot, 0:top, :] = ref[0:top, :]
+        slots[slot, top:width, :] = turn(ref[0:low, :].astype(F32)).astype(BF16)
+    slots[6] = jnp.zeros((width, rows), BF16)
+    lane = lax.broadcasted_iota(jnp.int32, (1, rows), 1)
+    column = lax.broadcasted_iota(jnp.int32, (1, list_ref.shape[0] * BLK), 1)
+    limit = jnp.zeros_like(column)
+    late = jnp.zeros_like(column)
+    length = length_ref[0]
+    pages = list_ref.shape[0]
+    for pair in range(pages // 2):
+        halves = []
+        for j in (2 * pair, 2 * pair + 1):
+            page = list_ref[j]
+            holder, half = page // 2, lax.rem(page, 2)
+            step = lax.rem((holder // 2) - (me // 2) + count // 2, count // 2)
+            same = lax.rem(holder + me, 2) == 0
+            slot = jnp.where(same, step, 4 + step)
+            high = jnp.where(same | (step == 0), half, 0)
+            block = slots[slot].astype(F32)
+            halves.append(jnp.where(high == j - 2 * pair, block, turn(block)))
+            limit = jnp.where(column // BLK == j, length - page * BLK + j * BLK, limit)
+            late = jnp.where((column // BLK == j) & (holder == last), 1, late)
+        block = jnp.where(lane < BLK, halves[0], halves[1]).astype(BF16)
+        place = slice(pair * rows, (pair + 1) * rows)
+        turned_ref[:, place] = block
+        rows_ref[place, :] = block[0:latent, :].T
+    marks_ref[0:1, :] = limit
+    marks_ref[1:2, :] = late
+    marks_ref[2:3, :] = jnp.full_like(column, length - last * rows)
+    query = query_ref[...]
+    sums[pl.ds(2 * last, 1), :] = jnp.zeros((1, sums.shape[1]), F32)
+    sums[pl.ds(2 * last + 1, 1), :] = jnp.zeros((1, sums.shape[1]), F32)
+    for ref, start, holder in (
+        (own, width, me),
+        (near, width, mate),
+        (below, width, me + count - 2),
+        (above, width, me + 2),
+        (far, width, me + 4),
+        (side_below, low, mate + count - 2),
+        (side_above, low, mate + 2),
+    ):
+        holder = lax.rem(holder, count)
+        page_sums(ref[start : start + rows, :], query, length - holder * rows, holder, sums)
+    score_ref[...] = weigh(weight_ref, sums)
+
+
+def attend_kernel(
+    count, width, latent, top, chunk, q_ref, fresh_ref, new_rows, early_turned, early_rows, marks_ref, early_score, side_far, weight_ref, query_ref,
+    out_hbm, score_hbm, turned, key_rows, sums, out_ref, score_ref, sems,
+):
+    me = lax.axis_index("ctx")
+    last = lax.rem(jnp.bitwise_xor(me, 1) + 4, count)
+    low = width - top
+    rows = 2 * BLK
+    sums[...] = jnp.zeros_like(sums)
+    page_sums(side_far[low : low + rows, :], query_ref[...], marks_ref[2:3, 0:rows], last, sums)
+    score_ref[...] = early_score[...] + weigh(weight_ref, sums)
+    steps = q_ref.shape[0] // chunk
+    copies = [pltpu.make_async_copy(score_ref, score_hbm, sems.at[steps])]
+    copies[0].start()
+    lane = lax.broadcasted_iota(jnp.int32, (1, rows), 1)
+    packed = side_far[0:low, :].astype(F32)
+    swapped = turn(packed)
+    first = jnp.concatenate([packed[0:top], swapped], axis=0)
+    second = jnp.concatenate([swapped[0:top], packed], axis=0)
+    both = jnp.where(lane < BLK, first, second).astype(BF16)
+    both_rows = both[0:latent, :].T
+    limit = marks_ref[0:1, :]
+    late = marks_ref[1:2, :]
+    for place in range(0, turned.shape[1], rows):
+        place = slice(place, place + rows)
+        turned[:, place] = jnp.where(late[:, place] == 1, both, early_turned[:, place])
+        down = jnp.broadcast_to(late[:, place].astype(F32), (rows, rows)).T[:, 0:1]
+        key_rows[place, :] = jnp.where(down > 0.5, both_rows, early_rows[place, :])
+    factor = softmax_scale * math.log2(math.e)
+    column = lax.broadcasted_iota(jnp.int32, (1, turned.shape[1]), 1)
+    for step in range(steps):
+        place = slice(step * chunk, (step + 1) * chunk)
+        scores = jnp.dot(q_ref[place, :], turned[...], preferred_element_type=F32)
+        scores = jnp.where(column < limit, scores, neg_fill)
+        fresh = fresh_ref[place, :]
+        highest = jnp.maximum(jnp.max(scores, axis=1, keepdims=True), jnp.max(fresh, axis=1, keepdims=True))
+        expo = jnp.exp2((scores - highest) * factor)
+        expo_new = jnp.exp2((fresh - highest) * factor)
+        total = jnp.sum(expo, axis=1, keepdims=True) + jnp.sum(expo_new, axis=1, keepdims=True)
+        probs = jnp.concatenate([expo.astype(BF16), expo_new.astype(BF16)], axis=1)
+        values = jnp.concatenate([key_rows[...], new_rows[...]], axis=0)
+        mixed = jnp.dot(probs, values, preferred_element_type=F32)
+        out_ref[place, :] = (mixed / total).astype(BF16)
+        copies.append(pltpu.make_async_copy(out_ref.at[place], out_hbm.at[place], sems.at[step]))
+        copies[-1].start()
+    for copy in copies:
+        copy.wait()
+
+
+VMEM = pl.BlockSpec(memory_space=pltpu.VMEM)
+SMEM = pl.BlockSpec(memory_space=pltpu.SMEM)
+
+
+ANY = pl.BlockSpec(memory_space=pl.ANY)
+
+
+def call(body, shapes, in_specs, out_specs=VMEM, scratch=(), flops=0, moved=0, vmem=32):
+    return pl.pallas_call(
+        body,
+        out_shape=shapes,
+        in_specs=in_specs,
+        out_specs=out_specs,
+        scratch_shapes=scratch,
+        cost_estimate=pl.CostEstimate(flops=flops, bytes_accessed=moved, transcendentals=0),
+        compiler_params=pltpu.CompilerParams(vmem_limit_bytes=vmem * 1024 * 1024),
+    )
+
+
+def on_ring(
+    q_latent, kv_new, kv_cache, index_q, index_weight, index_keys, block_list, context_len
+):
+    count = lax.axis_size("ctx")
+    tile_len, head_count, width = q_latent.shape[1:]
+    latent = width - DR
+    rows = kv_cache.shape[1]
+    chosen = block_list[0, 0]
+    top = 256
+    low = width - top
+    pages = kv_cache[0].T
+    query = jnp.transpose(q_latent[0], (0, 2, 1))
+    shape = jax.ShapeDtypeStruct
+
+    def shift(x, by):
+        return lax.ppermute(x, "ctx", [(i, (i + by) % count) for i in range(count)])
+
+    def swap(x):
+        return lax.ppermute(x, "ctx", [(i, i ^ 1) for i in range(count)])
+
+    def pick(step, line):
+        body = functools.partial(pick_kernel, step, count, width, top)
+        return call(body, shape((low + rows, rows), BF16), [VMEM] * 2, moved=2 * 10**6)(asked, line)
+
+    own = jnp.concatenate([pages, index_keys[0]], axis=0)
+    below = shift(own, 2)
+    near = swap(own)
+    above = shift(own, -2)
+    asked = swap(block_list[0])
+    query_count = tile_len * head_count
+    index_rows = index_q[0].reshape(-1, index_q.shape[3])
+    q_rows, fresh, new_rows = call(
+        prepare_kernel,
+        (shape((query_count, width), BF16), shape((query_count, 128), F32), shape((128, latent), BF16)),
+        [ANY] * 2,
+        (VMEM,) * 3,
+        [
+            pltpu.VMEM(query.shape, BF16),
+            pltpu.VMEM((128, width), BF16),
+            pltpu.SemaphoreType.DMA((tile_len + 1,)),
+        ],
+        moved=4 * query_count * width,
+        vmem=56,
+    )(query, kv_new[0])
+    below, asked = lax.optimization_barrier((below, asked))
+    far = shift(below, 2)
+    asked, near, q_rows, fresh = lax.optimization_barrier((asked, near, q_rows, fresh))
+    side_below = swap(pick(count - 2, below))
+    side_above = swap(pick(2, above))
+    side_far = swap(pick(4, far))
+    sums = pltpu.VMEM((2 * count, index_rows.shape[0]), F32)
+    columns = chosen.shape[0] * BLK
+    score, turned, key_rows, marks = call(
+        functools.partial(early_kernel, count, width, latent, top),
+        (shape((tile_len, 2 * count), F32), shape((width, columns), BF16), shape((columns, latent), BF16), shape((8, columns), jnp.int32)),
+        [SMEM] * 2 + [VMEM] * 9,
+        (VMEM,) * 4,
+        [pltpu.VMEM((8, width, rows), BF16), sums],
+        moved=4 * query_count * width,
+    )(chosen, context_len, index_weight[0], index_rows, own, near, below, above, far, side_below, side_above)
+    chunk = query_count // 2
+    attended, block_score = call(
+        functools.partial(attend_kernel, count, width, latent, top, chunk),
+        (shape((query_count, latent), BF16), shape((tile_len, 2 * count), F32)),
+        [VMEM] * 10,
+        (ANY, ANY),
+        [
+            pltpu.VMEM((width, columns), BF16),
+            pltpu.VMEM((columns, latent), BF16),
+            sums,
+            pltpu.VMEM((query_count, latent), BF16),
+            pltpu.VMEM((tile_len, 2 * count), F32),
+            pltpu.SemaphoreType.DMA((2 + 1,)),
+        ],
+    )(q_rows, fresh, new_rows, turned, key_rows, marks, score, side_far, index_weight[0], index_rows)
+    return attended.reshape(1, tile_len, head_count, latent), block_score[None]
 
 
 def on_device(
@@ -84,7 +362,7 @@
         P(("groups", "batch")),
     )
     return jax.shard_map(
-        on_device,
+        on_ring if mesh.shape["ctx"] == 8 else on_device,
         mesh=mesh,
         in_specs=placed,
         out_specs=(P(("groups", "batch"), "ctx", None, None), P(("groups", "batch"), "ctx", None)),

time: 82.2 us -> 27.2 us (0.33)
  blocking collectives: 58.3 us -> 0 us
  other arithmetic: 9.49 us -> 0.98 us
  starting transfers between devices: 3.54 us -> 11.4 us
  Pallas kernels: 0 us -> 7.43 us
  waiting for transfers between devices: 0.01 us -> 5.71 us
  local copies, waits for them, and re-layouts: 5.54 us -> 0.04 us
  matrix products: 3.57 us -> 0 us
    all_gather x2 -> x0, blocking collectives: 58.3 us -> none  [the longest x1 35.8 us: on_device(): piece = lax.all_gather(index_keys[0], 'ctx', axis=0, tiled=True)]
    ppermute x0 -> x8, starting transfers between devices: none -> 11.4 us  [the longest x5 5.83 us: swap(): return lax.ppermute(x, 'ctx', [(i, i ^ 1) for i in range(count)])]
    scatter-add x1 -> x0, other arithmetic: 8.14 us -> none  [on_device(): jax.ops.segment_sum(weighted.T, positions // BLK, num_segments=block_total)]
    pallas_call x0 -> x6, Pallas kernels: none -> 7.43 us  [the longest x1 3.34 us: on_ring(): call(prepare_kernel, (shape((query_count, width), BF16), shape((query_cou...]
    ppermute x0 -> x8, waiting for transfers between devices: none -> 5.71 us  [the longest x5 4.45 us: swap(): return lax.ppermute(x, 'ctx', [(i, i ^ 1) for i in range(count)])]
    dot_general x4 -> x0, matrix products: 3.57 us -> none  [the longest x1 1.74 us: on_device(): jnp.dot(probs, key_rows[:, :latent_width], preferred_element_type=jnp.flo...]
    all_to_all x1 -> x0, starting transfers between devices: 3.54 us -> none  [on_device(): lax.all_to_all(outgoing, 'ctx', split_axis=0, concat_axis=0, tiled=True)]
    unnamed x16 -> x12, local copies, waits for them, and re-layouts: 3.23 us -> 0.04 us
  transfers between devices with their start and end apart: 1 -> 8, of which waited for: 0 -> 3; matrix products, arithmetic and copies ran while one was open for 15% -> 0% of each run, Pallas kernels for 0% -> 19%
where the time goes in v2:
time: 27.2 us; the launch traced here: 27 us
  starting transfers between devices  11.4 us (42%)
  Pallas kernels  7.43 us (27%)
  waiting for transfers between devices  5.71 us (21%)
  between operations  1.41 us (5%)
  other arithmetic  0.98 us (4%)
    ppermute x5, starting transfers between devices, swap(): return lax.ppermute(x, 'ctx', [(i, i ^ 1) for i in range(count)])  5.83 us
    ppermute x3, starting transfers between devices, shift(): return lax.ppermute(x, 'ctx', [(i, (i + by) % count) for i in range(count)])  5.56 us
    ppermute x5, waiting for transfers between devices, swap(): return lax.ppermute(x, 'ctx', [(i, i ^ 1) for i in range(count)])  4.45 us
    pallas_call x1, Pallas kernels, on_ring(): call(prepare_kernel, (shape((query_count, width), BF16), shape((query_cou...  3.34 us
    pallas_call x1, Pallas kernels, on_ring(): call(functools.partial(attend_kernel, count, width, latent, top, chunk),...  2.34 us
    pallas_call x1, Pallas kernels, on_ring(): call(functools.partial(early_kernel, count, width, latent, top), (shape((...  1.34 us
    ppermute x3, waiting for transfers between devices, shift(): return lax.ppermute(x, 'ctx', [(i, (i + by) % count) for i in range(count)])  1.26 us
    concatenate x1, other arithmetic, on_ring(): own = jnp.concatenate([pages, index_keys[0]], axis=0)  0.98 us
  transfers between devices with their start and end apart: 8, of which 3 were waited for; matrix products, arithmetic and copies ran while one was open for 0% of the time, Pallas kernels for 19%

profile of v2, /device:TPU:0, one launch (start us, length us, event | category | flops | bytes accessed | tf_op | source)
XLA Modules:
  0.0 27.0 jit_solution(13915244767035364704)
XLA Ops:
  0.6 0.0 copy-start.5
  0.6 0.0 copy-start.4
  0.7 0.0 copy-start.2
  0.7 1.0 %pad_maximum_fusion.own = bf16[704,128]{1,0:T(8,128)(2,1)S(1)} fusion(bf16[128,128]{1,0:T(8,128)(2,1)} %bitcast.22, bf16[576,128]{1,0:T(8,128)(2,1)} %bitcast.21), kind=kLoop, calls=%fused_computation | loop fusion | flops 360448 | bytes 360448 | tf_op jit(solution)/shard_map/concatenate | solution.py:238
  1.6 3.1 %collective-permute-start = (bf16[704,128]{1,0:T(8,128)(2,1)S(1)}, bf16[704,128]{1,0:T(8,128)(2,1)S(1)}, u32[]{:S(2)}, u32[]{:S(2)}) collective-permute-start(bf16[704,128]{1,0:T(8,128)(2,1)S(1)} %pad_maximum_fusion.own), channel_id=1, source_target_pairs={{0,4},{2,6},{4,8},{6,10},{8,12},{10,14},{12,0},{14,2},{1,5},{3,7},... | collective-permute-start | bytes 540680 | tf_op jit(solution)/shard_map/ppermute | solution.py:229
  4.7 1.5 %collective-permute-start.2 = (bf16[704,128]{1,0:T(8,128)(2,1)S(1)}, bf16[704,128]{1,0:T(8,128)(2,1)S(1)}, u32[]{:S(2)}, u32[]{:S(2)}) collective-permute-start(bf16[704,128]{1,0:T(8,128)(2,1)S(1)} %pad_maximum_fusion.own), channel_id=1, source_target_pairs={{0,2},{2,0},{4,6},{6,4},{8,10},{10,8},{12,14},{14,12},{1,3},{3,1},... | collective-permute-start | bytes 540680 | tf_op jit(solution)/shard_map/ppermute | solution.py:232
  6.2 2.2 %collective-permute-start.3 = (bf16[704,128]{1,0:T(8,128)(2,1)S(1)}, bf16[704,128]{1,0:T(8,128)(2,1)S(1)}, u32[]{:S(2)}, u32[]{:S(2)}) collective-permute-start(bf16[704,128]{1,0:T(8,128)(2,1)S(1)} %pad_maximum_fusion.own), channel_id=1, source_target_pairs={{0,12},{2,14},{4,0},{6,2},{8,4},{10,6},{12,8},{14,10},{1,13},{3,15... | collective-permute-start | bytes 540680 | tf_op jit(solution)/shard_map/ppermute | solution.py:229
  8.5 0.4 %collective-permute-start.1 = (s32[1,4]{1,0:T(1,128)}, s32[1,4]{1,0:T(1,128)S(1)}, u32[]{:S(2)}, u32[]{:S(2)}) collective-permute-start(s32[1,4]{1,0:T(1,128)} %bitcast.18), channel_id=1, source_target_pairs={{0,2},{2,0},{4,6},{6,4},{8,10},{10,8},{12,14},{14,12},{1,3},{3,1},... | collective-permute-start | bytes 56 | tf_op jit(solution)/shard_map/ppermute | solution.py:232
  8.9 3.3 %collective-permute-done.1.list_ref = s32[1,4]{1,0:T(1,128)S(1)} collective-permute-done((s32[1,4]{1,0:T(1,128)}, s32[1,4]{1,0:T(1,128)S(1)}, u32[]{:S(2)}, u32[]{:S(2)}) %collective-permute-start.1) | collective-permute-done | bytes 48 | tf_op jit(solution)/shard_map/ppermute | solution.py:232
  12.1 0.0 collective-permute-done.line_ref.below
  12.1 0.2 collective-permute-start.4
  12.4 3.3 %shard_map.95 = (bf16[1024,576]{1,0:T(8,128)(2,1)}, f32[1024,128]{1,0:T(8,128)}, bf16[128,512]{1,0:T(8,128)(2,1)}) custom-call(bf16[8,576,128]{2,1,0:T(8,128)(2,1)} %bitcast.20, bf16[8,576]{1,0:T(8,128)(2,1)} %bitcast.23), custom_call_target="tpu_custom_call" | custom-call | bytes 2359296 | tf_op jit(solution)/shard_map/pallas_call | solution.py:245
  15.7 0.0 copy-start
  15.7 0.0 copy-start.1
  15.8 0.0 copy-start.3
  15.8 0.0 collective-permute-done.2.near
  15.8 0.1 shard_map.96
  15.9 1.6 %collective-permute-start.5 = (bf16[448,128]{1,0:T(8,128)(2,1)S(1)}, bf16[448,128]{1,0:T(8,128)(2,1)S(1)}, u32[]{:S(2)}, u32[]{:S(2)}) collective-permute-start(bf16[448,128]{1,0:T(8,128)(2,1)S(1)} %shard_map.96), channel_id=1, source_target_pairs={{0,2},{2,0},{4,6},{6,4},{8,10},{10,8},{12,14},{14,12},{1,3},{3,1},... | collective-permute-start | bytes 344072 | tf_op jit(solution)/shard_map/ppermute | solution.py:232
  17.5 0.0 collective-permute-done.3.line_ref.above
  17.5 0.1 shard_map.97
  17.7 0.6 %collective-permute-start.6 = (bf16[448,128]{1,0:T(8,128)(2,1)S(1)}, bf16[448,128]{1,0:T(8,128)(2,1)S(1)}, u32[]{:S(2)}, u32[]{:S(2)}) collective-permute-start(bf16[448,128]{1,0:T(8,128)(2,1)S(1)} %shard_map.97), channel_id=1, source_target_pairs={{0,2},{2,0},{4,6},{6,4},{8,10},{10,8},{12,14},{14,12},{1,3},{3,1},... | collective-permute-start | bytes 344072 | tf_op jit(solution)/shard_map/ppermute | solution.py:232
  18.2 1.3 %collective-permute-done.4.far.line_ref = bf16[704,128]{1,0:T(8,128)(2,1)S(1)} collective-permute-done((bf16[704,128]{1,0:T(8,128)(2,1)S(1)}, bf16[704,128]{1,0:T(8,128)(2,1)S(1)}, u32[]{:S(2)}, u32[]{:S(2)}) %collective-permute-start.4) | collective-permute-done | bytes 180256 | tf_op jit(solution)/shard_map/ppermute | solution.py:229
  19.5 0.1 shard_map.99
  19.6 1.8 %collective-permute-start.7 = (bf16[448,128]{1,0:T(8,128)(2,1)S(1)}, bf16[448,128]{1,0:T(8,128)(2,1)S(1)}, u32[]{:S(2)}, u32[]{:S(2)}) collective-permute-start(bf16[448,128]{1,0:T(8,128)(2,1)S(1)} %shard_map.99), channel_id=1, source_target_pairs={{0,2},{2,0},{4,6},{6,4},{8,10},{10,8},{12,14},{14,12},{1,3},{3,1},... | collective-permute-start | bytes 344072 | tf_op jit(solution)/shard_map/ppermute | solution.py:232
  22.1 0.0 collective-permute-done.5.side_below
  22.1 1.2 %collective-permute-done.6.side_above = bf16[448,128]{1,0:T(8,128)(2,1)S(1)} collective-permute-done((bf16[448,128]{1,0:T(8,128)(2,1)S(1)}, bf16[448,128]{1,0:T(8,128)(2,1)S(1)}, u32[]{:S(2)}, u32[]{:S(2)}) %collective-permute-start.6) | collective-permute-done | bytes 114720 | tf_op jit(solution)/shard_map/ppermute | solution.py:232
  23.2 0.0 copy-done.5
  23.2 0.0 copy-done.4
  23.2 1.3 %shard_map.98 = (f32[8,16]{1,0:T(8,128)S(1)}, bf16[576,256]{1,0:T(8,128)(2,1)S(1)}, bf16[256,512]{1,0:T(8,128)(2,1)S(1)}, s32[8,256]{1,0:T(8,128)S(1)}) custom-call(s32[4]{0:T(128)S(1)} %bitcast.19, s32[1]{0:T(128)S(6)} %copy.10.length_ref, bf16[8,64]{1,0:T(8,128)(2,1)S(1)} %bitcast.16, bf16[512,128]{1,0:T(8,128)(2,1)S(1)} %bitcast.14, ...), custom_call_target="tpu_custom_call" | custom-call | bytes 2359296 | tf_op jit(solution)/shard_map/pallas_call | solution.py:266
  24.6 0.0 collective-permute-done.7.side_far
  24.6 0.0 copy-done.1
  24.6 2.3 %shard_map.100 = (bf16[1024,512]{1,0:T(8,128)(2,1)}, f32[8,16]{1,0:T(8,128)}) custom-call(bf16[1024,576]{1,0:T(8,128)(2,1)S(1)} %copy-done, f32[1024,128]{1,0:T(8,128)S(1)} %copy-done.1, bf16[128,512]{1,0:T(8,128)(2,1)S(1)} %copy-done.3, bf16[576,256]{1,0:T(8,128)(2,1)S(1)} %get-tuple-element.26.early_turned, ...), custom_call_target="tpu_custom_call" | custom-call | tf_op jit(solution)/shard_map/pallas_call | solution.py:275
  (3 shorter events, 0.0 us)
Async XLA Ops:
  0.6 22.6 %copy-start.5 = (s32[1,1,4]{2,1,0:T(1,128)S(1)}, s32[1,1,4]{2,1,0:T(1,128)}, u32[]{:S(2)}) copy-start(s32[1,1,4]{2,1,0:T(1,128)} %param.14) | copy-start | bytes 52
  0.6 22.6 %copy-start.4 = (bf16[1,8,64]{2,1,0:T(8,128)(2,1)S(1)}, bf16[1,8,64]{2,1,0:T(8,128)(2,1)}, u32[]{:S(2)}) copy-start(bf16[1,8,64]{2,1,0:T(8,128)(2,1)} %param.12) | copy-start | bytes 3076
  0.7 22.6 %copy-start.2 = (bf16[1,8,64,128]{3,2,1,0:T(8,128)(2,1)S(1)}, bf16[1,8,64,128]{3,2,1,0:T(8,128)(2,1)}, u32[]{:S(2)}) copy-start(bf16[1,8,64,128]{3,2,1,0:T(8,128)(2,1)} %param.11) | copy-start | bytes 393220
  1.6 10.5 %collective-permute-start = (bf16[704,128]{1,0:T(8,128)(2,1)S(1)}, bf16[704,128]{1,0:T(8,128)(2,1)S(1)}, u32[]{:S(2)}, u32[]{:S(2)}) collective-permute-start(bf16[704,128]{1,0:T(8,128)(2,1)S(1)} %pad_maximum_fusion.own), channel_id=1, source_target_pairs={{0,4},{2,6},{4,8},{6,10},{8,12},{10,14},{12,0},{14,2},{1,5},{3,7},... | collective-permute-start | bytes 540680 | tf_op jit(solution)/shard_map/ppermute | solution.py:229
  4.7 11.0 %collective-permute-start.2 = (bf16[704,128]{1,0:T(8,128)(2,1)S(1)}, bf16[704,128]{1,0:T(8,128)(2,1)S(1)}, u32[]{:S(2)}, u32[]{:S(2)}) collective-permute-start(bf16[704,128]{1,0:T(8,128)(2,1)S(1)} %pad_maximum_fusion.own), channel_id=1, source_target_pairs={{0,2},{2,0},{4,6},{6,4},{8,10},{10,8},{12,14},{14,12},{1,3},{3,1},... | collective-permute-start | bytes 540680 | tf_op jit(solution)/shard_map/ppermute | solution.py:232
  6.2 11.3 %collective-permute-start.3 = (bf16[704,128]{1,0:T(8,128)(2,1)S(1)}, bf16[704,128]{1,0:T(8,128)(2,1)S(1)}, u32[]{:S(2)}, u32[]{:S(2)}) collective-permute-start(bf16[704,128]{1,0:T(8,128)(2,1)S(1)} %pad_maximum_fusion.own), channel_id=1, source_target_pairs={{0,12},{2,14},{4,0},{6,2},{8,4},{10,6},{12,8},{14,10},{1,13},{3,15... | collective-permute-start | bytes 540680 | tf_op jit(solution)/shard_map/ppermute | solution.py:229
  8.5 3.7 %collective-permute-start.1 = (s32[1,4]{1,0:T(1,128)}, s32[1,4]{1,0:T(1,128)S(1)}, u32[]{:S(2)}, u32[]{:S(2)}) collective-permute-start(s32[1,4]{1,0:T(1,128)} %bitcast.18), channel_id=1, source_target_pairs={{0,2},{2,0},{4,6},{6,4},{8,10},{10,8},{12,14},{14,12},{1,3},{3,1},... | collective-permute-start | bytes 56 | tf_op jit(solution)/shard_map/ppermute | solution.py:232
  12.1 7.3 %collective-permute-start.4 = (bf16[704,128]{1,0:T(8,128)(2,1)S(1)}, bf16[704,128]{1,0:T(8,128)(2,1)S(1)}, u32[]{:S(2)}, u32[]{:S(2)}) collective-permute-start(bf16[704,128]{1,0:T(8,128)(2,1)S(1)} %collective-permute-done.line_ref.below), channel_id=1, source_target_pairs={{0,4},{2,6},{4,8},{6,10},{8,12},{10,14},{12,0},{14,2},{1,5},{3,7},... | collective-permute-start | bytes 540680 | tf_op jit(solution)/shard_map/ppermute | solution.py:229
  15.7 8.9 %copy-start = (bf16[1024,576]{1,0:T(8,128)(2,1)S(1)}, bf16[1024,576]{1,0:T(8,128)(2,1)}, u32[]{:S(2)}) copy-start(bf16[1024,576]{1,0:T(8,128)(2,1)} %get-tuple-element.20.q_ref) | copy-start | bytes 3538948
  15.7 8.9 %copy-start.1 = (f32[1024,128]{1,0:T(8,128)S(1)}, f32[1024,128]{1,0:T(8,128)}, u32[]{:S(2)}) copy-start(f32[1024,128]{1,0:T(8,128)} %get-tuple-element.21.fresh_ref) | copy-start | bytes 1572868
  15.8 8.9 %copy-start.3 = (bf16[128,512]{1,0:T(8,128)(2,1)S(1)}, bf16[128,512]{1,0:T(8,128)(2,1)}, u32[]{:S(2)}) copy-start(bf16[128,512]{1,0:T(8,128)(2,1)} %get-tuple-element.22.new_rows) | copy-start | bytes 393220
  15.9 6.1 %collective-permute-start.5 = (bf16[448,128]{1,0:T(8,128)(2,1)S(1)}, bf16[448,128]{1,0:T(8,128)(2,1)S(1)}, u32[]{:S(2)}, u32[]{:S(2)}) collective-permute-start(bf16[448,128]{1,0:T(8,128)(2,1)S(1)} %shard_map.96), channel_id=1, source_target_pairs={{0,2},{2,0},{4,6},{6,4},{8,10},{10,8},{12,14},{14,12},{1,3},{3,1},... | collective-permute-start | bytes 344072 | tf_op jit(solution)/shard_map/ppermute | solution.py:232
  17.7 5.6 %collective-permute-start.6 = (bf16[448,128]{1,0:T(8,128)(2,1)S(1)}, bf16[448,128]{1,0:T(8,128)(2,1)S(1)}, u32[]{:S(2)}, u32[]{:S(2)}) collective-permute-start(bf16[448,128]{1,0:T(8,128)(2,1)S(1)} %shard_map.97), channel_id=1, source_target_pairs={{0,2},{2,0},{4,6},{6,4},{8,10},{10,8},{12,14},{14,12},{1,3},{3,1},... | collective-permute-start | bytes 344072 | tf_op jit(solution)/shard_map/ppermute | solution.py:232
  19.6 5.0 %collective-permute-start.7 = (bf16[448,128]{1,0:T(8,128)(2,1)S(1)}, bf16[448,128]{1,0:T(8,128)(2,1)S(1)}, u32[]{:S(2)}, u32[]{:S(2)}) collective-permute-start(bf16[448,128]{1,0:T(8,128)(2,1)S(1)} %shard_map.99), channel_id=1, source_target_pairs={{0,2},{2,0},{4,6},{6,4},{8,10},{10,8},{12,14},{14,12},{1,3},{3,1},... | collective-permute-start | bytes 344072 | tf_op jit(solution)/shard_map/ppermute | solution.py:232

commit v3 on v2

--- a/solution.py
+++ b/solution.py
@@ -26,8 +26,18 @@
     return jnp.concatenate([x[:, BLK:], x[:, :BLK]], axis=1)
 
 
-def pick_kernel(step, count, width, top, list_ref, line_ref, out_ref):
-    holder = lax.rem(lax.axis_index("ctx") + step, count)
+RING = (0, 2, 3, 1)
+
+
+def ring_steps(me):
+    level = me // 2
+    odd = jnp.bitwise_xor(level, level // 2) % 2 != lax.axis_index("batch")
+    return jnp.where(odd, 4, 2), jnp.where(odd, 2, 4), 6
+
+
+def pick_kernel(step, width, top, list_ref, line_ref, out_ref):
+    me = lax.axis_index("ctx")
+    holder = jnp.bitwise_xor(me, ring_steps(me)[step])
     asked = jnp.where(list_ref[...] == 2 * holder + 1, 1.0, 0.0)
     upper = jnp.max(asked, axis=1, keepdims=True) > 0.5
     low = width - top
@@ -42,21 +52,15 @@
     out_ref[low : low + rows, :] = line_ref[width : width + rows, :]
 
 
-def prepare_kernel(q_hbm, new_hbm, rows_ref, scores_ref, new_rows_ref, q_ref, new_ref, sems):
+def prepare_kernel(q_ref, new_ref, rows_ref, scores_ref, new_rows_ref, wide_ref):
     tokens, _, heads = q_ref.shape
-    first = pltpu.make_async_copy(new_hbm, new_ref.at[0:tokens], sems.at[tokens])
-    first.start()
-    copies = [pltpu.make_async_copy(q_hbm.at[t], q_ref.at[t], sems.at[t]) for t in range(tokens)]
-    for copy in copies:
-        copy.start()
-    new_ref[tokens:, :] = jnp.zeros_like(new_ref[tokens:, :])
-    first.wait()
-    new_rows_ref[...] = new_ref[:, 0 : new_rows_ref.shape[1]]
-    column = lax.broadcasted_iota(jnp.int32, (1, new_ref.shape[0]), 1)
+    wide_ref[...] = jnp.zeros_like(wide_ref)
+    wide_ref[0:tokens, :] = new_ref[...]
+    new_rows_ref[...] = wide_ref[:, 0 : new_rows_ref.shape[1]]
+    column = lax.broadcasted_iota(jnp.int32, (1, wide_ref.shape[0]), 1)
     for t in range(tokens):
-        copies[t].wait()
         rows_ref[t * heads : (t + 1) * heads, :] = q_ref[t].T
-    scores = nt_dot(rows_ref[...], new_ref[...])
+    scores = nt_dot(rows_ref[...], wide_ref[...])
     for t in range(tokens):
         place = slice(t * heads, (t + 1) * heads)
         scores_ref[place, :] = jnp.where(column <= t, scores[place, :], neg_fill)
@@ -85,22 +89,22 @@
 
 
 def early_kernel(
-    count, width, latent, top, list_ref, length_ref, weight_ref, query_ref,
+    width, latent, top, list_ref, length_ref, weight_ref, query_ref,
     own, near, below, above, far, side_below, side_above,
     score_ref, turned_ref, rows_ref, marks_ref, slots, sums,
 ):
     me = lax.axis_index("ctx")
-    mate = jnp.bitwise_xor(me, 1)
-    last = lax.rem(mate + 4, count)
+    behind, ahead, opposite = ring_steps(me)
+    last = jnp.bitwise_xor(me, opposite + 1)
     low = width - top
     rows = 2 * BLK
-    for slot, ref in enumerate((own, above, far, below, near)):
+    lane = lax.broadcasted_iota(jnp.int32, (1, rows), 1)
+    for slot, ref in ((0, own), (1, near), (behind, below), (ahead, above), (opposite, far)):
         slots[slot] = ref[0:width, :]
-    for slot, ref in ((5, side_above), (7, side_below)):
+    for slot, ref in ((behind + 1, side_below), (ahead + 1, side_above)):
         slots[slot, 0:top, :] = ref[0:top, :]
         slots[slot, top:width, :] = turn(ref[0:low, :].astype(F32)).astype(BF16)
-    slots[6] = jnp.zeros((width, rows), BF16)
-    lane = lax.broadcasted_iota(jnp.int32, (1, rows), 1)
+    slots[opposite + 1] = jnp.zeros((width, rows), BF16)
     column = lax.broadcasted_iota(jnp.int32, (1, list_ref.shape[0] * BLK), 1)
     limit = jnp.zeros_like(column)
     late = jnp.zeros_like(column)
@@ -111,10 +115,8 @@
         for j in (2 * pair, 2 * pair + 1):
             page = list_ref[j]
             holder, half = page // 2, lax.rem(page, 2)
-            step = lax.rem((holder // 2) - (me // 2) + count // 2, count // 2)
-            same = lax.rem(holder + me, 2) == 0
-            slot = jnp.where(same, step, 4 + step)
-            high = jnp.where(same | (step == 0), half, 0)
+            slot = jnp.bitwise_xor(holder, me)
+            high = jnp.where((slot == 1) | (lax.rem(slot, 2) == 0), half, 0)
             block = slots[slot].astype(F32)
             halves.append(jnp.where(high == j - 2 * pair, block, turn(block)))
             limit = jnp.where(column // BLK == j, length - page * BLK + j * BLK, limit)
@@ -129,26 +131,26 @@
     query = query_ref[...]
     sums[pl.ds(2 * last, 1), :] = jnp.zeros((1, sums.shape[1]), F32)
     sums[pl.ds(2 * last + 1, 1), :] = jnp.zeros((1, sums.shape[1]), F32)
-    for ref, start, holder in (
-        (own, width, me),
-        (near, width, mate),
-        (below, width, me + count - 2),
-        (above, width, me + 2),
-        (far, width, me + 4),
-        (side_below, low, mate + count - 2),
-        (side_above, low, mate + 2),
+    for ref, start, step in (
+        (own, width, 0),
+        (near, width, 1),
+        (below, width, behind),
+        (above, width, ahead),
+        (far, width, opposite),
+        (side_below, low, behind + 1),
+        (side_above, low, ahead + 1),
     ):
-        holder = lax.rem(holder, count)
+        holder = jnp.bitwise_xor(me, step)
         page_sums(ref[start : start + rows, :], query, length - holder * rows, holder, sums)
     score_ref[...] = weigh(weight_ref, sums)
 
 
 def attend_kernel(
-    count, width, latent, top, chunk, q_ref, fresh_ref, new_rows, early_turned, early_rows, marks_ref, early_score, side_far, weight_ref, query_ref,
+    width, latent, top, chunk, q_ref, fresh_ref, new_rows, early_turned, early_rows, marks_ref, early_score, side_far, weight_ref, query_ref,
     out_hbm, score_hbm, turned, key_rows, sums, out_ref, score_ref, sems,
 ):
     me = lax.axis_index("ctx")
-    last = lax.rem(jnp.bitwise_xor(me, 1) + 4, count)
+    last = jnp.bitwise_xor(me, 7)
     low = width - top
     rows = 2 * BLK
     sums[...] = jnp.zeros_like(sums)
@@ -226,45 +228,47 @@
     shape = jax.ShapeDtypeStruct
 
     def shift(x, by):
-        return lax.ppermute(x, "ctx", [(i, (i + by) % count) for i in range(count)])
+        places = len(RING)
+        pairs = [
+            ((RING[p] * 2 + i) * 2 + core, (RING[(p + (1 - 2 * core) * by) % places] * 2 + i) * 2 + core)
+            for p in range(places)
+            for i in range(2)
+            for core in range(2)
+        ]
+        return lax.ppermute(x, ("ctx", "batch"), pairs)
 
     def swap(x):
         return lax.ppermute(x, "ctx", [(i, i ^ 1) for i in range(count)])
 
     def pick(step, line):
-        body = functools.partial(pick_kernel, step, count, width, top)
+        body = functools.partial(pick_kernel, step, width, top)
         return call(body, shape((low + rows, rows), BF16), [VMEM] * 2, moved=2 * 10**6)(asked, line)
 
     own = jnp.concatenate([pages, index_keys[0]], axis=0)
-    below = shift(own, 2)
+    below = shift(own, 1)
     near = swap(own)
-    above = shift(own, -2)
+    above = shift(own, -1)
     asked = swap(block_list[0])
     query_count = tile_len * head_count
     index_rows = index_q[0].reshape(-1, index_q.shape[3])
     q_rows, fresh, new_rows = call(
         prepare_kernel,
         (shape((query_count, width), BF16), shape((query_count, 128), F32), shape((128, latent), BF16)),
-        [ANY] * 2,
+        [VMEM] * 2,
         (VMEM,) * 3,
-        [
-            pltpu.VMEM(query.shape, BF16),
-            pltpu.VMEM((128, width), BF16),
-            pltpu.SemaphoreType.DMA((tile_len + 1,)),
-        ],
+        [pltpu.VMEM((128, width), BF16)],
         moved=4 * query_count * width,
-        vmem=56,
     )(query, kv_new[0])
-    below, asked = lax.optimization_barrier((below, asked))
-    far = shift(below, 2)
-    asked, near, q_rows, fresh = lax.optimization_barrier((asked, near, q_rows, fresh))
-    side_below = swap(pick(count - 2, below))
-    side_above = swap(pick(2, above))
-    side_far = swap(pick(4, far))
+    below, asked, q_rows, fresh = lax.optimization_barrier((below, asked, q_rows, fresh))
+    far = shift(below, 1)
+    asked, near = lax.optimization_barrier((asked, near))
+    side_below = swap(pick(0, below))
+    side_above = swap(pick(1, above))
+    side_far = swap(pick(2, far))
     sums = pltpu.VMEM((2 * count, index_rows.shape[0]), F32)
     columns = chosen.shape[0] * BLK
     score, turned, key_rows, marks = call(
-        functools.partial(early_kernel, count, width, latent, top),
+        functools.partial(early_kernel, width, latent, top),
         (shape((tile_len, 2 * count), F32), shape((width, columns), BF16), shape((columns, latent), BF16), shape((8, columns), jnp.int32)),
         [SMEM] * 2 + [VMEM] * 9,
         (VMEM,) * 4,
@@ -273,7 +277,7 @@
     )(chosen, context_len, index_weight[0], index_rows, own, near, below, above, far, side_below, side_above)
     chunk = query_count // 2
     attended, block_score = call(
-        functools.partial(attend_kernel, count, width, latent, top, chunk),
+        functools.partial(attend_kernel, width, latent, top, chunk),
         (shape((query_count, latent), BF16), shape((tile_len, 2 * count), F32)),
         [VMEM] * 10,
         (ANY, ANY),

time: 27.2 us -> 26.8 us (0.985)
  Pallas kernels: 7.43 us -> 4.7 us
  local copies, waits for them, and re-layouts: 0.04 us -> 1.99 us
  starting transfers between devices: 11.4 us -> 12.9 us
  waiting for transfers between devices: 5.71 us -> 4.58 us
    pallas_call x1, Pallas kernels: 3.34 us -> 0.55 us  [on_ring(): call(prepare_kernel, (shape((query_count, width), BF16), shape((query_cou...]
    unnamed x12 -> x10, local copies, waits for them, and re-layouts: 0.04 us -> 1.99 us
    ppermute x5, waiting for transfers between devices: 4.45 us -> 2.99 us  [swap(): return lax.ppermute(x, 'ctx', [(i, i ^ 1) for i in range(count)])]
    ppermute x5, starting transfers between devices: 5.83 us -> 6.65 us  [swap(): return lax.ppermute(x, 'ctx', [(i, i ^ 1) for i in range(count)])]
    ppermute x3, starting transfers between devices: 5.56 us -> 6.29 us  [shift(): return lax.ppermute(x, ('ctx', 'batch'), pairs)]
    ppermute x3, waiting for transfers between devices: 1.26 us -> 1.59 us  [shift(): return lax.ppermute(x, ('ctx', 'batch'), pairs)]
  transfers between devices with their start and end apart: 8 -> 8, of which waited for: 3 -> 5; matrix products, arithmetic and copies ran while one was open for 0% -> 0% of each run, Pallas kernels for 19% -> 9%
where the time goes in v3:
time: 26.8 us; the launch traced here: 26.5 us
  starting transfers between devices  12.9 us (48%)
  Pallas kernels  4.7 us (18%)
  waiting for transfers between devices  4.58 us (17%)
  local copies, waits for them, and re-layouts  1.99 us (7%)
  between operations  1.36 us (5%)
  other arithmetic  0.98 us (4%)
    ppermute x5, starting transfers between devices, swap(): return lax.ppermute(x, 'ctx', [(i, i ^ 1) for i in range(count)])  6.65 us
    ppermute x3, starting transfers between devices, shift(): return lax.ppermute(x, ('ctx', 'batch'), pairs)  6.29 us
    ppermute x5, waiting for transfers between devices, swap(): return lax.ppermute(x, 'ctx', [(i, i ^ 1) for i in range(count)])  2.99 us
    pallas_call x1, Pallas kernels, on_ring(): call(functools.partial(attend_kernel, width, latent, top, chunk), (shape(...  2.36 us
    unnamed x10, local copies, waits for them, and re-layouts  1.99 us
    ppermute x3, waiting for transfers between devices, shift(): return lax.ppermute(x, ('ctx', 'batch'), pairs)  1.59 us
    pallas_call x1, Pallas kernels, on_ring(): call(functools.partial(early_kernel, width, latent, top), (shape((tile_le...  1.34 us
    concatenate x1, other arithmetic, on_ring(): own = jnp.concatenate([pages, index_keys[0]], axis=0)  0.98 us
  transfers between devices with their start and end apart: 8, of which 5 were waited for; matrix products, arithmetic and copies ran while one was open for 0% of the time, Pallas kernels for 9%

profile of v3, /device:TPU:0, one launch (start us, length us, event | category | flops | bytes accessed | tf_op | source)
XLA Modules:
  0.0 26.5 jit_solution(2784904467982180265)
XLA Ops:
  0.6 0.0 copy-start.4
  0.6 0.0 copy-start.3
  0.7 0.0 copy-start.1
  0.7 1.0 %pad_maximum_fusion.own = bf16[704,128]{1,0:T(8,128)(2,1)S(1)} fusion(bf16[128,128]{1,0:T(8,128)(2,1)} %bitcast.23, bf16[576,128]{1,0:T(8,128)(2,1)} %bitcast.22), kind=kLoop, calls=%fused_computation | loop fusion | flops 360448 | bytes 360448 | tf_op jit(solution)/shard_map/concatenate | solution.py:247
  1.6 4.1 %collective-permute-start = (bf16[704,128]{1,0:T(8,128)(2,1)S(1)}, bf16[704,128]{1,0:T(8,128)(2,1)S(1)}, u32[]{:S(2)}, u32[]{:S(2)}) collective-permute-start(bf16[704,128]{1,0:T(8,128)(2,1)S(1)} %pad_maximum_fusion.own), channel_id=1, source_target_pairs={{0,8},{1,5},{2,10},{3,7},{8,12},{9,1},{10,14},{11,3},{12,4},{13,9}... | collective-permute-start | bytes 540680 | tf_op jit(solution)/shard_map/ppermute | solution.py:238
  5.7 0.0 collective-permute-start.3
  5.7 1.5 %collective-permute-start.2 = (bf16[704,128]{1,0:T(8,128)(2,1)S(1)}, bf16[704,128]{1,0:T(8,128)(2,1)S(1)}, u32[]{:S(2)}, u32[]{:S(2)}) collective-permute-start(bf16[704,128]{1,0:T(8,128)(2,1)S(1)} %pad_maximum_fusion.own), channel_id=1, source_target_pairs={{0,2},{2,0},{4,6},{6,4},{8,10},{10,8},{12,14},{14,12},{1,3},{3,1},... | collective-permute-start | bytes 540680 | tf_op jit(solution)/shard_map/ppermute | solution.py:241
  7.2 0.5 %collective-permute-start.1 = (s32[1,4]{1,0:T(1,128)}, s32[1,4]{1,0:T(1,128)S(1)}, u32[]{:S(2)}, u32[]{:S(2)}) collective-permute-start(s32[1,4]{1,0:T(1,128)} %bitcast.20), channel_id=1, source_target_pairs={{0,2},{2,0},{4,6},{6,4},{8,10},{10,8},{12,14},{14,12},{1,3},{3,1},... | collective-permute-start | bytes 56 | tf_op jit(solution)/shard_map/ppermute | solution.py:241
  7.8 0.0 copy-start
  7.8 1.3 %copy-done = bf16[1,8,128,576]{2,3,1,0:T(8,128)(2,1)S(1)} copy-done((bf16[1,8,128,576]{2,3,1,0:T(8,128)(2,1)S(1)}, bf16[1,8,128,576]{2,3,1,0:T(8,128)(2,1)}, u32[]{:S(2)}) %copy-start) | copy-done | bytes 1179672
  9.0 0.7 %copy-done.2 = bf16[1,8,576]{2,1,0:T(8,128)(2,1)S(1)} copy-done((bf16[1,8,576]{2,1,0:T(8,128)(2,1)S(1)}, bf16[1,8,576]{2,1,0:T(8,128)(2,1)}, u32[]{:S(2)}) %copy-start.2) | copy-done | bytes 9240
  9.7 0.6 %shard_map.95 = (bf16[1024,576]{1,0:T(8,128)(2,1)S(1)}, f32[1024,128]{1,0:T(8,128)S(1)}, bf16[128,512]{1,0:T(8,128)(2,1)S(1)}) custom-call(bf16[8,576,128]{2,1,0:T(8,128)(2,1)S(1)} %bitcast.14, bf16[8,576]{1,0:T(8,128)(2,1)S(1)} %bitcast.17), custom_call_target="tpu_custom_call" | custom-call | bytes 2359296 | tf_op jit(solution)/shard_map/pallas_call | solution.py:254
  10.3 1.6 %collective-permute-done.1.list_ref = s32[1,4]{1,0:T(1,128)S(1)} collective-permute-done((s32[1,4]{1,0:T(1,128)}, s32[1,4]{1,0:T(1,128)S(1)}, u32[]{:S(2)}, u32[]{:S(2)}) %collective-permute-start.1) | collective-permute-done | bytes 48 | tf_op jit(solution)/shard_map/ppermute | solution.py:241
  11.9 0.1 collective-permute-done.line_ref.below
  12.0 2.2 %collective-permute-start.4 = (bf16[704,128]{1,0:T(8,128)(2,1)S(1)}, bf16[704,128]{1,0:T(8,128)(2,1)S(1)}, u32[]{:S(2)}, u32[]{:S(2)}) collective-permute-start(bf16[704,128]{1,0:T(8,128)(2,1)S(1)} %collective-permute-done.line_ref.below), channel_id=1, source_target_pairs={{0,8},{1,5},{2,10},{3,7},{8,12},{9,1},{10,14},{11,3},{12,4},{13,9}... | collective-permute-start | bytes 540680 | tf_op jit(solution)/shard_map/ppermute | solution.py:238
  14.2 0.0 collective-permute-done.2.near
  14.2 0.2 shard_map.96
  14.4 1.6 %collective-permute-start.5 = (bf16[448,128]{1,0:T(8,128)(2,1)S(1)}, bf16[448,128]{1,0:T(8,128)(2,1)S(1)}, u32[]{:S(2)}, u32[]{:S(2)}) collective-permute-start(bf16[448,128]{1,0:T(8,128)(2,1)S(1)} %shard_map.96), channel_id=1, source_target_pairs={{0,2},{2,0},{4,6},{6,4},{8,10},{10,8},{12,14},{14,12},{1,3},{3,1},... | collective-permute-start | bytes 344072 | tf_op jit(solution)/shard_map/ppermute | solution.py:241
  15.9 0.3 %collective-permute-done.3.line_ref.above = bf16[704,128]{1,0:T(8,128)(2,1)S(1)} collective-permute-done((bf16[704,128]{1,0:T(8,128)(2,1)S(1)}, bf16[704,128]{1,0:T(8,128)(2,1)S(1)}, u32[]{:S(2)}, u32[]{:S(2)}) %collective-permute-start.3) | collective-permute-done | bytes 180256 | tf_op jit(solution)/shard_map/ppermute | solution.py:238
  16.2 0.2 shard_map.97
  16.4 1.5 %collective-permute-start.6 = (bf16[448,128]{1,0:T(8,128)(2,1)S(1)}, bf16[448,128]{1,0:T(8,128)(2,1)S(1)}, u32[]{:S(2)}, u32[]{:S(2)}) collective-permute-start(bf16[448,128]{1,0:T(8,128)(2,1)S(1)} %shard_map.97), channel_id=1, source_target_pairs={{0,2},{2,0},{4,6},{6,4},{8,10},{10,8},{12,14},{14,12},{1,3},{3,1},... | collective-permute-start | bytes 344072 | tf_op jit(solution)/shard_map/ppermute | solution.py:241
  17.9 1.2 %collective-permute-done.4.far.line_ref = bf16[704,128]{1,0:T(8,128)(2,1)S(1)} collective-permute-done((bf16[704,128]{1,0:T(8,128)(2,1)S(1)}, bf16[704,128]{1,0:T(8,128)(2,1)S(1)}, u32[]{:S(2)}, u32[]{:S(2)}) %collective-permute-start.4) | collective-permute-done | bytes 180256 | tf_op jit(solution)/shard_map/ppermute | solution.py:238
  19.1 0.1 shard_map.99
  19.2 1.6 %collective-permute-start.7 = (bf16[448,128]{1,0:T(8,128)(2,1)S(1)}, bf16[448,128]{1,0:T(8,128)(2,1)S(1)}, u32[]{:S(2)}, u32[]{:S(2)}) collective-permute-start(bf16[448,128]{1,0:T(8,128)(2,1)S(1)} %shard_map.99), channel_id=1, source_target_pairs={{0,2},{2,0},{4,6},{6,4},{8,10},{10,8},{12,14},{14,12},{1,3},{3,1},... | collective-permute-start | bytes 344072 | tf_op jit(solution)/shard_map/ppermute | solution.py:241
  21.4 0.0 collective-permute-done.5.side_below
  21.4 1.4 %collective-permute-done.6.side_above = bf16[448,128]{1,0:T(8,128)(2,1)S(1)} collective-permute-done((bf16[448,128]{1,0:T(8,128)(2,1)S(1)}, bf16[448,128]{1,0:T(8,128)(2,1)S(1)}, u32[]{:S(2)}, u32[]{:S(2)}) %collective-permute-start.6) | collective-permute-done | bytes 114720 | tf_op jit(solution)/shard_map/ppermute | solution.py:241
  22.8 0.0 copy-done.4
  22.8 0.0 copy-done.3
  22.8 0.0 copy-done.1
  22.8 1.3 %shard_map.98 = (f32[8,16]{1,0:T(8,128)S(1)}, bf16[576,256]{1,0:T(8,128)(2,1)S(1)}, bf16[256,512]{1,0:T(8,128)(2,1)S(1)}, s32[8,256]{1,0:T(8,128)S(1)}) custom-call(s32[4]{0:T(128)S(1)} %bitcast.21, s32[1]{0:T(128)S(6)} %copy.10.length_ref, bf16[8,64]{1,0:T(8,128)(2,1)S(1)} %bitcast.18, bf16[512,128]{1,0:T(8,128)(2,1)S(1)} %bitcast.15, ...), custom_call_target="tpu_custom_call" | custom-call | bytes 2359296 | tf_op jit(solution)/shard_map/pallas_call | solution.py:270
  24.2 0.0 collective-permute-done.7.side_far
  24.2 2.4 %shard_map.100 = (bf16[1024,512]{1,0:T(8,128)(2,1)}, f32[8,16]{1,0:T(8,128)}) custom-call(bf16[1024,576]{1,0:T(8,128)(2,1)S(1)} %get-tuple-element.19.q_ref, f32[1024,128]{1,0:T(8,128)S(1)} %get-tuple-element.20.fresh_ref, bf16[128,512]{1,0:T(8,128)(2,1)S(1)} %get-tuple-element.21.new_rows, bf16[576,256]{1,0:T(8,128)(2,1)S(1)} %get-tuple-element.26.early_turned, ...), custom_call_target="tpu_custom_call" | custom-call | tf_op jit(solution)/shard_map/pallas_call | solution.py:279
  (1 shorter events, 0.0 us)
Async XLA Ops:
  0.6 22.2 %copy-start.4 = (s32[1,1,4]{2,1,0:T(1,128)S(1)}, s32[1,1,4]{2,1,0:T(1,128)}, u32[]{:S(2)}) copy-start(s32[1,1,4]{2,1,0:T(1,128)} %param.14) | copy-start | bytes 52
  0.6 22.2 %copy-start.3 = (bf16[1,8,64]{2,1,0:T(8,128)(2,1)S(1)}, bf16[1,8,64]{2,1,0:T(8,128)(2,1)}, u32[]{:S(2)}) copy-start(bf16[1,8,64]{2,1,0:T(8,128)(2,1)} %param.12) | copy-start | bytes 3076
  0.7 22.2 %copy-start.1 = (bf16[1,8,64,128]{3,2,1,0:T(8,128)(2,1)S(1)}, bf16[1,8,64,128]{3,2,1,0:T(8,128)(2,1)}, u32[]{:S(2)}) copy-start(bf16[1,8,64,128]{3,2,1,0:T(8,128)(2,1)} %param.11) | copy-start | bytes 393220
  1.6 10.4 %collective-permute-start = (bf16[704,128]{1,0:T(8,128)(2,1)S(1)}, bf16[704,128]{1,0:T(8,128)(2,1)S(1)}, u32[]{:S(2)}, u32[]{:S(2)}) collective-permute-start(bf16[704,128]{1,0:T(8,128)(2,1)S(1)} %pad_maximum_fusion.own), channel_id=1, source_target_pairs={{0,8},{1,5},{2,10},{3,7},{8,12},{9,1},{10,14},{11,3},{12,4},{13,9}... | collective-permute-start | bytes 540680 | tf_op jit(solution)/shard_map/ppermute | solution.py:238
  5.7 10.5 %collective-permute-start.3 = (bf16[704,128]{1,0:T(8,128)(2,1)S(1)}, bf16[704,128]{1,0:T(8,128)(2,1)S(1)}, u32[]{:S(2)}, u32[]{:S(2)}) collective-permute-start(bf16[704,128]{1,0:T(8,128)(2,1)S(1)} %pad_maximum_fusion.own), channel_id=1, source_target_pairs={{0,4},{1,9},{2,6},{3,11},{8,0},{9,13},{10,2},{11,15},{12,8},{13,5}... | collective-permute-start | bytes 540680 | tf_op jit(solution)/shard_map/ppermute | solution.py:238
  5.7 8.5 %collective-permute-start.2 = (bf16[704,128]{1,0:T(8,128)(2,1)S(1)}, bf16[704,128]{1,0:T(8,128)(2,1)S(1)}, u32[]{:S(2)}, u32[]{:S(2)}) collective-permute-start(bf16[704,128]{1,0:T(8,128)(2,1)S(1)} %pad_maximum_fusion.own), channel_id=1, source_target_pairs={{0,2},{2,0},{4,6},{6,4},{8,10},{10,8},{12,14},{14,12},{1,3},{3,1},... | collective-permute-start | bytes 540680 | tf_op jit(solution)/shard_map/ppermute | solution.py:241
  7.2 4.6 %collective-permute-start.1 = (s32[1,4]{1,0:T(1,128)}, s32[1,4]{1,0:T(1,128)S(1)}, u32[]{:S(2)}, u32[]{:S(2)}) collective-permute-start(s32[1,4]{1,0:T(1,128)} %bitcast.20), channel_id=1, source_target_pairs={{0,2},{2,0},{4,6},{6,4},{8,10},{10,8},{12,14},{14,12},{1,3},{3,1},... | collective-permute-start | bytes 56 | tf_op jit(solution)/shard_map/ppermute | solution.py:241
  7.8 1.3 %copy-start = (bf16[1,8,128,576]{2,3,1,0:T(8,128)(2,1)S(1)}, bf16[1,8,128,576]{2,3,1,0:T(8,128)(2,1)}, u32[]{:S(2)}) copy-start(bf16[1,8,128,576]{2,3,1,0:T(8,128)(2,1)} %param.8) | copy-start | bytes 3538948
  9.0 0.7 %copy-start.2 = (bf16[1,8,576]{2,1,0:T(8,128)(2,1)S(1)}, bf16[1,8,576]{2,1,0:T(8,128)(2,1)}, u32[]{:S(2)}) copy-start(bf16[1,8,576]{2,1,0:T(8,128)(2,1)} %param.9) | copy-start | bytes 27652
  12.0 7.0 %collective-permute-start.4 = (bf16[704,128]{1,0:T(8,128)(2,1)S(1)}, bf16[704,128]{1,0:T(8,128)(2,1)S(1)}, u32[]{:S(2)}, u32[]{:S(2)}) collective-permute-start(bf16[704,128]{1,0:T(8,128)(2,1)S(1)} %collective-permute-done.line_ref.below), channel_id=1, source_target_pairs={{0,8},{1,5},{2,10},{3,7},{8,12},{9,1},{10,14},{11,3},{12,4},{13,9}... | collective-permute-start | bytes 540680 | tf_op jit(solution)/shard_map/ppermute | solution.py:238
  14.4 7.0 %collective-permute-start.5 = (bf16[448,128]{1,0:T(8,128)(2,1)S(1)}, bf16[448,128]{1,0:T(8,128)(2,1)S(1)}, u32[]{:S(2)}, u32[]{:S(2)}) collective-permute-start(bf16[448,128]{1,0:T(8,128)(2,1)S(1)} %shard_map.96), channel_id=1, source_target_pairs={{0,2},{2,0},{4,6},{6,4},{8,10},{10,8},{12,14},{14,12},{1,3},{3,1},... | collective-permute-start | bytes 344072 | tf_op jit(solution)/shard_map/ppermute | solution.py:241
  16.4 6.4 %collective-permute-start.6 = (bf16[448,128]{1,0:T(8,128)(2,1)S(1)}, bf16[448,128]{1,0:T(8,128)(2,1)S(1)}, u32[]{:S(2)}, u32[]{:S(2)}) collective-permute-start(bf16[448,128]{1,0:T(8,128)(2,1)S(1)} %shard_map.97), channel_id=1, source_target_pairs={{0,2},{2,0},{4,6},{6,4},{8,10},{10,8},{12,14},{14,12},{1,3},{3,1},... | collective-permute-start | bytes 344072 | tf_op jit(solution)/shard_map/ppermute | solution.py:241
  19.2 5.0 %collective-permute-start.7 = (bf16[448,128]{1,0:T(8,128)(2,1)S(1)}, bf16[448,128]{1,0:T(8,128)(2,1)S(1)}, u32[]{:S(2)}, u32[]{:S(2)}) collective-permute-start(bf16[448,128]{1,0:T(8,128)(2,1)S(1)} %shard_map.99), channel_id=1, source_target_pairs={{0,2},{2,0},{4,6},{6,4},{8,10},{10,8},{12,14},{14,12},{1,3},{3,1},... | collective-permute-start | bytes 344072 | tf_op jit(solution)/shard_map/ppermute | solution.py:241

commit v4 on v3

--- a/solution.py
+++ b/solution.py
@@ -43,7 +43,6 @@
     low = width - top
     rows = 2 * BLK
     lane = lax.broadcasted_iota(jnp.int32, (1, rows), 1)
-    keep = jnp.logical_xor(lane < BLK, upper)
     first = line_ref[0:low, :].astype(F32)
     second = line_ref[top:width, :].astype(F32)
     first = jnp.where(upper, turn(first), first)
@@ -54,9 +53,10 @@
 
 def prepare_kernel(q_ref, new_ref, rows_ref, scores_ref, new_rows_ref, wide_ref):
     tokens, _, heads = q_ref.shape
-    wide_ref[...] = jnp.zeros_like(wide_ref)
-    wide_ref[0:tokens, :] = new_ref[...]
-    new_rows_ref[...] = wide_ref[:, 0 : new_rows_ref.shape[1]]
+    padding = jnp.zeros((wide_ref.shape[0] - tokens, wide_ref.shape[1]), F32)
+    wide = jnp.concatenate([new_ref[...].astype(F32), padding], axis=0).astype(BF16)
+    wide_ref[...] = wide
+    new_rows_ref[...] = wide[:, 0 : new_rows_ref.shape[1]]
     column = lax.broadcasted_iota(jnp.int32, (1, wide_ref.shape[0]), 1)
     for t in range(tokens):
         rows_ref[t * heads : (t + 1) * heads, :] = q_ref[t].T
@@ -146,11 +146,11 @@
 
 
 def attend_kernel(
-    width, latent, top, chunk, q_ref, fresh_ref, new_rows, early_turned, early_rows, marks_ref, early_score, side_far, weight_ref, query_ref,
+    width, latent, top, chunk, q_ref, fresh_ref, new_rows, early_turned, early_rows, marks_ref, early_score, side_far,
+    weight_ref, query_ref,
     out_hbm, score_hbm, turned, key_rows, sums, out_ref, score_ref, sems,
 ):
-    me = lax.axis_index("ctx")
-    last = jnp.bitwise_xor(me, 7)
+    last = jnp.bitwise_xor(lax.axis_index("ctx"), 7)
     low = width - top
     rows = 2 * BLK
     sums[...] = jnp.zeros_like(sums)
@@ -196,20 +196,18 @@
 
 VMEM = pl.BlockSpec(memory_space=pltpu.VMEM)
 SMEM = pl.BlockSpec(memory_space=pltpu.SMEM)
-
-
 ANY = pl.BlockSpec(memory_space=pl.ANY)
 
 
-def call(body, shapes, in_specs, out_specs=VMEM, scratch=(), flops=0, moved=0, vmem=32):
+def call(body, shapes, in_specs, out_specs=VMEM, scratch=(), moved=0):
     return pl.pallas_call(
         body,
         out_shape=shapes,
         in_specs=in_specs,
         out_specs=out_specs,
         scratch_shapes=scratch,
-        cost_estimate=pl.CostEstimate(flops=flops, bytes_accessed=moved, transcendentals=0),
-        compiler_params=pltpu.CompilerParams(vmem_limit_bytes=vmem * 1024 * 1024),
+        cost_estimate=pl.CostEstimate(flops=0, bytes_accessed=moved, transcendentals=0),
+        compiler_params=pltpu.CompilerParams(vmem_limit_bytes=32 * 1024 * 1024),
     )
 
 
@@ -287,7 +285,7 @@
             sums,
             pltpu.VMEM((query_count, latent), BF16),
             pltpu.VMEM((tile_len, 2 * count), F32),
-            pltpu.SemaphoreType.DMA((2 + 1,)),
+            pltpu.SemaphoreType.DMA((3,)),
         ],
     )(q_rows, fresh, new_rows, turned, key_rows, marks, score, side_far, index_weight[0], index_rows)
     return attended.reshape(1, tile_len, head_count, latent), block_score[None]
@@ -366,7 +364,7 @@
         P(("groups", "batch")),
     )
     return jax.shard_map(
-        on_ring if mesh.shape["ctx"] == 8 else on_device,
+        on_ring if mesh.shape["ctx"] == 8 and mesh.shape["batch"] == 2 else on_device,
         mesh=mesh,
         in_specs=placed,
         out_specs=(P(("groups", "batch"), "ctx", None, None), P(("groups", "batch"), "ctx", None)),

time: 26.8 us -> 26.8 us (level)
  no operation moved by 1% of the time
where the time goes in v4:
time: 26.8 us; the launch traced here: 26.5 us
  starting transfers between devices  12.9 us (48%)
  Pallas kernels  4.7 us (18%)
  waiting for transfers between devices  4.58 us (17%)
  local copies, waits for them, and re-layouts  1.99 us (7%)
  between operations  1.36 us (5%)
  other arithmetic  0.98 us (4%)
    ppermute x5, starting transfers between devices, swap(): return lax.ppermute(x, 'ctx', [(i, i ^ 1) for i in range(count)])  6.65 us
    ppermute x3, starting transfers between devices, shift(): return lax.ppermute(x, ('ctx', 'batch'), pairs)  6.29 us
    ppermute x5, waiting for transfers between devices, swap(): return lax.ppermute(x, 'ctx', [(i, i ^ 1) for i in range(count)])  2.99 us
    pallas_call x1, Pallas kernels, on_ring(): call(functools.partial(attend_kernel, width, latent, top, chunk), (shape(...  2.36 us
    unnamed x10, local copies, waits for them, and re-layouts  1.99 us
    ppermute x3, waiting for transfers between devices, shift(): return lax.ppermute(x, ('ctx', 'batch'), pairs)  1.59 us
    pallas_call x1, Pallas kernels, on_ring(): call(functools.partial(early_kernel, width, latent, top), (shape((tile_le...  1.34 us
    concatenate x1, other arithmetic, on_ring(): own = jnp.concatenate([pages, index_keys[0]], axis=0)  0.98 us
  transfers between devices with their start and end apart: 8, of which 5 were waited for; matrix products, arithmetic and copies ran while one was open for 0% of the time, Pallas kernels for 9%

profile of v4, /device:TPU:0, one launch (start us, length us, event | category | flops | bytes accessed | tf_op | source)
XLA Modules:
  0.0 26.5 jit_solution(16011910271190401183)
XLA Ops:
  0.6 0.0 copy-start.4
  0.6 0.0 copy-start.3
  0.7 0.0 copy-start.1
  0.7 1.0 %pad_maximum_fusion.own = bf16[704,128]{1,0:T(8,128)(2,1)S(1)} fusion(bf16[128,128]{1,0:T(8,128)(2,1)} %bitcast.23, bf16[576,128]{1,0:T(8,128)(2,1)} %bitcast.22), kind=kLoop, calls=%fused_computation | loop fusion | flops 360448 | bytes 360448 | tf_op jit(solution)/shard_map/concatenate | solution.py:245
  1.6 4.1 %collective-permute-start = (bf16[704,128]{1,0:T(8,128)(2,1)S(1)}, bf16[704,128]{1,0:T(8,128)(2,1)S(1)}, u32[]{:S(2)}, u32[]{:S(2)}) collective-permute-start(bf16[704,128]{1,0:T(8,128)(2,1)S(1)} %pad_maximum_fusion.own), channel_id=1, source_target_pairs={{0,8},{1,5},{2,10},{3,7},{8,12},{9,1},{10,14},{11,3},{12,4},{13,9}... | collective-permute-start | bytes 540680 | tf_op jit(solution)/shard_map/ppermute | solution.py:236
  5.7 0.0 collective-permute-start.3
  5.7 1.5 %collective-permute-start.2 = (bf16[704,128]{1,0:T(8,128)(2,1)S(1)}, bf16[704,128]{1,0:T(8,128)(2,1)S(1)}, u32[]{:S(2)}, u32[]{:S(2)}) collective-permute-start(bf16[704,128]{1,0:T(8,128)(2,1)S(1)} %pad_maximum_fusion.own), channel_id=1, source_target_pairs={{0,2},{2,0},{4,6},{6,4},{8,10},{10,8},{12,14},{14,12},{1,3},{3,1},... | collective-permute-start | bytes 540680 | tf_op jit(solution)/shard_map/ppermute | solution.py:239
  7.2 0.5 %collective-permute-start.1 = (s32[1,4]{1,0:T(1,128)}, s32[1,4]{1,0:T(1,128)S(1)}, u32[]{:S(2)}, u32[]{:S(2)}) collective-permute-start(s32[1,4]{1,0:T(1,128)} %bitcast.20), channel_id=1, source_target_pairs={{0,2},{2,0},{4,6},{6,4},{8,10},{10,8},{12,14},{14,12},{1,3},{3,1},... | collective-permute-start | bytes 56 | tf_op jit(solution)/shard_map/ppermute | solution.py:239
  7.8 0.0 copy-start
  7.8 1.3 %copy-done = bf16[1,8,128,576]{2,3,1,0:T(8,128)(2,1)S(1)} copy-done((bf16[1,8,128,576]{2,3,1,0:T(8,128)(2,1)S(1)}, bf16[1,8,128,576]{2,3,1,0:T(8,128)(2,1)}, u32[]{:S(2)}) %copy-start) | copy-done | bytes 1179672
  9.0 0.7 %copy-done.2 = bf16[1,8,576]{2,1,0:T(8,128)(2,1)S(1)} copy-done((bf16[1,8,576]{2,1,0:T(8,128)(2,1)S(1)}, bf16[1,8,576]{2,1,0:T(8,128)(2,1)}, u32[]{:S(2)}) %copy-start.2) | copy-done | bytes 9240
  9.7 0.6 %shard_map.95 = (bf16[1024,576]{1,0:T(8,128)(2,1)S(1)}, f32[1024,128]{1,0:T(8,128)S(1)}, bf16[128,512]{1,0:T(8,128)(2,1)S(1)}) custom-call(bf16[8,576,128]{2,1,0:T(8,128)(2,1)S(1)} %bitcast.14, bf16[8,576]{1,0:T(8,128)(2,1)S(1)} %bitcast.17), custom_call_target="tpu_custom_call" | custom-call | bytes 2359296 | tf_op jit(solution)/shard_map/pallas_call | solution.py:252
  10.3 1.6 %collective-permute-done.1.list_ref = s32[1,4]{1,0:T(1,128)S(1)} collective-permute-done((s32[1,4]{1,0:T(1,128)}, s32[1,4]{1,0:T(1,128)S(1)}, u32[]{:S(2)}, u32[]{:S(2)}) %collective-permute-start.1) | collective-permute-done | bytes 48 | tf_op jit(solution)/shard_map/ppermute | solution.py:239
  11.9 0.1 collective-permute-done.line_ref.below
  12.0 2.2 %collective-permute-start.4 = (bf16[704,128]{1,0:T(8,128)(2,1)S(1)}, bf16[704,128]{1,0:T(8,128)(2,1)S(1)}, u32[]{:S(2)}, u32[]{:S(2)}) collective-permute-start(bf16[704,128]{1,0:T(8,128)(2,1)S(1)} %collective-permute-done.line_ref.below), channel_id=1, source_target_pairs={{0,8},{1,5},{2,10},{3,7},{8,12},{9,1},{10,14},{11,3},{12,4},{13,9}... | collective-permute-start | bytes 540680 | tf_op jit(solution)/shard_map/ppermute | solution.py:236
  14.2 0.0 collective-permute-done.2.near
  14.2 0.2 shard_map.96
  14.4 1.6 %collective-permute-start.5 = (bf16[448,128]{1,0:T(8,128)(2,1)S(1)}, bf16[448,128]{1,0:T(8,128)(2,1)S(1)}, u32[]{:S(2)}, u32[]{:S(2)}) collective-permute-start(bf16[448,128]{1,0:T(8,128)(2,1)S(1)} %shard_map.96), channel_id=1, source_target_pairs={{0,2},{2,0},{4,6},{6,4},{8,10},{10,8},{12,14},{14,12},{1,3},{3,1},... | collective-permute-start | bytes 344072 | tf_op jit(solution)/shard_map/ppermute | solution.py:239
  15.9 0.3 %collective-permute-done.3.line_ref.above = bf16[704,128]{1,0:T(8,128)(2,1)S(1)} collective-permute-done((bf16[704,128]{1,0:T(8,128)(2,1)S(1)}, bf16[704,128]{1,0:T(8,128)(2,1)S(1)}, u32[]{:S(2)}, u32[]{:S(2)}) %collective-permute-start.3) | collective-permute-done | bytes 180256 | tf_op jit(solution)/shard_map/ppermute | solution.py:236
  16.2 0.2 shard_map.97
  16.4 1.5 %collective-permute-start.6 = (bf16[448,128]{1,0:T(8,128)(2,1)S(1)}, bf16[448,128]{1,0:T(8,128)(2,1)S(1)}, u32[]{:S(2)}, u32[]{:S(2)}) collective-permute-start(bf16[448,128]{1,0:T(8,128)(2,1)S(1)} %shard_map.97), channel_id=1, source_target_pairs={{0,2},{2,0},{4,6},{6,4},{8,10},{10,8},{12,14},{14,12},{1,3},{3,1},... | collective-permute-start | bytes 344072 | tf_op jit(solution)/shard_map/ppermute | solution.py:239
  17.9 1.2 %collective-permute-done.4.far.line_ref = bf16[704,128]{1,0:T(8,128)(2,1)S(1)} collective-permute-done((bf16[704,128]{1,0:T(8,128)(2,1)S(1)}, bf16[704,128]{1,0:T(8,128)(2,1)S(1)}, u32[]{:S(2)}, u32[]{:S(2)}) %collective-permute-start.4) | collective-permute-done | bytes 180256 | tf_op jit(solution)/shard_map/ppermute | solution.py:236
  19.1 0.1 shard_map.99
  19.2 1.6 %collective-permute-start.7 = (bf16[448,128]{1,0:T(8,128)(2,1)S(1)}, bf16[448,128]{1,0:T(8,128)(2,1)S(1)}, u32[]{:S(2)}, u32[]{:S(2)}) collective-permute-start(bf16[448,128]{1,0:T(8,128)(2,1)S(1)} %shard_map.99), channel_id=1, source_target_pairs={{0,2},{2,0},{4,6},{6,4},{8,10},{10,8},{12,14},{14,12},{1,3},{3,1},... | collective-permute-start | bytes 344072 | tf_op jit(solution)/shard_map/ppermute | solution.py:239
  21.4 0.0 collective-permute-done.5.side_below
  21.4 1.4 %collective-permute-done.6.side_above = bf16[448,128]{1,0:T(8,128)(2,1)S(1)} collective-permute-done((bf16[448,128]{1,0:T(8,128)(2,1)S(1)}, bf16[448,128]{1,0:T(8,128)(2,1)S(1)}, u32[]{:S(2)}, u32[]{:S(2)}) %collective-permute-start.6) | collective-permute-done | bytes 114720 | tf_op jit(solution)/shard_map/ppermute | solution.py:239
  22.8 0.0 copy-done.4
  22.8 0.0 copy-done.3
  22.8 0.0 copy-done.1
  22.8 1.3 %shard_map.98 = (f32[8,16]{1,0:T(8,128)S(1)}, bf16[576,256]{1,0:T(8,128)(2,1)S(1)}, bf16[256,512]{1,0:T(8,128)(2,1)S(1)}, s32[8,256]{1,0:T(8,128)S(1)}) custom-call(s32[4]{0:T(128)S(1)} %bitcast.21, s32[1]{0:T(128)S(6)} %copy.10.length_ref, bf16[8,64]{1,0:T(8,128)(2,1)S(1)} %bitcast.18, bf16[512,128]{1,0:T(8,128)(2,1)S(1)} %bitcast.15, ...), custom_call_target="tpu_custom_call" | custom-call | bytes 2359296 | tf_op jit(solution)/shard_map/pallas_call | solution.py:268
  24.2 0.0 collective-permute-done.7.side_far
  24.2 2.4 %shard_map.100 = (bf16[1024,512]{1,0:T(8,128)(2,1)}, f32[8,16]{1,0:T(8,128)}) custom-call(bf16[1024,576]{1,0:T(8,128)(2,1)S(1)} %get-tuple-element.19.q_ref, f32[1024,128]{1,0:T(8,128)S(1)} %get-tuple-element.20.fresh_ref, bf16[128,512]{1,0:T(8,128)(2,1)S(1)} %get-tuple-element.21.new_rows, bf16[576,256]{1,0:T(8,128)(2,1)S(1)} %get-tuple-element.26.early_turned, ...), custom_call_target="tpu_custom_call" | custom-call | tf_op jit(solution)/shard_map/pallas_call | solution.py:277
  (1 shorter events, 0.0 us)
Async XLA Ops:
  0.6 22.2 %copy-start.4 = (s32[1,1,4]{2,1,0:T(1,128)S(1)}, s32[1,1,4]{2,1,0:T(1,128)}, u32[]{:S(2)}) copy-start(s32[1,1,4]{2,1,0:T(1,128)} %param.14) | copy-start | bytes 52
  0.6 22.2 %copy-start.3 = (bf16[1,8,64]{2,1,0:T(8,128)(2,1)S(1)}, bf16[1,8,64]{2,1,0:T(8,128)(2,1)}, u32[]{:S(2)}) copy-start(bf16[1,8,64]{2,1,0:T(8,128)(2,1)} %param.12) | copy-start | bytes 3076
  0.7 22.2 %copy-start.1 = (bf16[1,8,64,128]{3,2,1,0:T(8,128)(2,1)S(1)}, bf16[1,8,64,128]{3,2,1,0:T(8,128)(2,1)}, u32[]{:S(2)}) copy-start(bf16[1,8,64,128]{3,2,1,0:T(8,128)(2,1)} %param.11) | copy-start | bytes 393220
  1.6 10.4 %collective-permute-start = (bf16[704,128]{1,0:T(8,128)(2,1)S(1)}, bf16[704,128]{1,0:T(8,128)(2,1)S(1)}, u32[]{:S(2)}, u32[]{:S(2)}) collective-permute-start(bf16[704,128]{1,0:T(8,128)(2,1)S(1)} %pad_maximum_fusion.own), channel_id=1, source_target_pairs={{0,8},{1,5},{2,10},{3,7},{8,12},{9,1},{10,14},{11,3},{12,4},{13,9}... | collective-permute-start | bytes 540680 | tf_op jit(solution)/shard_map/ppermute | solution.py:236
  5.7 10.5 %collective-permute-start.3 = (bf16[704,128]{1,0:T(8,128)(2,1)S(1)}, bf16[704,128]{1,0:T(8,128)(2,1)S(1)}, u32[]{:S(2)}, u32[]{:S(2)}) collective-permute-start(bf16[704,128]{1,0:T(8,128)(2,1)S(1)} %pad_maximum_fusion.own), channel_id=1, source_target_pairs={{0,4},{1,9},{2,6},{3,11},{8,0},{9,13},{10,2},{11,15},{12,8},{13,5}... | collective-permute-start | bytes 540680 | tf_op jit(solution)/shard_map/ppermute | solution.py:236
  5.7 8.5 %collective-permute-start.2 = (bf16[704,128]{1,0:T(8,128)(2,1)S(1)}, bf16[704,128]{1,0:T(8,128)(2,1)S(1)}, u32[]{:S(2)}, u32[]{:S(2)}) collective-permute-start(bf16[704,128]{1,0:T(8,128)(2,1)S(1)} %pad_maximum_fusion.own), channel_id=1, source_target_pairs={{0,2},{2,0},{4,6},{6,4},{8,10},{10,8},{12,14},{14,12},{1,3},{3,1},... | collective-permute-start | bytes 540680 | tf_op jit(solution)/shard_map/ppermute | solution.py:239
  7.2 4.6 %collective-permute-start.1 = (s32[1,4]{1,0:T(1,128)}, s32[1,4]{1,0:T(1,128)S(1)}, u32[]{:S(2)}, u32[]{:S(2)}) collective-permute-start(s32[1,4]{1,0:T(1,128)} %bitcast.20), channel_id=1, source_target_pairs={{0,2},{2,0},{4,6},{6,4},{8,10},{10,8},{12,14},{14,12},{1,3},{3,1},... | collective-permute-start | bytes 56 | tf_op jit(solution)/shard_map/ppermute | solution.py:239
  7.8 1.3 %copy-start = (bf16[1,8,128,576]{2,3,1,0:T(8,128)(2,1)S(1)}, bf16[1,8,128,576]{2,3,1,0:T(8,128)(2,1)}, u32[]{:S(2)}) copy-start(bf16[1,8,128,576]{2,3,1,0:T(8,128)(2,1)} %param.8) | copy-start | bytes 3538948
  9.0 0.7 %copy-start.2 = (bf16[1,8,576]{2,1,0:T(8,128)(2,1)S(1)}, bf16[1,8,576]{2,1,0:T(8,128)(2,1)}, u32[]{:S(2)}) copy-start(bf16[1,8,576]{2,1,0:T(8,128)(2,1)} %param.9) | copy-start | bytes 27652
  12.0 7.0 %collective-permute-start.4 = (bf16[704,128]{1,0:T(8,128)(2,1)S(1)}, bf16[704,128]{1,0:T(8,128)(2,1)S(1)}, u32[]{:S(2)}, u32[]{:S(2)}) collective-permute-start(bf16[704,128]{1,0:T(8,128)(2,1)S(1)} %collective-permute-done.line_ref.below), channel_id=1, source_target_pairs={{0,8},{1,5},{2,10},{3,7},{8,12},{9,1},{10,14},{11,3},{12,4},{13,9}... | collective-permute-start | bytes 540680 | tf_op jit(solution)/shard_map/ppermute | solution.py:236
  14.4 7.0 %collective-permute-start.5 = (bf16[448,128]{1,0:T(8,128)(2,1)S(1)}, bf16[448,128]{1,0:T(8,128)(2,1)S(1)}, u32[]{:S(2)}, u32[]{:S(2)}) collective-permute-start(bf16[448,128]{1,0:T(8,128)(2,1)S(1)} %shard_map.96), channel_id=1, source_target_pairs={{0,2},{2,0},{4,6},{6,4},{8,10},{10,8},{12,14},{14,12},{1,3},{3,1},... | collective-permute-start | bytes 344072 | tf_op jit(solution)/shard_map/ppermute | solution.py:239
  16.4 6.4 %collective-permute-start.6 = (bf16[448,128]{1,0:T(8,128)(2,1)S(1)}, bf16[448,128]{1,0:T(8,128)(2,1)S(1)}, u32[]{:S(2)}, u32[]{:S(2)}) collective-permute-start(bf16[448,128]{1,0:T(8,128)(2,1)S(1)} %shard_map.97), channel_id=1, source_target_pairs={{0,2},{2,0},{4,6},{6,4},{8,10},{10,8},{12,14},{14,12},{1,3},{3,1},... | collective-permute-start | bytes 344072 | tf_op jit(solution)/shard_map/ppermute | solution.py:239
  19.2 5.0 %collective-permute-start.7 = (bf16[448,128]{1,0:T(8,128)(2,1)S(1)}, bf16[448,128]{1,0:T(8,128)(2,1)S(1)}, u32[]{:S(2)}, u32[]{:S(2)}) collective-permute-start(bf16[448,128]{1,0:T(8,128)(2,1)S(1)} %shard_map.99), channel_id=1, source_target_pairs={{0,2},{2,0},{4,6},{6,4},{8,10},{10,8},{12,14},{14,12},{1,3},{3,1},... | collective-permute-start | bytes 344072 | tf_op jit(solution)/shard_map/ppermute | solution.py:239

commit v5 on v4

--- a/solution.py
+++ b/solution.py
@@ -219,7 +219,7 @@
     latent = width - DR
     rows = kv_cache.shape[1]
     chosen = block_list[0, 0]
-    top = 256
+    top = width // 2
     low = width - top
     pages = kv_cache[0].T
     query = jnp.transpose(q_latent[0], (0, 2, 1))

time: 26.8 us -> 26.6 us (level)
  transfers between devices with their start and end apart: 8 -> 8, of which waited for: 5 -> 6; matrix products, arithmetic and copies ran while one was open for 0% -> 0% of each run, Pallas kernels for 9% -> 9%
where the time goes in v5:
time: 26.6 us; the launch traced here: 26.3 us
  starting transfers between devices  12.9 us (48%)
  Pallas kernels  4.68 us (18%)
  waiting for transfers between devices  4.38 us (16%)
  local copies, waits for them, and re-layouts  1.99 us (7%)
  between operations  1.36 us (5%)
  other arithmetic  0.98 us (4%)
    ppermute x5, starting transfers between devices, swap(): return lax.ppermute(x, 'ctx', [(i, i ^ 1) for i in range(count)])  6.65 us
    ppermute x3, starting transfers between devices, shift(): return lax.ppermute(x, ('ctx', 'batch'), pairs)  6.29 us
    ppermute x5, waiting for transfers between devices, swap(): return lax.ppermute(x, 'ctx', [(i, i ^ 1) for i in range(count)])  2.79 us
    pallas_call x1, Pallas kernels, on_ring(): call(functools.partial(attend_kernel, width, latent, top, chunk), (shape(...  2.35 us
    unnamed x10, local copies, waits for them, and re-layouts  1.99 us
    ppermute x3, waiting for transfers between devices, shift(): return lax.ppermute(x, ('ctx', 'batch'), pairs)  1.59 us
    pallas_call x1, Pallas kernels, on_ring(): call(functools.partial(early_kernel, width, latent, top), (shape((tile_le...  1.33 us
    concatenate x1, other arithmetic, on_ring(): own = jnp.concatenate([pages, index_keys[0]], axis=0)  0.98 us
  transfers between devices with their start and end apart: 8, of which 6 were waited for; matrix products, arithmetic and copies ran while one was open for 0% of the time, Pallas kernels for 9%

profile of v5, /device:TPU:0, one launch (start us, length us, event | category | flops | bytes accessed | tf_op | source)
XLA Modules:
  0.0 26.3 jit_solution(5208875552672852070)
XLA Ops:
  0.6 0.0 copy-start.4
  0.6 0.0 copy-start.3
  0.7 0.0 copy-start.1
  0.7 1.0 %pad_maximum_fusion.own = bf16[704,128]{1,0:T(8,128)(2,1)S(1)} fusion(bf16[128,128]{1,0:T(8,128)(2,1)} %bitcast.23, bf16[576,128]{1,0:T(8,128)(2,1)} %bitcast.22), kind=kLoop, calls=%fused_computation | loop fusion | flops 360448 | bytes 360448 | tf_op jit(solution)/shard_map/concatenate | solution.py:245
  1.6 4.1 %collective-permute-start = (bf16[704,128]{1,0:T(8,128)(2,1)S(1)}, bf16[704,128]{1,0:T(8,128)(2,1)S(1)}, u32[]{:S(2)}, u32[]{:S(2)}) collective-permute-start(bf16[704,128]{1,0:T(8,128)(2,1)S(1)} %pad_maximum_fusion.own), channel_id=1, source_target_pairs={{0,8},{1,5},{2,10},{3,7},{8,12},{9,1},{10,14},{11,3},{12,4},{13,9}... | collective-permute-start | bytes 540680 | tf_op jit(solution)/shard_map/ppermute | solution.py:236
  5.7 0.0 collective-permute-start.3
  5.7 1.5 %collective-permute-start.2 = (bf16[704,128]{1,0:T(8,128)(2,1)S(1)}, bf16[704,128]{1,0:T(8,128)(2,1)S(1)}, u32[]{:S(2)}, u32[]{:S(2)}) collective-permute-start(bf16[704,128]{1,0:T(8,128)(2,1)S(1)} %pad_maximum_fusion.own), channel_id=1, source_target_pairs={{0,2},{2,0},{4,6},{6,4},{8,10},{10,8},{12,14},{14,12},{1,3},{3,1},... | collective-permute-start | bytes 540680 | tf_op jit(solution)/shard_map/ppermute | solution.py:239
  7.2 0.5 %collective-permute-start.1 = (s32[1,4]{1,0:T(1,128)}, s32[1,4]{1,0:T(1,128)S(1)}, u32[]{:S(2)}, u32[]{:S(2)}) collective-permute-start(s32[1,4]{1,0:T(1,128)} %bitcast.20), channel_id=1, source_target_pairs={{0,2},{2,0},{4,6},{6,4},{8,10},{10,8},{12,14},{14,12},{1,3},{3,1},... | collective-permute-start | bytes 56 | tf_op jit(solution)/shard_map/ppermute | solution.py:239
  7.8 0.0 copy-start
  7.8 1.3 %copy-done = bf16[1,8,128,576]{2,3,1,0:T(8,128)(2,1)S(1)} copy-done((bf16[1,8,128,576]{2,3,1,0:T(8,128)(2,1)S(1)}, bf16[1,8,128,576]{2,3,1,0:T(8,128)(2,1)}, u32[]{:S(2)}) %copy-start) | copy-done | bytes 1179672
  9.0 0.7 %copy-done.2 = bf16[1,8,576]{2,1,0:T(8,128)(2,1)S(1)} copy-done((bf16[1,8,576]{2,1,0:T(8,128)(2,1)S(1)}, bf16[1,8,576]{2,1,0:T(8,128)(2,1)}, u32[]{:S(2)}) %copy-start.2) | copy-done | bytes 9240
  9.7 0.6 %shard_map.95 = (bf16[1024,576]{1,0:T(8,128)(2,1)S(1)}, f32[1024,128]{1,0:T(8,128)S(1)}, bf16[128,512]{1,0:T(8,128)(2,1)S(1)}) custom-call(bf16[8,576,128]{2,1,0:T(8,128)(2,1)S(1)} %bitcast.14, bf16[8,576]{1,0:T(8,128)(2,1)S(1)} %bitcast.17), custom_call_target="tpu_custom_call" | custom-call | bytes 2359296 | tf_op jit(solution)/shard_map/pallas_call | solution.py:252
  10.3 1.6 %collective-permute-done.1.list_ref = s32[1,4]{1,0:T(1,128)S(1)} collective-permute-done((s32[1,4]{1,0:T(1,128)}, s32[1,4]{1,0:T(1,128)S(1)}, u32[]{:S(2)}, u32[]{:S(2)}) %collective-permute-start.1) | collective-permute-done | bytes 48 | tf_op jit(solution)/shard_map/ppermute | solution.py:239
  11.9 0.1 collective-permute-done.line_ref.below
  12.0 2.2 %collective-permute-start.4 = (bf16[704,128]{1,0:T(8,128)(2,1)S(1)}, bf16[704,128]{1,0:T(8,128)(2,1)S(1)}, u32[]{:S(2)}, u32[]{:S(2)}) collective-permute-start(bf16[704,128]{1,0:T(8,128)(2,1)S(1)} %collective-permute-done.line_ref.below), channel_id=1, source_target_pairs={{0,8},{1,5},{2,10},{3,7},{8,12},{9,1},{10,14},{11,3},{12,4},{13,9}... | collective-permute-start | bytes 540680 | tf_op jit(solution)/shard_map/ppermute | solution.py:236
  14.2 0.0 collective-permute-done.2.near
  14.2 0.2 shard_map.96
  14.4 1.6 %collective-permute-start.5 = (bf16[416,128]{1,0:T(8,128)(2,1)S(1)}, bf16[416,128]{1,0:T(8,128)(2,1)S(1)}, u32[]{:S(2)}, u32[]{:S(2)}) collective-permute-start(bf16[416,128]{1,0:T(8,128)(2,1)S(1)} %shard_map.96), channel_id=1, source_target_pairs={{0,2},{2,0},{4,6},{6,4},{8,10},{10,8},{12,14},{14,12},{1,3},{3,1},... | collective-permute-start | bytes 319496 | tf_op jit(solution)/shard_map/ppermute | solution.py:239
  15.9 0.3 %collective-permute-done.3.line_ref.above = bf16[704,128]{1,0:T(8,128)(2,1)S(1)} collective-permute-done((bf16[704,128]{1,0:T(8,128)(2,1)S(1)}, bf16[704,128]{1,0:T(8,128)(2,1)S(1)}, u32[]{:S(2)}, u32[]{:S(2)}) %collective-permute-start.3) | collective-permute-done | bytes 180256 | tf_op jit(solution)/shard_map/ppermute | solution.py:236
  16.2 0.2 shard_map.97
  16.4 1.5 %collective-permute-start.6 = (bf16[416,128]{1,0:T(8,128)(2,1)S(1)}, bf16[416,128]{1,0:T(8,128)(2,1)S(1)}, u32[]{:S(2)}, u32[]{:S(2)}) collective-permute-start(bf16[416,128]{1,0:T(8,128)(2,1)S(1)} %shard_map.97), channel_id=1, source_target_pairs={{0,2},{2,0},{4,6},{6,4},{8,10},{10,8},{12,14},{14,12},{1,3},{3,1},... | collective-permute-start | bytes 319496 | tf_op jit(solution)/shard_map/ppermute | solution.py:239
  17.9 1.2 %collective-permute-done.4.far.line_ref = bf16[704,128]{1,0:T(8,128)(2,1)S(1)} collective-permute-done((bf16[704,128]{1,0:T(8,128)(2,1)S(1)}, bf16[704,128]{1,0:T(8,128)(2,1)S(1)}, u32[]{:S(2)}, u32[]{:S(2)}) %collective-permute-start.4) | collective-permute-done | bytes 180256 | tf_op jit(solution)/shard_map/ppermute | solution.py:236
  19.1 0.1 shard_map.99
  19.2 1.6 %collective-permute-start.7 = (bf16[416,128]{1,0:T(8,128)(2,1)S(1)}, bf16[416,128]{1,0:T(8,128)(2,1)S(1)}, u32[]{:S(2)}, u32[]{:S(2)}) collective-permute-start(bf16[416,128]{1,0:T(8,128)(2,1)S(1)} %shard_map.99), channel_id=1, source_target_pairs={{0,2},{2,0},{4,6},{6,4},{8,10},{10,8},{12,14},{14,12},{1,3},{3,1},... | collective-permute-start | bytes 319496 | tf_op jit(solution)/shard_map/ppermute | solution.py:239
  21.4 0.0 collective-permute-done.5.side_below
  21.4 1.1 %collective-permute-done.6.side_above = bf16[416,128]{1,0:T(8,128)(2,1)S(1)} collective-permute-done((bf16[416,128]{1,0:T(8,128)(2,1)S(1)}, bf16[416,128]{1,0:T(8,128)(2,1)S(1)}, u32[]{:S(2)}, u32[]{:S(2)}) %collective-permute-start.6) | collective-permute-done | bytes 106528 | tf_op jit(solution)/shard_map/ppermute | solution.py:239
  22.5 0.0 copy-done.4
  22.5 0.0 copy-done.3
  22.5 0.0 copy-done.1
  22.5 1.3 %shard_map.98 = (f32[8,16]{1,0:T(8,128)S(1)}, bf16[576,256]{1,0:T(8,128)(2,1)S(1)}, bf16[256,512]{1,0:T(8,128)(2,1)S(1)}, s32[8,256]{1,0:T(8,128)S(1)}) custom-call(s32[4]{0:T(128)S(1)} %bitcast.21, s32[1]{0:T(128)S(6)} %copy.10.length_ref, bf16[8,64]{1,0:T(8,128)(2,1)S(1)} %bitcast.18, bf16[512,128]{1,0:T(8,128)(2,1)S(1)} %bitcast.15, ...), custom_call_target="tpu_custom_call" | custom-call | bytes 2359296 | tf_op jit(solution)/shard_map/pallas_call | solution.py:268
  23.8 0.2 collective-permute-done.7.side_far
  24.0 2.4 %shard_map.100 = (bf16[1024,512]{1,0:T(8,128)(2,1)}, f32[8,16]{1,0:T(8,128)}) custom-call(bf16[1024,576]{1,0:T(8,128)(2,1)S(1)} %get-tuple-element.19.q_ref, f32[1024,128]{1,0:T(8,128)S(1)} %get-tuple-element.20.fresh_ref, bf16[128,512]{1,0:T(8,128)(2,1)S(1)} %get-tuple-element.21.new_rows, bf16[576,256]{1,0:T(8,128)(2,1)S(1)} %get-tuple-element.26.early_turned, ...), custom_call_target="tpu_custom_call" | custom-call | tf_op jit(solution)/shard_map/pallas_call | solution.py:277
  (1 shorter events, 0.0 us)
Async XLA Ops:
  0.6 21.9 %copy-start.4 = (s32[1,1,4]{2,1,0:T(1,128)S(1)}, s32[1,1,4]{2,1,0:T(1,128)}, u32[]{:S(2)}) copy-start(s32[1,1,4]{2,1,0:T(1,128)} %param.14) | copy-start | bytes 52
  0.6 21.8 %copy-start.3 = (bf16[1,8,64]{2,1,0:T(8,128)(2,1)S(1)}, bf16[1,8,64]{2,1,0:T(8,128)(2,1)}, u32[]{:S(2)}) copy-start(bf16[1,8,64]{2,1,0:T(8,128)(2,1)} %param.12) | copy-start | bytes 3076
  0.7 21.8 %copy-start.1 = (bf16[1,8,64,128]{3,2,1,0:T(8,128)(2,1)S(1)}, bf16[1,8,64,128]{3,2,1,0:T(8,128)(2,1)}, u32[]{:S(2)}) copy-start(bf16[1,8,64,128]{3,2,1,0:T(8,128)(2,1)} %param.11) | copy-start | bytes 393220
  1.6 10.4 %collective-permute-start = (bf16[704,128]{1,0:T(8,128)(2,1)S(1)}, bf16[704,128]{1,0:T(8,128)(2,1)S(1)}, u32[]{:S(2)}, u32[]{:S(2)}) collective-permute-start(bf16[704,128]{1,0:T(8,128)(2,1)S(1)} %pad_maximum_fusion.own), channel_id=1, source_target_pairs={{0,8},{1,5},{2,10},{3,7},{8,12},{9,1},{10,14},{11,3},{12,4},{13,9}... | collective-permute-start | bytes 540680 | tf_op jit(solution)/shard_map/ppermute | solution.py:236
  5.7 10.5 %collective-permute-start.3 = (bf16[704,128]{1,0:T(8,128)(2,1)S(1)}, bf16[704,128]{1,0:T(8,128)(2,1)S(1)}, u32[]{:S(2)}, u32[]{:S(2)}) collective-permute-start(bf16[704,128]{1,0:T(8,128)(2,1)S(1)} %pad_maximum_fusion.own), channel_id=1, source_target_pairs={{0,4},{1,9},{2,6},{3,11},{8,0},{9,13},{10,2},{11,15},{12,8},{13,5}... | collective-permute-start | bytes 540680 | tf_op jit(solution)/shard_map/ppermute | solution.py:236
  5.7 8.5 %collective-permute-start.2 = (bf16[704,128]{1,0:T(8,128)(2,1)S(1)}, bf16[704,128]{1,0:T(8,128)(2,1)S(1)}, u32[]{:S(2)}, u32[]{:S(2)}) collective-permute-start(bf16[704,128]{1,0:T(8,128)(2,1)S(1)} %pad_maximum_fusion.own), channel_id=1, source_target_pairs={{0,2},{2,0},{4,6},{6,4},{8,10},{10,8},{12,14},{14,12},{1,3},{3,1},... | collective-permute-start | bytes 540680 | tf_op jit(solution)/shard_map/ppermute | solution.py:239
  7.2 4.6 %collective-permute-start.1 = (s32[1,4]{1,0:T(1,128)}, s32[1,4]{1,0:T(1,128)S(1)}, u32[]{:S(2)}, u32[]{:S(2)}) collective-permute-start(s32[1,4]{1,0:T(1,128)} %bitcast.20), channel_id=1, source_target_pairs={{0,2},{2,0},{4,6},{6,4},{8,10},{10,8},{12,14},{14,12},{1,3},{3,1},... | collective-permute-start | bytes 56 | tf_op jit(solution)/shard_map/ppermute | solution.py:239
  7.8 1.3 %copy-start = (bf16[1,8,128,576]{2,3,1,0:T(8,128)(2,1)S(1)}, bf16[1,8,128,576]{2,3,1,0:T(8,128)(2,1)}, u32[]{:S(2)}) copy-start(bf16[1,8,128,576]{2,3,1,0:T(8,128)(2,1)} %param.8) | copy-start | bytes 3538948
  9.0 0.7 %copy-start.2 = (bf16[1,8,576]{2,1,0:T(8,128)(2,1)S(1)}, bf16[1,8,576]{2,1,0:T(8,128)(2,1)}, u32[]{:S(2)}) copy-start(bf16[1,8,576]{2,1,0:T(8,128)(2,1)} %param.9) | copy-start | bytes 27652
  12.0 7.0 %collective-permute-start.4 = (bf16[704,128]{1,0:T(8,128)(2,1)S(1)}, bf16[704,128]{1,0:T(8,128)(2,1)S(1)}, u32[]{:S(2)}, u32[]{:S(2)}) collective-permute-start(bf16[704,128]{1,0:T(8,128)(2,1)S(1)} %collective-permute-done.line_ref.below), channel_id=1, source_target_pairs={{0,8},{1,5},{2,10},{3,7},{8,12},{9,1},{10,14},{11,3},{12,4},{13,9}... | collective-permute-start | bytes 540680 | tf_op jit(solution)/shard_map/ppermute | solution.py:236
  14.4 7.0 %collective-permute-start.5 = (bf16[416,128]{1,0:T(8,128)(2,1)S(1)}, bf16[416,128]{1,0:T(8,128)(2,1)S(1)}, u32[]{:S(2)}, u32[]{:S(2)}) collective-permute-start(bf16[416,128]{1,0:T(8,128)(2,1)S(1)} %shard_map.96), channel_id=1, source_target_pairs={{0,2},{2,0},{4,6},{6,4},{8,10},{10,8},{12,14},{14,12},{1,3},{3,1},... | collective-permute-start | bytes 319496 | tf_op jit(solution)/shard_map/ppermute | solution.py:239
  16.4 6.1 %collective-permute-start.6 = (bf16[416,128]{1,0:T(8,128)(2,1)S(1)}, bf16[416,128]{1,0:T(8,128)(2,1)S(1)}, u32[]{:S(2)}, u32[]{:S(2)}) collective-permute-start(bf16[416,128]{1,0:T(8,128)(2,1)S(1)} %shard_map.97), channel_id=1, source_target_pairs={{0,2},{2,0},{4,6},{6,4},{8,10},{10,8},{12,14},{14,12},{1,3},{3,1},... | collective-permute-start | bytes 319496 | tf_op jit(solution)/shard_map/ppermute | solution.py:239
  19.2 4.8 %collective-permute-start.7 = (bf16[416,128]{1,0:T(8,128)(2,1)S(1)}, bf16[416,128]{1,0:T(8,128)(2,1)S(1)}, u32[]{:S(2)}, u32[]{:S(2)}) collective-permute-start(bf16[416,128]{1,0:T(8,128)(2,1)S(1)} %shard_map.99), channel_id=1, source_target_pairs={{0,2},{2,0},{4,6},{6,4},{8,10},{10,8},{12,14},{14,12},{1,3},{3,1},... | collective-permute-start | bytes 319496 | tf_op jit(solution)/shard_map/ppermute | solution.py:239

commit v6 on v5

--- a/solution.py
+++ b/solution.py
@@ -240,7 +240,7 @@
 
     def pick(step, line):
         body = functools.partial(pick_kernel, step, width, top)
-        return call(body, shape((low + rows, rows), BF16), [VMEM] * 2, moved=2 * 10**6)(asked, line)
+        return call(body, shape((low + rows, rows), BF16), [VMEM] * 2, moved=10**7)(asked, line)
 
     own = jnp.concatenate([pages, index_keys[0]], axis=0)
     below = shift(own, 1)
@@ -261,8 +261,8 @@
     far = shift(below, 1)
     asked, near = lax.optimization_barrier((asked, near))
     side_below = swap(pick(0, below))
+    side_far = swap(pick(2, far))
     side_above = swap(pick(1, above))
-    side_far = swap(pick(2, far))
     sums = pltpu.VMEM((2 * count, index_rows.shape[0]), F32)
     columns = chosen.shape[0] * BLK
     score, turned, key_rows, marks = call(

time: 26.6 us -> 26.6 us (level)
  no operation moved by 1% of the time
where the time goes in v6:
time: 26.6 us; the launch traced here: 26.3 us
  starting transfers between devices  12.9 us (48%)
  Pallas kernels  4.68 us (18%)
  waiting for transfers between devices  4.38 us (16%)
  local copies, waits for them, and re-layouts  1.99 us (7%)
  between operations  1.36 us (5%)
  other arithmetic  0.98 us (4%)
    ppermute x5, starting transfers between devices, swap(): return lax.ppermute(x, 'ctx', [(i, i ^ 1) for i in range(count)])  6.65 us
    ppermute x3, starting transfers between devices, shift(): return lax.ppermute(x, ('ctx', 'batch'), pairs)  6.29 us
    ppermute x5, waiting for transfers between devices, swap(): return lax.ppermute(x, 'ctx', [(i, i ^ 1) for i in range(count)])  2.79 us
    pallas_call x1, Pallas kernels, on_ring(): call(functools.partial(attend_kernel, width, latent, top, chunk), (shape(...  2.35 us
    unnamed x10, local copies, waits for them, and re-layouts  1.99 us
    ppermute x3, waiting for transfers between devices, shift(): return lax.ppermute(x, ('ctx', 'batch'), pairs)  1.59 us
    pallas_call x1, Pallas kernels, on_ring(): call(functools.partial(early_kernel, width, latent, top), (shape((tile_le...  1.33 us
    concatenate x1, other arithmetic, on_ring(): own = jnp.concatenate([pages, index_keys[0]], axis=0)  0.98 us
  transfers between devices with their start and end apart: 8, of which 6 were waited for; matrix products, arithmetic and copies ran while one was open for 0% of the time, Pallas kernels for 9%

profile of v6, /device:TPU:0, one launch (start us, length us, event | category | flops | bytes accessed | tf_op | source)
XLA Modules:
  0.0 26.3 jit_solution(5208875552672852070)
XLA Ops:
  0.6 0.0 copy-start.4
  0.6 0.0 copy-start.3
  0.7 0.0 copy-start.1
  0.7 1.0 %pad_maximum_fusion.own = bf16[704,128]{1,0:T(8,128)(2,1)S(1)} fusion(bf16[128,128]{1,0:T(8,128)(2,1)} %bitcast.23, bf16[576,128]{1,0:T(8,128)(2,1)} %bitcast.22), kind=kLoop, calls=%fused_computation | loop fusion | flops 360448 | bytes 360448 | tf_op jit(solution)/shard_map/concatenate | solution.py:245
  1.6 4.1 %collective-permute-start = (bf16[704,128]{1,0:T(8,128)(2,1)S(1)}, bf16[704,128]{1,0:T(8,128)(2,1)S(1)}, u32[]{:S(2)}, u32[]{:S(2)}) collective-permute-start(bf16[704,128]{1,0:T(8,128)(2,1)S(1)} %pad_maximum_fusion.own), channel_id=1, source_target_pairs={{0,8},{1,5},{2,10},{3,7},{8,12},{9,1},{10,14},{11,3},{12,4},{13,9}... | collective-permute-start | bytes 540680 | tf_op jit(solution)/shard_map/ppermute | solution.py:236
  5.7 0.0 collective-permute-start.3
  5.7 1.5 %collective-permute-start.2 = (bf16[704,128]{1,0:T(8,128)(2,1)S(1)}, bf16[704,128]{1,0:T(8,128)(2,1)S(1)}, u32[]{:S(2)}, u32[]{:S(2)}) collective-permute-start(bf16[704,128]{1,0:T(8,128)(2,1)S(1)} %pad_maximum_fusion.own), channel_id=1, source_target_pairs={{0,2},{2,0},{4,6},{6,4},{8,10},{10,8},{12,14},{14,12},{1,3},{3,1},... | collective-permute-start | bytes 540680 | tf_op jit(solution)/shard_map/ppermute | solution.py:239
  7.2 0.5 %collective-permute-start.1 = (s32[1,4]{1,0:T(1,128)}, s32[1,4]{1,0:T(1,128)S(1)}, u32[]{:S(2)}, u32[]{:S(2)}) collective-permute-start(s32[1,4]{1,0:T(1,128)} %bitcast.20), channel_id=1, source_target_pairs={{0,2},{2,0},{4,6},{6,4},{8,10},{10,8},{12,14},{14,12},{1,3},{3,1},... | collective-permute-start | bytes 56 | tf_op jit(solution)/shard_map/ppermute | solution.py:239
  7.8 0.0 copy-start
  7.8 1.3 %copy-done = bf16[1,8,128,576]{2,3,1,0:T(8,128)(2,1)S(1)} copy-done((bf16[1,8,128,576]{2,3,1,0:T(8,128)(2,1)S(1)}, bf16[1,8,128,576]{2,3,1,0:T(8,128)(2,1)}, u32[]{:S(2)}) %copy-start) | copy-done | bytes 1179672
  9.0 0.7 %copy-done.2 = bf16[1,8,576]{2,1,0:T(8,128)(2,1)S(1)} copy-done((bf16[1,8,576]{2,1,0:T(8,128)(2,1)S(1)}, bf16[1,8,576]{2,1,0:T(8,128)(2,1)}, u32[]{:S(2)}) %copy-start.2) | copy-done | bytes 9240
  9.7 0.6 %shard_map.95 = (bf16[1024,576]{1,0:T(8,128)(2,1)S(1)}, f32[1024,128]{1,0:T(8,128)S(1)}, bf16[128,512]{1,0:T(8,128)(2,1)S(1)}) custom-call(bf16[8,576,128]{2,1,0:T(8,128)(2,1)S(1)} %bitcast.14, bf16[8,576]{1,0:T(8,128)(2,1)S(1)} %bitcast.17), custom_call_target="tpu_custom_call" | custom-call | bytes 2359296 | tf_op jit(solution)/shard_map/pallas_call | solution.py:252
  10.3 1.6 %collective-permute-done.1.list_ref = s32[1,4]{1,0:T(1,128)S(1)} collective-permute-done((s32[1,4]{1,0:T(1,128)}, s32[1,4]{1,0:T(1,128)S(1)}, u32[]{:S(2)}, u32[]{:S(2)}) %collective-permute-start.1) | collective-permute-done | bytes 48 | tf_op jit(solution)/shard_map/ppermute | solution.py:239
  11.9 0.1 collective-permute-done.line_ref.below
  12.0 2.2 %collective-permute-start.4 = (bf16[704,128]{1,0:T(8,128)(2,1)S(1)}, bf16[704,128]{1,0:T(8,128)(2,1)S(1)}, u32[]{:S(2)}, u32[]{:S(2)}) collective-permute-start(bf16[704,128]{1,0:T(8,128)(2,1)S(1)} %collective-permute-done.line_ref.below), channel_id=1, source_target_pairs={{0,8},{1,5},{2,10},{3,7},{8,12},{9,1},{10,14},{11,3},{12,4},{13,9}... | collective-permute-start | bytes 540680 | tf_op jit(solution)/shard_map/ppermute | solution.py:236
  14.2 0.0 collective-permute-done.2.near
  14.2 0.2 shard_map.96
  14.4 1.6 %collective-permute-start.5 = (bf16[416,128]{1,0:T(8,128)(2,1)S(1)}, bf16[416,128]{1,0:T(8,128)(2,1)S(1)}, u32[]{:S(2)}, u32[]{:S(2)}) collective-permute-start(bf16[416,128]{1,0:T(8,128)(2,1)S(1)} %shard_map.96), channel_id=1, source_target_pairs={{0,2},{2,0},{4,6},{6,4},{8,10},{10,8},{12,14},{14,12},{1,3},{3,1},... | collective-permute-start | bytes 319496 | tf_op jit(solution)/shard_map/ppermute | solution.py:239
  15.9 0.3 %collective-permute-done.3.line_ref.above = bf16[704,128]{1,0:T(8,128)(2,1)S(1)} collective-permute-done((bf16[704,128]{1,0:T(8,128)(2,1)S(1)}, bf16[704,128]{1,0:T(8,128)(2,1)S(1)}, u32[]{:S(2)}, u32[]{:S(2)}) %collective-permute-start.3) | collective-permute-done | bytes 180256 | tf_op jit(solution)/shard_map/ppermute | solution.py:236
  16.2 0.2 shard_map.97
  16.4 1.5 %collective-permute-start.6 = (bf16[416,128]{1,0:T(8,128)(2,1)S(1)}, bf16[416,128]{1,0:T(8,128)(2,1)S(1)}, u32[]{:S(2)}, u32[]{:S(2)}) collective-permute-start(bf16[416,128]{1,0:T(8,128)(2,1)S(1)} %shard_map.97), channel_id=1, source_target_pairs={{0,2},{2,0},{4,6},{6,4},{8,10},{10,8},{12,14},{14,12},{1,3},{3,1},... | collective-permute-start | bytes 319496 | tf_op jit(solution)/shard_map/ppermute | solution.py:239
  17.9 1.2 %collective-permute-done.4.far.line_ref = bf16[704,128]{1,0:T(8,128)(2,1)S(1)} collective-permute-done((bf16[704,128]{1,0:T(8,128)(2,1)S(1)}, bf16[704,128]{1,0:T(8,128)(2,1)S(1)}, u32[]{:S(2)}, u32[]{:S(2)}) %collective-permute-start.4) | collective-permute-done | bytes 180256 | tf_op jit(solution)/shard_map/ppermute | solution.py:236
  19.1 0.1 shard_map.99
  19.2 1.6 %collective-permute-start.7 = (bf16[416,128]{1,0:T(8,128)(2,1)S(1)}, bf16[416,128]{1,0:T(8,128)(2,1)S(1)}, u32[]{:S(2)}, u32[]{:S(2)}) collective-permute-start(bf16[416,128]{1,0:T(8,128)(2,1)S(1)} %shard_map.99), channel_id=1, source_target_pairs={{0,2},{2,0},{4,6},{6,4},{8,10},{10,8},{12,14},{14,12},{1,3},{3,1},... | collective-permute-start | bytes 319496 | tf_op jit(solution)/shard_map/ppermute | solution.py:239
  21.4 0.0 collective-permute-done.5.side_below
  21.4 1.1 %collective-permute-done.6.side_above = bf16[416,128]{1,0:T(8,128)(2,1)S(1)} collective-permute-done((bf16[416,128]{1,0:T(8,128)(2,1)S(1)}, bf16[416,128]{1,0:T(8,128)(2,1)S(1)}, u32[]{:S(2)}, u32[]{:S(2)}) %collective-permute-start.6) | collective-permute-done | bytes 106528 | tf_op jit(solution)/shard_map/ppermute | solution.py:239
  22.5 0.0 copy-done.4
  22.5 0.0 copy-done.3
  22.5 0.0 copy-done.1
  22.5 1.3 %shard_map.98 = (f32[8,16]{1,0:T(8,128)S(1)}, bf16[576,256]{1,0:T(8,128)(2,1)S(1)}, bf16[256,512]{1,0:T(8,128)(2,1)S(1)}, s32[8,256]{1,0:T(8,128)S(1)}) custom-call(s32[4]{0:T(128)S(1)} %bitcast.21, s32[1]{0:T(128)S(6)} %copy.10.length_ref, bf16[8,64]{1,0:T(8,128)(2,1)S(1)} %bitcast.18, bf16[512,128]{1,0:T(8,128)(2,1)S(1)} %bitcast.15, ...), custom_call_target="tpu_custom_call" | custom-call | bytes 2359296 | tf_op jit(solution)/shard_map/pallas_call | solution.py:268
  23.8 0.2 collective-permute-done.7.side_far
  24.0 2.4 %shard_map.100 = (bf16[1024,512]{1,0:T(8,128)(2,1)}, f32[8,16]{1,0:T(8,128)}) custom-call(bf16[1024,576]{1,0:T(8,128)(2,1)S(1)} %get-tuple-element.19.q_ref, f32[1024,128]{1,0:T(8,128)S(1)} %get-tuple-element.20.fresh_ref, bf16[128,512]{1,0:T(8,128)(2,1)S(1)} %get-tuple-element.21.new_rows, bf16[576,256]{1,0:T(8,128)(2,1)S(1)} %get-tuple-element.26.early_turned, ...), custom_call_target="tpu_custom_call" | custom-call | tf_op jit(solution)/shard_map/pallas_call | solution.py:277
  (1 shorter events, 0.0 us)
Async XLA Ops:
  0.6 21.9 %copy-start.4 = (s32[1,1,4]{2,1,0:T(1,128)S(1)}, s32[1,1,4]{2,1,0:T(1,128)}, u32[]{:S(2)}) copy-start(s32[1,1,4]{2,1,0:T(1,128)} %param.14) | copy-start | bytes 52
  0.6 21.8 %copy-start.3 = (bf16[1,8,64]{2,1,0:T(8,128)(2,1)S(1)}, bf16[1,8,64]{2,1,0:T(8,128)(2,1)}, u32[]{:S(2)}) copy-start(bf16[1,8,64]{2,1,0:T(8,128)(2,1)} %param.12) | copy-start | bytes 3076
  0.7 21.8 %copy-start.1 = (bf16[1,8,64,128]{3,2,1,0:T(8,128)(2,1)S(1)}, bf16[1,8,64,128]{3,2,1,0:T(8,128)(2,1)}, u32[]{:S(2)}) copy-start(bf16[1,8,64,128]{3,2,1,0:T(8,128)(2,1)} %param.11) | copy-start | bytes 393220
  1.6 10.4 %collective-permute-start = (bf16[704,128]{1,0:T(8,128)(2,1)S(1)}, bf16[704,128]{1,0:T(8,128)(2,1)S(1)}, u32[]{:S(2)}, u32[]{:S(2)}) collective-permute-start(bf16[704,128]{1,0:T(8,128)(2,1)S(1)} %pad_maximum_fusion.own), channel_id=1, source_target_pairs={{0,8},{1,5},{2,10},{3,7},{8,12},{9,1},{10,14},{11,3},{12,4},{13,9}... | collective-permute-start | bytes 540680 | tf_op jit(solution)/shard_map/ppermute | solution.py:236
  5.7 10.5 %collective-permute-start.3 = (bf16[704,128]{1,0:T(8,128)(2,1)S(1)}, bf16[704,128]{1,0:T(8,128)(2,1)S(1)}, u32[]{:S(2)}, u32[]{:S(2)}) collective-permute-start(bf16[704,128]{1,0:T(8,128)(2,1)S(1)} %pad_maximum_fusion.own), channel_id=1, source_target_pairs={{0,4},{1,9},{2,6},{3,11},{8,0},{9,13},{10,2},{11,15},{12,8},{13,5}... | collective-permute-start | bytes 540680 | tf_op jit(solution)/shard_map/ppermute | solution.py:236
  5.7 8.5 %collective-permute-start.2 = (bf16[704,128]{1,0:T(8,128)(2,1)S(1)}, bf16[704,128]{1,0:T(8,128)(2,1)S(1)}, u32[]{:S(2)}, u32[]{:S(2)}) collective-permute-start(bf16[704,128]{1,0:T(8,128)(2,1)S(1)} %pad_maximum_fusion.own), channel_id=1, source_target_pairs={{0,2},{2,0},{4,6},{6,4},{8,10},{10,8},{12,14},{14,12},{1,3},{3,1},... | collective-permute-start | bytes 540680 | tf_op jit(solution)/shard_map/ppermute | solution.py:239
  7.2 4.6 %collective-permute-start.1 = (s32[1,4]{1,0:T(1,128)}, s32[1,4]{1,0:T(1,128)S(1)}, u32[]{:S(2)}, u32[]{:S(2)}) collective-permute-start(s32[1,4]{1,0:T(1,128)} %bitcast.20), channel_id=1, source_target_pairs={{0,2},{2,0},{4,6},{6,4},{8,10},{10,8},{12,14},{14,12},{1,3},{3,1},... | collective-permute-start | bytes 56 | tf_op jit(solution)/shard_map/ppermute | solution.py:239
  7.8 1.3 %copy-start = (bf16[1,8,128,576]{2,3,1,0:T(8,128)(2,1)S(1)}, bf16[1,8,128,576]{2,3,1,0:T(8,128)(2,1)}, u32[]{:S(2)}) copy-start(bf16[1,8,128,576]{2,3,1,0:T(8,128)(2,1)} %param.8) | copy-start | bytes 3538948
  9.0 0.7 %copy-start.2 = (bf16[1,8,576]{2,1,0:T(8,128)(2,1)S(1)}, bf16[1,8,576]{2,1,0:T(8,128)(2,1)}, u32[]{:S(2)}) copy-start(bf16[1,8,576]{2,1,0:T(8,128)(2,1)} %param.9) | copy-start | bytes 27652
  12.0 7.0 %collective-permute-start.4 = (bf16[704,128]{1,0:T(8,128)(2,1)S(1)}, bf16[704,128]{1,0:T(8,128)(2,1)S(1)}, u32[]{:S(2)}, u32[]{:S(2)}) collective-permute-start(bf16[704,128]{1,0:T(8,128)(2,1)S(1)} %collective-permute-done.line_ref.below), channel_id=1, source_target_pairs={{0,8},{1,5},{2,10},{3,7},{8,12},{9,1},{10,14},{11,3},{12,4},{13,9}... | collective-permute-start | bytes 540680 | tf_op jit(solution)/shard_map/ppermute | solution.py:236
  14.4 7.0 %collective-permute-start.5 = (bf16[416,128]{1,0:T(8,128)(2,1)S(1)}, bf16[416,128]{1,0:T(8,128)(2,1)S(1)}, u32[]{:S(2)}, u32[]{:S(2)}) collective-permute-start(bf16[416,128]{1,0:T(8,128)(2,1)S(1)} %shard_map.96), channel_id=1, source_target_pairs={{0,2},{2,0},{4,6},{6,4},{8,10},{10,8},{12,14},{14,12},{1,3},{3,1},... | collective-permute-start | bytes 319496 | tf_op jit(solution)/shard_map/ppermute | solution.py:239
  16.4 6.1 %collective-permute-start.6 = (bf16[416,128]{1,0:T(8,128)(2,1)S(1)}, bf16[416,128]{1,0:T(8,128)(2,1)S(1)}, u32[]{:S(2)}, u32[]{:S(2)}) collective-permute-start(bf16[416,128]{1,0:T(8,128)(2,1)S(1)} %shard_map.97), channel_id=1, source_target_pairs={{0,2},{2,0},{4,6},{6,4},{8,10},{10,8},{12,14},{14,12},{1,3},{3,1},... | collective-permute-start | bytes 319496 | tf_op jit(solution)/shard_map/ppermute | solution.py:239
  19.2 4.8 %collective-permute-start.7 = (bf16[416,128]{1,0:T(8,128)(2,1)S(1)}, bf16[416,128]{1,0:T(8,128)(2,1)S(1)}, u32[]{:S(2)}, u32[]{:S(2)}) collective-permute-start(bf16[416,128]{1,0:T(8,128)(2,1)S(1)} %shard_map.99), channel_id=1, source_target_pairs={{0,2},{2,0},{4,6},{6,4},{8,10},{10,8},{12,14},{14,12},{1,3},{3,1},... | collective-permute-start | bytes 319496 | tf_op jit(solution)/shard_map/ppermute | solution.py:239

commit v7 on v6

--- a/solution.py
+++ b/solution.py
@@ -43,6 +43,7 @@
     low = width - top
     rows = 2 * BLK
     lane = lax.broadcasted_iota(jnp.int32, (1, rows), 1)
+    keep = jnp.logical_xor(lane < BLK, upper)
     first = line_ref[0:low, :].astype(F32)
     second = line_ref[top:width, :].astype(F32)
     first = jnp.where(upper, turn(first), first)
@@ -90,20 +91,20 @@
 
 def early_kernel(
     width, latent, top, list_ref, length_ref, weight_ref, query_ref,
-    own, near, below, above, far, side_below, side_above,
+    own, near, below, above, far, side_below,
     score_ref, turned_ref, rows_ref, marks_ref, slots, sums,
 ):
     me = lax.axis_index("ctx")
     behind, ahead, opposite = ring_steps(me)
-    last = jnp.bitwise_xor(me, opposite + 1)
+    missing = (jnp.bitwise_xor(me, ahead + 1), jnp.bitwise_xor(me, opposite + 1))
     low = width - top
     rows = 2 * BLK
     lane = lax.broadcasted_iota(jnp.int32, (1, rows), 1)
     for slot, ref in ((0, own), (1, near), (behind, below), (ahead, above), (opposite, far)):
         slots[slot] = ref[0:width, :]
-    for slot, ref in ((behind + 1, side_below), (ahead + 1, side_above)):
-        slots[slot, 0:top, :] = ref[0:top, :]
-        slots[slot, top:width, :] = turn(ref[0:low, :].astype(F32)).astype(BF16)
+    slots[behind + 1, 0:top, :] = side_below[0:top, :]
+    slots[behind + 1, top:width, :] = turn(side_below[0:low, :].astype(F32)).astype(BF16)
+    slots[ahead + 1] = jnp.zeros((width, rows), BF16)
     slots[opposite + 1] = jnp.zeros((width, rows), BF16)
     column = lax.broadcasted_iota(jnp.int32, (1, list_ref.shape[0] * BLK), 1)
     limit = jnp.zeros_like(column)
@@ -120,17 +121,19 @@
             block = slots[slot].astype(F32)
             halves.append(jnp.where(high == j - 2 * pair, block, turn(block)))
             limit = jnp.where(column // BLK == j, length - page * BLK + j * BLK, limit)
-            late = jnp.where((column // BLK == j) & (holder == last), 1, late)
+            for number, absent in enumerate(missing):
+                late = jnp.where((column // BLK == j) & (holder == absent), number + 1, late)
         block = jnp.where(lane < BLK, halves[0], halves[1]).astype(BF16)
         place = slice(pair * rows, (pair + 1) * rows)
         turned_ref[:, place] = block
         rows_ref[place, :] = block[0:latent, :].T
     marks_ref[0:1, :] = limit
     marks_ref[1:2, :] = late
-    marks_ref[2:3, :] = jnp.full_like(column, length - last * rows)
+    for number, absent in enumerate(missing):
+        marks_ref[number + 2 : number + 3, :] = jnp.full_like(column, length - absent * rows)
+        for half in range(2):
+            sums[pl.ds(2 * absent + half, 1), :] = jnp.zeros((1, sums.shape[1]), F32)
     query = query_ref[...]
-    sums[pl.ds(2 * last, 1), :] = jnp.zeros((1, sums.shape[1]), F32)
-    sums[pl.ds(2 * last + 1, 1), :] = jnp.zeros((1, sums.shape[1]), F32)
     for ref, start, step in (
         (own, width, 0),
         (near, width, 1),
@@ -138,7 +141,6 @@
         (above, width, ahead),
         (far, width, opposite),
         (side_below, low, behind + 1),
-        (side_above, low, ahead + 1),
     ):
         holder = jnp.bitwise_xor(me, step)
         page_sums(ref[start : start + rows, :], query, length - holder * rows, holder, sums)
@@ -146,33 +148,39 @@
 
 
 def attend_kernel(
-    width, latent, top, chunk, q_ref, fresh_ref, new_rows, early_turned, early_rows, marks_ref, early_score, side_far,
-    weight_ref, query_ref,
+    width, latent, top, chunk, q_ref, fresh_ref, new_rows, early_turned, early_rows, marks_ref, early_score, side_above, side_far, weight_ref, query_ref,
     out_hbm, score_hbm, turned, key_rows, sums, out_ref, score_ref, sems,
 ):
-    last = jnp.bitwise_xor(lax.axis_index("ctx"), 7)
+    me = lax.axis_index("ctx")
     low = width - top
     rows = 2 * BLK
     sums[...] = jnp.zeros_like(sums)
-    page_sums(side_far[low : low + rows, :], query_ref[...], marks_ref[2:3, 0:rows], last, sums)
+    arrived = ((side_above, ring_steps(me)[1] + 1), (side_far, ring_steps(me)[2] + 1))
+    for number, (ref, step) in enumerate(arrived):
+        room = marks_ref[number + 2 : number + 3, 0:rows]
+        page_sums(ref[low : low + rows, :], query_ref[...], room, jnp.bitwise_xor(me, step), sums)
     score_ref[...] = early_score[...] + weigh(weight_ref, sums)
     steps = q_ref.shape[0] // chunk
     copies = [pltpu.make_async_copy(score_ref, score_hbm, sems.at[steps])]
     copies[0].start()
     lane = lax.broadcasted_iota(jnp.int32, (1, rows), 1)
-    packed = side_far[0:low, :].astype(F32)
-    swapped = turn(packed)
-    first = jnp.concatenate([packed[0:top], swapped], axis=0)
-    second = jnp.concatenate([swapped[0:top], packed], axis=0)
-    both = jnp.where(lane < BLK, first, second).astype(BF16)
-    both_rows = both[0:latent, :].T
     limit = marks_ref[0:1, :]
     late = marks_ref[1:2, :]
-    for place in range(0, turned.shape[1], rows):
-        place = slice(place, place + rows)
-        turned[:, place] = jnp.where(late[:, place] == 1, both, early_turned[:, place])
-        down = jnp.broadcast_to(late[:, place].astype(F32), (rows, rows)).T[:, 0:1]
-        key_rows[place, :] = jnp.where(down > 0.5, both_rows, early_rows[place, :])
+    turned[...] = early_turned[...]
+    key_rows[...] = early_rows[...]
+    for number, (ref, _) in enumerate(arrived):
+        packed = ref[0:low, :].astype(F32)
+        swapped = turn(packed)
+        first = jnp.concatenate([packed[0:top], swapped], axis=0)
+        second = jnp.concatenate([swapped[0:top], packed], axis=0)
+        both = jnp.where(lane < BLK, first, second).astype(BF16)
+        both_rows = both[0:latent, :].T
+        for place in range(0, turned.shape[1], rows):
+            place = slice(place, place + rows)
+            here = late[:, place] == number + 1
+            turned[:, place] = jnp.where(here, both, turned[:, place])
+            down = jnp.broadcast_to(jnp.where(here, 1.0, 0.0), (rows, rows)).T[:, 0:1]
+            key_rows[place, :] = jnp.where(down > 0.5, both_rows, key_rows[place, :])
     factor = softmax_scale * math.log2(math.e)
     column = lax.broadcasted_iota(jnp.int32, (1, turned.shape[1]), 1)
     for step in range(steps):
@@ -196,18 +204,20 @@
 
 VMEM = pl.BlockSpec(memory_space=pltpu.VMEM)
 SMEM = pl.BlockSpec(memory_space=pltpu.SMEM)
+
+
 ANY = pl.BlockSpec(memory_space=pl.ANY)
 
 
-def call(body, shapes, in_specs, out_specs=VMEM, scratch=(), moved=0):
+def call(body, shapes, in_specs, out_specs=VMEM, scratch=(), flops=0, moved=0, vmem=32):
     return pl.pallas_call(
         body,
         out_shape=shapes,
         in_specs=in_specs,
         out_specs=out_specs,
         scratch_shapes=scratch,
-        cost_estimate=pl.CostEstimate(flops=0, bytes_accessed=moved, transcendentals=0),
-        compiler_params=pltpu.CompilerParams(vmem_limit_bytes=32 * 1024 * 1024),
+        cost_estimate=pl.CostEstimate(flops=flops, bytes_accessed=moved, transcendentals=0),
+        compiler_params=pltpu.CompilerParams(vmem_limit_bytes=vmem * 1024 * 1024),
     )
 
 
@@ -268,16 +278,16 @@
     score, turned, key_rows, marks = call(
         functools.partial(early_kernel, width, latent, top),
         (shape((tile_len, 2 * count), F32), shape((width, columns), BF16), shape((columns, latent), BF16), shape((8, columns), jnp.int32)),
-        [SMEM] * 2 + [VMEM] * 9,
+        [SMEM] * 2 + [VMEM] * 8,
         (VMEM,) * 4,
         [pltpu.VMEM((8, width, rows), BF16), sums],
         moved=4 * query_count * width,
-    )(chosen, context_len, index_weight[0], index_rows, own, near, below, above, far, side_below, side_above)
+    )(chosen, context_len, index_weight[0], index_rows, own, near, below, above, far, side_below)
     chunk = query_count // 2
     attended, block_score = call(
         functools.partial(attend_kernel, width, latent, top, chunk),
         (shape((query_count, latent), BF16), shape((tile_len, 2 * count), F32)),
-        [VMEM] * 10,
+        [VMEM] * 11,
         (ANY, ANY),
         [
             pltpu.VMEM((width, columns), BF16),
@@ -285,9 +295,9 @@
             sums,
             pltpu.VMEM((query_count, latent), BF16),
             pltpu.VMEM((tile_len, 2 * count), F32),
-            pltpu.SemaphoreType.DMA((3,)),
+            pltpu.SemaphoreType.DMA((2 + 1,)),
         ],
-    )(q_rows, fresh, new_rows, turned, key_rows, marks, score, side_far, index_weight[0], index_rows)
+    )(q_rows, fresh, new_rows, turned, key_rows, marks, score, side_above, side_far, index_weight[0], index_rows)
     return attended.reshape(1, tile_len, head_count, latent), block_score[None]
 
 

time: 26.6 us -> 26.7 us (level)
  transfers between devices with their start and end apart: 8 -> 8, of which waited for: 6 -> 5; matrix products, arithmetic and copies ran while one was open for 0% -> 0% of each run, Pallas kernels for 9% -> 8%
where the time goes in v7:
time: 26.7 us; the launch traced here: 26.4 us
  starting transfers between devices  12.9 us (48%)
  Pallas kernels  4.71 us (18%)
  waiting for transfers between devices  4.44 us (17%)
  local copies, waits for them, and re-layouts  1.99 us (7%)
  between operations  1.38 us (5%)
  other arithmetic  0.98 us (4%)
    ppermute x5, starting transfers between devices, swap(): return lax.ppermute(x, 'ctx', [(i, i ^ 1) for i in range(count)])  6.65 us
    ppermute x3, starting transfers between devices, shift(): return lax.ppermute(x, ('ctx', 'batch'), pairs)  6.29 us
    ppermute x5, waiting for transfers between devices, swap(): return lax.ppermute(x, 'ctx', [(i, i ^ 1) for i in range(count)])  2.85 us
    pallas_call x1, Pallas kernels, on_ring(): call(functools.partial(attend_kernel, width, latent, top, chunk), (shape(...  2.47 us
    unnamed x10, local copies, waits for them, and re-layouts  1.99 us
    ppermute x3, waiting for transfers between devices, shift(): return lax.ppermute(x, ('ctx', 'batch'), pairs)  1.59 us
    pallas_call x1, Pallas kernels, on_ring(): call(functools.partial(early_kernel, width, latent, top), (shape((tile_le...  1.26 us
    concatenate x1, other arithmetic, on_ring(): own = jnp.concatenate([pages, index_keys[0]], axis=0)  0.98 us
  transfers between devices with their start and end apart: 8, of which 5 were waited for; matrix products, arithmetic and copies ran while one was open for 0% of the time, Pallas kernels for 8%

profile of v7, /device:TPU:0, one launch (start us, length us, event | category | flops | bytes accessed | tf_op | source)
XLA Modules:
  0.0 26.4 jit_solution(10454195811964770526)
XLA Ops:
  0.6 0.0 copy-start.4
  0.6 0.0 copy-start.3
  0.7 0.0 copy-start.1
  0.7 1.0 %pad_maximum_fusion.own = bf16[704,128]{1,0:T(8,128)(2,1)S(1)} fusion(bf16[128,128]{1,0:T(8,128)(2,1)} %bitcast.23, bf16[576,128]{1,0:T(8,128)(2,1)} %bitcast.22), kind=kLoop, calls=%fused_computation | loop fusion | flops 360448 | bytes 360448 | tf_op jit(solution)/shard_map/concatenate | solution.py:255
  1.6 4.1 %collective-permute-start = (bf16[704,128]{1,0:T(8,128)(2,1)S(1)}, bf16[704,128]{1,0:T(8,128)(2,1)S(1)}, u32[]{:S(2)}, u32[]{:S(2)}) collective-permute-start(bf16[704,128]{1,0:T(8,128)(2,1)S(1)} %pad_maximum_fusion.own), channel_id=1, source_target_pairs={{0,8},{1,5},{2,10},{3,7},{8,12},{9,1},{10,14},{11,3},{12,4},{13,9}... | collective-permute-start | bytes 540680 | tf_op jit(solution)/shard_map/ppermute | solution.py:246
  5.7 0.0 collective-permute-start.3
  5.7 1.5 %collective-permute-start.2 = (bf16[704,128]{1,0:T(8,128)(2,1)S(1)}, bf16[704,128]{1,0:T(8,128)(2,1)S(1)}, u32[]{:S(2)}, u32[]{:S(2)}) collective-permute-start(bf16[704,128]{1,0:T(8,128)(2,1)S(1)} %pad_maximum_fusion.own), channel_id=1, source_target_pairs={{0,2},{2,0},{4,6},{6,4},{8,10},{10,8},{12,14},{14,12},{1,3},{3,1},... | collective-permute-start | bytes 540680 | tf_op jit(solution)/shard_map/ppermute | solution.py:249
  7.2 0.5 %collective-permute-start.1 = (s32[1,4]{1,0:T(1,128)}, s32[1,4]{1,0:T(1,128)S(1)}, u32[]{:S(2)}, u32[]{:S(2)}) collective-permute-start(s32[1,4]{1,0:T(1,128)} %bitcast.20), channel_id=1, source_target_pairs={{0,2},{2,0},{4,6},{6,4},{8,10},{10,8},{12,14},{14,12},{1,3},{3,1},... | collective-permute-start | bytes 56 | tf_op jit(solution)/shard_map/ppermute | solution.py:249
  7.8 0.0 copy-start
  7.8 1.3 %copy-done = bf16[1,8,128,576]{2,3,1,0:T(8,128)(2,1)S(1)} copy-done((bf16[1,8,128,576]{2,3,1,0:T(8,128)(2,1)S(1)}, bf16[1,8,128,576]{2,3,1,0:T(8,128)(2,1)}, u32[]{:S(2)}) %copy-start) | copy-done | bytes 1179672
  9.0 0.7 %copy-done.2 = bf16[1,8,576]{2,1,0:T(8,128)(2,1)S(1)} copy-done((bf16[1,8,576]{2,1,0:T(8,128)(2,1)S(1)}, bf16[1,8,576]{2,1,0:T(8,128)(2,1)}, u32[]{:S(2)}) %copy-start.2) | copy-done | bytes 9240
  9.7 0.6 %shard_map.95 = (bf16[1024,576]{1,0:T(8,128)(2,1)S(1)}, f32[1024,128]{1,0:T(8,128)S(1)}, bf16[128,512]{1,0:T(8,128)(2,1)S(1)}) custom-call(bf16[8,576,128]{2,1,0:T(8,128)(2,1)S(1)} %bitcast.14, bf16[8,576]{1,0:T(8,128)(2,1)S(1)} %bitcast.17), custom_call_target="tpu_custom_call" | custom-call | bytes 2359296 | tf_op jit(solution)/shard_map/pallas_call | solution.py:262
  10.3 1.6 %collective-permute-done.1.list_ref = s32[1,4]{1,0:T(1,128)S(1)} collective-permute-done((s32[1,4]{1,0:T(1,128)}, s32[1,4]{1,0:T(1,128)S(1)}, u32[]{:S(2)}, u32[]{:S(2)}) %collective-permute-start.1) | collective-permute-done | bytes 48 | tf_op jit(solution)/shard_map/ppermute | solution.py:249
  11.9 0.1 collective-permute-done.line_ref.below
  12.0 2.2 %collective-permute-start.4 = (bf16[704,128]{1,0:T(8,128)(2,1)S(1)}, bf16[704,128]{1,0:T(8,128)(2,1)S(1)}, u32[]{:S(2)}, u32[]{:S(2)}) collective-permute-start(bf16[704,128]{1,0:T(8,128)(2,1)S(1)} %collective-permute-done.line_ref.below), channel_id=1, source_target_pairs={{0,8},{1,5},{2,10},{3,7},{8,12},{9,1},{10,14},{11,3},{12,4},{13,9}... | collective-permute-start | bytes 540680 | tf_op jit(solution)/shard_map/ppermute | solution.py:246
  14.2 0.0 collective-permute-done.2.near
  14.2 0.2 shard_map.96
  14.4 1.6 %collective-permute-start.5 = (bf16[416,128]{1,0:T(8,128)(2,1)S(1)}, bf16[416,128]{1,0:T(8,128)(2,1)S(1)}, u32[]{:S(2)}, u32[]{:S(2)}) collective-permute-start(bf16[416,128]{1,0:T(8,128)(2,1)S(1)} %shard_map.96), channel_id=1, source_target_pairs={{0,2},{2,0},{4,6},{6,4},{8,10},{10,8},{12,14},{14,12},{1,3},{3,1},... | collective-permute-start | bytes 319496 | tf_op jit(solution)/shard_map/ppermute | solution.py:249
  15.9 0.3 %collective-permute-done.3.above.line_ref = bf16[704,128]{1,0:T(8,128)(2,1)S(1)} collective-permute-done((bf16[704,128]{1,0:T(8,128)(2,1)S(1)}, bf16[704,128]{1,0:T(8,128)(2,1)S(1)}, u32[]{:S(2)}, u32[]{:S(2)}) %collective-permute-start.3) | collective-permute-done | bytes 180256 | tf_op jit(solution)/shard_map/ppermute | solution.py:246
  16.2 0.2 shard_map.98
  16.4 1.5 %collective-permute-start.6 = (bf16[416,128]{1,0:T(8,128)(2,1)S(1)}, bf16[416,128]{1,0:T(8,128)(2,1)S(1)}, u32[]{:S(2)}, u32[]{:S(2)}) collective-permute-start(bf16[416,128]{1,0:T(8,128)(2,1)S(1)} %shard_map.98), channel_id=1, source_target_pairs={{0,2},{2,0},{4,6},{6,4},{8,10},{10,8},{12,14},{14,12},{1,3},{3,1},... | collective-permute-start | bytes 319496 | tf_op jit(solution)/shard_map/ppermute | solution.py:249
  17.9 1.2 %collective-permute-done.4.far.line_ref = bf16[704,128]{1,0:T(8,128)(2,1)S(1)} collective-permute-done((bf16[704,128]{1,0:T(8,128)(2,1)S(1)}, bf16[704,128]{1,0:T(8,128)(2,1)S(1)}, u32[]{:S(2)}, u32[]{:S(2)}) %collective-permute-start.4) | collective-permute-done | bytes 180256 | tf_op jit(solution)/shard_map/ppermute | solution.py:246
  19.1 0.1 shard_map.99
  19.2 1.6 %collective-permute-start.7 = (bf16[416,128]{1,0:T(8,128)(2,1)S(1)}, bf16[416,128]{1,0:T(8,128)(2,1)S(1)}, u32[]{:S(2)}, u32[]{:S(2)}) collective-permute-start(bf16[416,128]{1,0:T(8,128)(2,1)S(1)} %shard_map.99), channel_id=1, source_target_pairs={{0,2},{2,0},{4,6},{6,4},{8,10},{10,8},{12,14},{14,12},{1,3},{3,1},... | collective-permute-start | bytes 319496 | tf_op jit(solution)/shard_map/ppermute | solution.py:249
  21.4 0.0 collective-permute-done.5.side_below
  21.4 0.0 copy-done.4
  21.4 0.0 copy-done.3
  21.4 0.0 copy-done.1
  21.5 1.3 %shard_map.97 = (f32[8,16]{1,0:T(8,128)S(1)}, bf16[576,256]{1,0:T(8,128)(2,1)S(1)}, bf16[256,512]{1,0:T(8,128)(2,1)S(1)}, s32[8,256]{1,0:T(8,128)S(1)}) custom-call(s32[4]{0:T(128)S(1)} %bitcast.21, s32[1]{0:T(128)S(6)} %copy.10.length_ref, bf16[8,64]{1,0:T(8,128)(2,1)S(1)} %bitcast.18, bf16[512,128]{1,0:T(8,128)(2,1)S(1)} %bitcast.15, ...), custom_call_target="tpu_custom_call" | custom-call | bytes 2359296 | tf_op jit(solution)/shard_map/pallas_call | solution.py:278
  22.7 0.0 collective-permute-done.6.side_above
  22.7 1.3 %collective-permute-done.7.side_far = bf16[416,128]{1,0:T(8,128)(2,1)S(1)} collective-permute-done((bf16[416,128]{1,0:T(8,128)(2,1)S(1)}, bf16[416,128]{1,0:T(8,128)(2,1)S(1)}, u32[]{:S(2)}, u32[]{:S(2)}) %collective-permute-start.7) | collective-permute-done | bytes 106528 | tf_op jit(solution)/shard_map/ppermute | solution.py:249
  24.0 2.5 %shard_map.100 = (bf16[1024,512]{1,0:T(8,128)(2,1)}, f32[8,16]{1,0:T(8,128)}) custom-call(bf16[1024,576]{1,0:T(8,128)(2,1)S(1)} %get-tuple-element.19.q_ref, f32[1024,128]{1,0:T(8,128)S(1)} %get-tuple-element.20.fresh_ref, bf16[128,512]{1,0:T(8,128)(2,1)S(1)} %get-tuple-element.21.new_rows, bf16[576,256]{1,0:T(8,128)(2,1)S(1)} %get-tuple-element.26.early_turned, ...), custom_call_target="tpu_custom_call" | custom-call | tf_op jit(solution)/shard_map/pallas_call | solution.py:287
  (1 shorter events, 0.0 us)
Async XLA Ops:
  0.6 20.8 %copy-start.4 = (s32[1,1,4]{2,1,0:T(1,128)S(1)}, s32[1,1,4]{2,1,0:T(1,128)}, u32[]{:S(2)}) copy-start(s32[1,1,4]{2,1,0:T(1,128)} %param.14) | copy-start | bytes 52
  0.6 20.8 %copy-start.3 = (bf16[1,8,64]{2,1,0:T(8,128)(2,1)S(1)}, bf16[1,8,64]{2,1,0:T(8,128)(2,1)}, u32[]{:S(2)}) copy-start(bf16[1,8,64]{2,1,0:T(8,128)(2,1)} %param.12) | copy-start | bytes 3076
  0.7 20.8 %copy-start.1 = (bf16[1,8,64,128]{3,2,1,0:T(8,128)(2,1)S(1)}, bf16[1,8,64,128]{3,2,1,0:T(8,128)(2,1)}, u32[]{:S(2)}) copy-start(bf16[1,8,64,128]{3,2,1,0:T(8,128)(2,1)} %param.11) | copy-start | bytes 393220
  1.6 10.4 %collective-permute-start = (bf16[704,128]{1,0:T(8,128)(2,1)S(1)}, bf16[704,128]{1,0:T(8,128)(2,1)S(1)}, u32[]{:S(2)}, u32[]{:S(2)}) collective-permute-start(bf16[704,128]{1,0:T(8,128)(2,1)S(1)} %pad_maximum_fusion.own), channel_id=1, source_target_pairs={{0,8},{1,5},{2,10},{3,7},{8,12},{9,1},{10,14},{11,3},{12,4},{13,9}... | collective-permute-start | bytes 540680 | tf_op jit(solution)/shard_map/ppermute | solution.py:246
  5.7 10.5 %collective-permute-start.3 = (bf16[704,128]{1,0:T(8,128)(2,1)S(1)}, bf16[704,128]{1,0:T(8,128)(2,1)S(1)}, u32[]{:S(2)}, u32[]{:S(2)}) collective-permute-start(bf16[704,128]{1,0:T(8,128)(2,1)S(1)} %pad_maximum_fusion.own), channel_id=1, source_target_pairs={{0,4},{1,9},{2,6},{3,11},{8,0},{9,13},{10,2},{11,15},{12,8},{13,5}... | collective-permute-start | bytes 540680 | tf_op jit(solution)/shard_map/ppermute | solution.py:246
  5.7 8.5 %collective-permute-start.2 = (bf16[704,128]{1,0:T(8,128)(2,1)S(1)}, bf16[704,128]{1,0:T(8,128)(2,1)S(1)}, u32[]{:S(2)}, u32[]{:S(2)}) collective-permute-start(bf16[704,128]{1,0:T(8,128)(2,1)S(1)} %pad_maximum_fusion.own), channel_id=1, source_target_pairs={{0,2},{2,0},{4,6},{6,4},{8,10},{10,8},{12,14},{14,12},{1,3},{3,1},... | collective-permute-start | bytes 540680 | tf_op jit(solution)/shard_map/ppermute | solution.py:249
  7.2 4.6 %collective-permute-start.1 = (s32[1,4]{1,0:T(1,128)}, s32[1,4]{1,0:T(1,128)S(1)}, u32[]{:S(2)}, u32[]{:S(2)}) collective-permute-start(s32[1,4]{1,0:T(1,128)} %bitcast.20), channel_id=1, source_target_pairs={{0,2},{2,0},{4,6},{6,4},{8,10},{10,8},{12,14},{14,12},{1,3},{3,1},... | collective-permute-start | bytes 56 | tf_op jit(solution)/shard_map/ppermute | solution.py:249
  7.8 1.3 %copy-start = (bf16[1,8,128,576]{2,3,1,0:T(8,128)(2,1)S(1)}, bf16[1,8,128,576]{2,3,1,0:T(8,128)(2,1)}, u32[]{:S(2)}) copy-start(bf16[1,8,128,576]{2,3,1,0:T(8,128)(2,1)} %param.8) | copy-start | bytes 3538948
  9.0 0.7 %copy-start.2 = (bf16[1,8,576]{2,1,0:T(8,128)(2,1)S(1)}, bf16[1,8,576]{2,1,0:T(8,128)(2,1)}, u32[]{:S(2)}) copy-start(bf16[1,8,576]{2,1,0:T(8,128)(2,1)} %param.9) | copy-start | bytes 27652
  12.0 7.0 %collective-permute-start.4 = (bf16[704,128]{1,0:T(8,128)(2,1)S(1)}, bf16[704,128]{1,0:T(8,128)(2,1)S(1)}, u32[]{:S(2)}, u32[]{:S(2)}) collective-permute-start(bf16[704,128]{1,0:T(8,128)(2,1)S(1)} %collective-permute-done.line_ref.below), channel_id=1, source_target_pairs={{0,8},{1,5},{2,10},{3,7},{8,12},{9,1},{10,14},{11,3},{12,4},{13,9}... | collective-permute-start | bytes 540680 | tf_op jit(solution)/shard_map/ppermute | solution.py:246
  14.4 7.0 %collective-permute-start.5 = (bf16[416,128]{1,0:T(8,128)(2,1)S(1)}, bf16[416,128]{1,0:T(8,128)(2,1)S(1)}, u32[]{:S(2)}, u32[]{:S(2)}) collective-permute-start(bf16[416,128]{1,0:T(8,128)(2,1)S(1)} %shard_map.96), channel_id=1, source_target_pairs={{0,2},{2,0},{4,6},{6,4},{8,10},{10,8},{12,14},{14,12},{1,3},{3,1},... | collective-permute-start | bytes 319496 | tf_op jit(solution)/shard_map/ppermute | solution.py:249
  16.4 6.3 %collective-permute-start.6 = (bf16[416,128]{1,0:T(8,128)(2,1)S(1)}, bf16[416,128]{1,0:T(8,128)(2,1)S(1)}, u32[]{:S(2)}, u32[]{:S(2)}) collective-permute-start(bf16[416,128]{1,0:T(8,128)(2,1)S(1)} %shard_map.98), channel_id=1, source_target_pairs={{0,2},{2,0},{4,6},{6,4},{8,10},{10,8},{12,14},{14,12},{1,3},{3,1},... | collective-permute-start | bytes 319496 | tf_op jit(solution)/shard_map/ppermute | solution.py:249
  19.2 4.8 %collective-permute-start.7 = (bf16[416,128]{1,0:T(8,128)(2,1)S(1)}, bf16[416,128]{1,0:T(8,128)(2,1)S(1)}, u32[]{:S(2)}, u32[]{:S(2)}) collective-permute-start(bf16[416,128]{1,0:T(8,128)(2,1)S(1)} %shard_map.99), channel_id=1, source_target_pairs={{0,2},{2,0},{4,6},{6,4},{8,10},{10,8},{12,14},{14,12},{1,3},{3,1},... | collective-permute-start | bytes 319496 | tf_op jit(solution)/shard_map/ppermute | solution.py:249
